TPU v7x, 256 devices: a whole 4x4x8 slice. The times are simulated.
256 devices in a mesh: lat: 64 (over y_hi, x, z), depth: 4 (over y_lo, core).
Axes of the slice: x: 4, y: 4 (y_hi: 2, y_lo: 2; y = y_hi * 2 + y_lo), z: 8, core: 2. Of those that a mesh axis runs over, the one named last changes fastest.
Arguments:
- head: float32 [64, 512, 4096], P('depth', 'lat'), may hold values from -1 to 0.5
- head_old: float32 [64, 512, 4096], P('depth', 'lat'), may hold values from -1 to 0.5
- soil: int32 [64, 512, 4096], P('depth', 'lat'), may hold values from 0 to 11
- cond_table: float32 [12], replicated, may hold values from 0.3 to 2
- shape_table: float32 [12], replicated, may hold values from 0.3 to 1.5
- pore_table: float32 [12], replicated, may hold values from 0.2 to 0.5
- pond: float32 [512, 4096], P('lat'), may hold values from 0.02 to 0.6
- ground: float32 [512, 4096], P('lat'), may hold values from -1.5 to 1.5
- ponded: int32 [512, 4096], P('lat'), may hold values 0 or 1
- river: int32 [512, 4096], P('lat'), may hold values 0 or 1
Outputs:
- head_new: float32 [64, 512, 4096], P('depth', 'lat')
- surface_new: float32 [512, 4096], P('lat', 'depth')
All inputs are finite; a program needn't handle non-finite values. No bound on the sum of `ponded` or of `river` on one device may be relied on, other than what follows from the above.
Results may differ from a plain program's by a relative error of at most 0.0003.
Values sent between devices are 32-bit elements; how exact they have to be, the bound alone decides.
No kernel may reach another device: no remote copies, remote signals or barrier semaphores. Data moves between devices by JAX's collectives and lax.ppermute only.
A program may use at most 128 MiB of HBM per device.

v0:
```python
import jax
import jax.numpy as jnp
from jax import lax
from jax.sharding import PartitionSpec as P

SWEEPS = 4


TIME_STEP = 20.0
SURFACE_STEP = 2.0
SPECIFIC_STORAGE = 0.01
LAND_CONVEYANCE = 3.0
RIVER_CONVEYANCE = 10.0
SLOPE_FLOOR = 0.01


def with_halo(x, sides, width):
    for axis, dim in sides:
        size, length = (lax.axis_size(axis), x.shape[dim])
        up = [(i, (i + 1) % size) for i in range(size - 1)]
        down = [(j, i) for i, j in up]
        last = lax.slice_in_dim(x, length - width, length, axis=dim)
        initial = lax.slice_in_dim(x, 0, width, axis=dim)
        before = lax.ppermute(last, axis, up)
        after = lax.ppermute(initial, axis, down)
        x = jnp.concatenate([before, x, after], axis=dim)
    return x


def from_root(value, axis, source):
    kept = jnp.where(lax.axis_index(axis) == source, value, 0).astype(value.dtype)
    return lax.psum(kept, axis)


def lookup(soil, table):
    value = jnp.zeros(soil.shape, jnp.float32)
    for soil_kind in range(table.shape[0]):
        value = jnp.where(soil == soil_kind, table[soil_kind], value)
    return value


def harmonic(first, second):
    total = first + second
    return 2.0 * first * second / jnp.where(total > 0.0, total, 1.0)


def soil_state(head, head_old, soil, cond_table, shape_table, pore_table):
    saturated = lookup(soil, cond_table)
    steepness = lookup(soil, shape_table)
    porosity = lookup(soil, pore_table)
    wetness = jnp.exp(steepness * jnp.minimum(head, 0.0))
    wetness_old = jnp.exp(steepness * jnp.minimum(head_old, 0.0))
    conductivity = saturated * wetness
    storage_change = porosity * (wetness - wetness_old) + SPECIFIC_STORAGE * (head - head_old)
    capacity = SPECIFIC_STORAGE + porosity * steepness * wetness
    return (conductivity, storage_change, capacity)


def vertical_terms(cond_ext, head_ext):
    vface = harmonic(cond_ext[:-1], cond_ext[1:])
    vflux = vface * (head_ext[:-1] - head_ext[1:] + 1.0)
    return (vface, vflux)


def lateral_inflow(conductivity, head, cond_rows, head_rows):
    face_x = harmonic(cond_rows[:, :-1], cond_rows[:, 1:])
    inflow = face_x[:, 1:] * (head_rows[:, 2:] - head) + face_x[:, :-1] * (head_rows[:, :-2] - head)
    cond_cols = jnp.pad(conductivity, ((0, 0), (0, 0), (1, 1)))
    head_cols = jnp.pad(head, ((0, 0), (0, 0), (1, 1)))
    face_y = harmonic(cond_cols[:, :, :-1], cond_cols[:, :, 1:])
    inflow = inflow + face_y[:, :, 1:] * (head_cols[:, :, 2:] - head)
    return inflow + face_y[:, :, :-1] * (head_cols[:, :, :-2] - head)


def newton_system(storage_change, capacity, vface, vflux, lateral, top_term, top_cond, bottom_term):
    inflow = jnp.concatenate([(vflux[0] + top_term)[None], vflux[1:-1]], 0)
    outflow = jnp.concatenate([vflux[1:-1], (vflux[-1] + bottom_term)[None]], 0)
    residual = storage_change / TIME_STEP - (inflow - outflow) - lateral
    diagonal = capacity / TIME_STEP + vface[:-1] + vface[1:]
    diagonal = jnp.concatenate([(diagonal[0] + 2.0 * top_cond)[None], diagonal[1:]], 0)
    return (residual, diagonal, -vface[:-1], -vface[1:])


def thomas(lower, middle, upper, rhs):
    count = middle.shape[0]
    ratios = []
    partial_values = []
    for row_index in range(count):
        if row_index == 0:
            pivot = middle[0]
            partial_values.append(rhs[0] / pivot)
        else:
            pivot = middle[row_index] - lower[row_index] * ratios[-1]
            partial_values.append((rhs[row_index] - lower[row_index] * partial_values[-1]) / pivot)
        ratios.append(upper[row_index] / pivot)
    result = [partial_values[-1]]
    for row_index in reversed(range(count - 1)):
        result.insert(0, partial_values[row_index] - ratios[row_index] * result[0])
    return jnp.stack(result, 0)


def reduced_down(pieces, beta_prev, gamma_prev):
    top_base, bottom_base, top_above, bottom_above, top_below, bottom_below = pieces
    scale = 1.0 - top_above * gamma_prev
    tau_value = (top_base - top_above * beta_prev) / scale
    sigma_value = top_below / scale
    beta_value = bottom_base - bottom_above * beta_prev + bottom_above * gamma_prev * tau_value
    gamma_value = bottom_below + bottom_above * gamma_prev * sigma_value
    return (beta_value, gamma_value, tau_value, sigma_value)


def face_k(pond_one, ground_one, conv_one, pond_two, ground_two, conv_two):
    depth_face = 0.5 * (pond_one + pond_two)
    slope = pond_two + ground_two - (pond_one + ground_one)
    return (
        jnp.power(depth_face, 5.0 / 3.0)
        * harmonic(conv_one, conv_two)
        / jnp.sqrt(jnp.abs(slope) + SLOPE_FLOOR)
    )


def row_terms(
    pond, ground, conv, exfil, pond_up, ground_up, conv_up, pond_down, ground_down, conv_down
):
    k_up = face_k(pond, ground, conv, pond_up, ground_up, conv_up)
    k_down = face_k(pond, ground, conv, pond_down, ground_down, conv_down)
    k_cols = face_k(
        pond[:, :-1], ground[:, :-1], conv[:, :-1], pond[:, 1:], ground[:, 1:], conv[:, 1:]
    )
    k_left = jnp.pad(k_cols, ((0, 0), (1, 0)))
    k_right = jnp.pad(k_cols, ((0, 0), (0, 1)))
    ground_left = jnp.pad(ground[:, :-1], ((0, 0), (1, 0)))
    ground_right = jnp.pad(ground[:, 1:], ((0, 0), (0, 1)))
    sdiag = 1.0 / SURFACE_STEP + k_up + k_down + k_left + k_right
    srhs = (
        pond / SURFACE_STEP + exfil + k_up * (ground_up - ground) + k_down * (ground_down - ground)
    )
    srhs = srhs + k_left * (ground_left - ground) + k_right * (ground_right - ground)
    return (k_up, k_down, k_left, k_right, sdiag, srhs)


def sweep(level, level_up, level_down, terms):
    k_up, k_down, k_left, k_right, sdiag, srhs = terms
    left = jnp.pad(level[:, :-1], ((0, 0), (1, 0)))
    right = jnp.pad(level[:, 1:], ((0, 0), (0, 1)))
    return (srhs + k_up * level_up + k_down * level_down + k_left * left + k_right * right) / sdiag


def per_device(
    head, head_old, soil, cond_table, shape_table, pore_table, pond, ground, ponded, river
):
    depth_index = lax.axis_index("depth")
    depth_count = lax.axis_size("depth")
    is_top = depth_index == 0
    is_bottom = depth_index == depth_count - 1
    conductivity, storage_change, capacity = soil_state(
        head, head_old, soil, cond_table, shape_table, pore_table
    )
    head_ext, cond_ext = (
        with_halo(head, (("lat", 1), ("depth", 0)), 1),
        with_halo(conductivity, (("lat", 1), ("depth", 0)), 1),
    )
    vface, vflux = vertical_terms(cond_ext[:, 1:-1], head_ext[:, 1:-1])
    lateral = lateral_inflow(conductivity, head, cond_ext[1:-1], head_ext[1:-1])
    wet_pond = ponded.astype(jnp.float32) * pond
    top_flux = conductivity[0] * (2.0 * (wet_pond - head[0]) + 1.0)
    exfil = from_root(-top_flux, "depth", 0)
    zero_plane = jnp.zeros_like(top_flux)
    top_term = jnp.where(is_top, top_flux, zero_plane)
    top_cond = jnp.where(is_top, conductivity[0], zero_plane)
    bottom_term = jnp.where(is_bottom, conductivity[-1], zero_plane)
    residual, diagonal, lower, upper = newton_system(
        storage_change, capacity, vface, vflux, lateral, top_term, top_cond, bottom_term
    )
    local_lower = jnp.concatenate([zero_plane[None], lower[1:]], 0)
    local_upper = jnp.concatenate([upper[:-1], zero_plane[None]], 0)
    coupling_up = jnp.concatenate([lower[:1], jnp.zeros_like(lower[1:])], 0)
    coupling_down = jnp.concatenate([jnp.zeros_like(upper[:-1]), upper[-1:]], 0)
    stacked_rhs = jnp.stack([-residual, coupling_up, coupling_down], axis=1)
    solved = thomas(local_lower, diagonal, local_upper, stacked_rhs)
    base_part = solved[:, 0]
    above_part = solved[:, 1]
    below_part = solved[:, 2]
    pieces = (
        base_part[0],
        base_part[-1],
        above_part[0],
        above_part[-1],
        below_part[0],
        below_part[-1],
    )
    gathered = (
        lax.all_gather(pieces[0][None], "depth", axis=0, tiled=True),
        lax.all_gather(pieces[1][None], "depth", axis=0, tiled=True),
        lax.all_gather(pieces[2][None], "depth", axis=0, tiled=True),
        lax.all_gather(pieces[3][None], "depth", axis=0, tiled=True),
        lax.all_gather(pieces[4][None], "depth", axis=0, tiled=True),
        lax.all_gather(pieces[5][None], "depth", axis=0, tiled=True),
    )
    beta_prev = zero_plane
    gamma_prev = zero_plane
    downward = []
    for slab_index in range(depth_count):
        slab_pieces = tuple((member[slab_index] for member in gathered))
        result = reduced_down(slab_pieces, beta_prev, gamma_prev)
        downward.append((beta_prev, gamma_prev) + result)
        beta_prev = result[0]
        gamma_prev = result[1]
    tops_list = [zero_plane] * depth_count
    belows_list = [zero_plane] * depth_count
    carried = zero_plane
    for slab_index in reversed(range(depth_count)):
        belows_list[slab_index] = carried
        tops_list[slab_index] = downward[slab_index][4] - downward[slab_index][5] * carried
        carried = tops_list[slab_index]
    aboves_list = [
        downward[slab_index][0] - downward[slab_index][1] * tops_list[slab_index]
        for slab_index in range(depth_count)
    ]
    above_bottom = lax.dynamic_index_in_dim(
        jnp.stack(aboves_list, 0), depth_index, 0, keepdims=False
    )
    below_top = lax.dynamic_index_in_dim(jnp.stack(belows_list, 0), depth_index, 0, keepdims=False)
    step = base_part - above_part * above_bottom - below_part * below_top
    head_new = head + step
    conveyance = LAND_CONVEYANCE + (RIVER_CONVEYANCE - LAND_CONVEYANCE) * river.astype(jnp.float32)
    pond_ext, ground_ext, conv_ext = (
        with_halo(pond, (("lat", 0),), 1),
        with_halo(ground, (("lat", 0),), 1),
        with_halo(conveyance, (("lat", 0),), 1),
    )
    terms = row_terms(
        pond,
        ground,
        conveyance,
        exfil,
        pond_ext[:-2],
        ground_ext[:-2],
        conv_ext[:-2],
        pond_ext[2:],
        ground_ext[2:],
        conv_ext[2:],
    )
    level = pond
    for sweep_index in range(SWEEPS):
        level_ext = with_halo(level, (("lat", 0),), 1)
        level = sweep(level, level_ext[:-2], level_ext[2:], terms)
    column_width = pond.shape[1] // depth_count
    surface_new = lax.dynamic_slice_in_dim(level, depth_index * column_width, column_width, 1)
    return (head_new, surface_new)


def solution(mesh):
    placed = (
        P("depth", "lat", None),
        P("depth", "lat", None),
        P("depth", "lat", None),
        P(),
        P(),
        P(),
        P("lat", None),
        P("lat", None),
        P("lat", None),
        P("lat", None),
    )
    return jax.shard_map(
        per_device,
        mesh=mesh,
        in_specs=placed,
        out_specs=(P("depth", "lat", None), P("lat", "depth")),
        check_vma=False,
    )
```

profile of v0, /device:TPU:25, one launch (start us, length us, event | category | flops | bytes accessed | tf_op | source)
XLA Modules:
  0.0 255.5 jit_solution(2533948784532000023)
XLA Ops:
  7.2 1.8 fusion.205
  9.0 1.8 fusion.206
  10.9 23.3 %select_multiply_fusion = (f32[16,8,4096]{2,1,0:T(8,128)S(1)}, pred[16,8,4096]{2,1,0:T(8,128)(4,1)S(1)}, pred[16,8,4096]{2,1,0:T(8,128)(4,1)S(1)}, pred[16,8,409...) fusion(f32[16,8,4096]{2,1,0:T(8,128)} %param.10, ...), kind=kLoop, calls=%fused_computation.53 | loop fusion | flops 20447232 | bytes 12583008 | tf_op jit(solution)/shard_map/mul | solution.py:53
  34.2 1.3 copy-done.1
  35.5 0.8 negate_select_fusion
  37.0 10.5 %collective-permute-start.12 = (f32[1,4096]{1,0:T(1,128)S(1)}, f32[1,4096]{1,0:T(1,128)S(1)}, u32[]{:S(2)}, u32[]{:S(2)}) collective-permute-start(f32[1,4096]{1,0:T(1,128)S(1)} %get-tuple-element.137), channel_id=1, source_target_pairs={{4,0},{8,4},{12,8},{16,12},{20,16},{24,20},{28,24},{32,28},{36,32}... | collective-permute-start | bytes 49160 | tf_op jit(solution)/shard_map/ppermute | solution.py:25
  47.5 1.9 collective-permute-start.9
  50.0 1.9 collective-permute-start.10
  52.6 9.1 %collective-permute-start.11 = (f32[1,4096]{1,0:T(1,128)}, f32[1,4096]{1,0:T(1,128)}, u32[]{:S(2)}, u32[]{:S(2)}) collective-permute-start(f32[1,4096]{1,0:T(1,128)} %get-tuple-element.135), channel_id=1, source_target_pairs={{4,0},{8,4},{12,8},{16,12},{20,16},{24,20},{28,24},{32,28},{36,32}... | collective-permute-start | bytes 49160 | tf_op jit(solution)/shard_map/ppermute | solution.py:25
  61.7 3.4 %collective-permute-start.13 = (f32[1,4096]{1,0:T(1,128)}, f32[1,4096]{1,0:T(1,128)}, u32[]{:S(2)}, u32[]{:S(2)}) collective-permute-start(f32[1,4096]{1,0:T(1,128)} %get-tuple-element.139), channel_id=1, source_target_pairs={{4,0},{8,4},{12,8},{16,12},{20,16},{24,20},{28,24},{32,28},{36,32}... | collective-permute-start | bytes 49160 | tf_op jit(solution)/shard_map/ppermute | solution.py:25
  65.0 0.9 fusion.200
  65.9 3.5 %fusion.190 = (f32[16,1,4096]{2,1,0:T(1,128)}, f32[16,1,4096]{2,1,0:T(1,128)}) fusion(f32[16,8,4096]{2,1,0:T(8,128)} %copy-done.1), kind=kLoop, calls=%fused_computation.374 | loop fusion | bytes 1048576 | tf_op jit(solution)/shard_map/slice | solution.py:22
  69.4 1.3 fusion.191
  70.7 2.0 fusion.8
  73.3 1.9 collective-permute-start.8
  75.9 1.9 collective-permute-start
  77.8 9.1 %collective-permute-start.1 = (f32[16,1,4096]{2,1,0:T(1,128)}, f32[16,1,4096]{2,1,0:T(1,128)}, u32[]{:S(2)}, u32[]{:S(2)}) collective-permute-start(f32[16,1,4096]{2,1,0:T(1,128)} %get-tuple-element.109), channel_id=1, source_target_pairs={{4,0},{8,4},{12,8},{16,12},{20,16},{24,20},{28,24},{32,28},{36,32}... | collective-permute-start | bytes 786440 | tf_op jit(solution)/shard_map/ppermute | solution.py:25
  86.9 1.9 collective-permute-start.4
  89.5 2.4 add_add_fusion.1
  91.9 1.6 fusion.88
  93.5 2.1 collective-permute-start.14
  95.6 9.1 %collective-permute-start.15 = (f32[1,4096]{1,0:T(1,128)S(1)}, f32[1,4096]{1,0:T(1,128)S(1)}, u32[]{:S(2)}, u32[]{:S(2)}) collective-permute-start(f32[1,4096]{1,0:T(1,128)S(1)} %get-tuple-element.129), channel_id=1, source_target_pairs={{4,0},{8,4},{12,8},{16,12},{20,16},{24,20},{28,24},{32,28},{36,32}... | collective-permute-start | bytes 49160 | tf_op jit(solution)/shard_map/ppermute | solution.py:25
  105.7 1.9 collective-permute-start.16
  107.7 9.4 %collective-permute-start.17 = (f32[1,4096]{1,0:T(1,128)S(1)}, f32[1,4096]{1,0:T(1,128)S(1)}, u32[]{:S(2)}, u32[]{:S(2)}) collective-permute-start(f32[1,4096]{1,0:T(1,128)S(1)} %get-tuple-element.125), channel_id=1, source_target_pairs={{4,0},{8,4},{12,8},{16,12},{20,16},{24,20},{28,24},{32,28},{36,32}... | collective-permute-start | bytes 49160 | tf_op jit(solution)/shard_map/ppermute | solution.py:25
  117.1 0.7 collective-permute-done.17
  118.1 1.9 collective-permute-start.18
  120.0 9.5 %collective-permute-start.19 = (f32[1,4096]{1,0:T(1,128)S(1)}, f32[1,4096]{1,0:T(1,128)S(1)}, u32[]{:S(2)}, u32[]{:S(2)}) collective-permute-start(f32[1,4096]{1,0:T(1,128)S(1)} %get-tuple-element.118), channel_id=1, source_target_pairs={{4,0},{8,4},{12,8},{16,12},{20,16},{24,20},{28,24},{32,28},{36,32}... | collective-permute-start | bytes 49160 | tf_op jit(solution)/shard_map/ppermute | solution.py:25
  129.6 3.4 %collective-permute-start.5 = (f32[16,1,4096]{2,1,0:T(1,128)S(1)}, f32[16,1,4096]{2,1,0:T(1,128)S(1)}, u32[]{:S(2)}, u32[]{:S(2)}) collective-permute-start(f32[16,1,4096]{2,1,0:T(1,128)S(1)} %copy-done.21), channel_id=1, source_target_pairs={{4,0},{8,4},{12,8},{16,12},{20,16},{24,20},{28,24},{32,28},{36,32}... | collective-permute-start | bytes 786440 | tf_op jit(solution)/shard_map/ppermute | solution.py:25
  133.0 1.5 fusion.149
  134.5 0.9 pad_maximum_fusion.21
  135.3 1.3 collective-permute-start.2
  136.6 8.5 %collective-permute-start.3 = (f32[1,10,4096]{2,1,0:T(8,128)S(1)}, f32[1,10,4096]{2,1,0:T(8,128)S(1)}, u32[]{:S(2)}, u32[]{:S(2)}) collective-permute-start(f32[1,10,4096]{2,1,0:T(8,128)S(1)} %get-tuple-element.78), channel_id=1, source_target_pairs={{1,0},{2,1},{3,2},{5,4},{6,5},{7,6},{9,8},{10,9},{11,10},{13,12},{... | collective-permute-start | bytes 491528 | tf_op jit(solution)/shard_map/ppermute | solution.py:25
  145.2 0.8 pad_maximum_fusion.18
  146.0 1.3 collective-permute-start.6
  147.3 4.5 %collective-permute-start.7 = (f32[1,10,4096]{2,1,0:T(8,128)S(1)}, f32[1,10,4096]{2,1,0:T(8,128)S(1)}, u32[]{:S(2)}, u32[]{:S(2)}) collective-permute-start(f32[1,10,4096]{2,1,0:T(8,128)S(1)} %get-tuple-element.80), channel_id=1, source_target_pairs={{1,0},{2,1},{3,2},{5,4},{6,5},{7,6},{9,8},{10,9},{11,10},{13,12},{... | collective-permute-start | bytes 491528 | tf_op jit(solution)/shard_map/ppermute | solution.py:25
  151.8 2.5 fusion
  154.3 3.8 %fusion.7 = (f32[17,8,4096]{2,1,0:T(8,128)S(1)}, f32[17,8,4096]{2,1,0:T(8,128)S(1)}) fusion(f32[1,10,4096]{2,1,0:T(8,128)S(1)} %collective-permute-done.7, f32[16,1,4096]{2,1,0:T(1,128)S(1)} %collective-permute-done.5, f32[16,8,4096]{2,1,0:T(8,128)S(1)} %copy-done, f32[16,1,4096]{2,1,0:T(1,128)} %collective-permute-done.4, ...), kind=kLoop, calls=%fused_computation.13 | loop fusion | flops 11698176 | bytes 10354688 | tf_op jit(solution)/shard_map/mul | solution.py:61
  158.4 1.3 copy-done.4
  160.5 23.2 %fusion.17 = (f32[16,1,8,4096]{3,2,1,0:T(8,128)S(1)}, f32[16,8,4096]{2,1,0:T(8,128)S(1)}) fusion(f32[16,8,4097]{2,1,0:T(8,128)S(1)} %copy-done.4, f32[16,8,4096]{2,1,0:T(8,128)S(1)} %copy-done, f32[16,1,4096]{2,1,0:T(1,128)} %collective-permute-done.4, f32[16,9,4096]{2,1,0:T(8,128)S(1)} %fusion, f32[16,1,4096]{2,1,0:T(1,128)S(1)} %collective-permute-done.5, ...), kind=kLoop, calls=%fused_computation.38 | loop fusion | flops 27787264 | bytes 25821280 | tf_op jit(solution)/shard_map/stack | solution.py:179
  183.7 10.9 %add_add_fusion = f32[16,8,4096]{2,1,0:T(8,128)S(1)} fusion(f32[16,8,4096]{2,1,0:T(8,128)S(1)} %get-tuple-element.60, f32[16,8,4096]{2,1,0:T(8,128)S(1)} %copy-done, f32[17,8,4096]{2,1,0:T(8,128)S(1)} %get-tuple-element.62, pred[16,8,4096]{2,1,0:T(8,128)(4,1)S(1)} %copy-done.14, pred[16,8,4096]{2,1,0:T(8,128)(4,1)S(1)} %copy-done.13, ...), kind=kLoop, calls=%fused_computation.50 | loop fusion | flops 10485760 | bytes 16777264 | tf_op jit(solution)/shard_map/add | solution.py:79
  197.1 1.5 constant_dynamic-update-slice_fusion.8
  198.6 10.2 %all-gather = f32[4,1,8,4096]{3,2,1,0:T(8,128)S(1)} all-gather(f32[1,1,8,4096]{3,2,1,0:T(8,128)S(1)} %get-tuple-element.117), channel_id=2, replica_groups=mesh['lat'=64,'depth'=4] {'depth'}, dimensions={0}, use_global_device_ids=true | all-gather | bytes 655360 | tf_op jit(solution)/shard_map/all_gather | solution.py:193
  208.8 7.3 %all-gather.1 = f32[4,1,8,4096]{3,2,1,0:T(8,128)S(1)} all-gather(f32[1,1,8,4096]{3,2,1,0:T(8,128)S(1)} %get-tuple-element.116), channel_id=3, replica_groups=mesh['lat'=64,'depth'=4] {'depth'}, dimensions={0}, use_global_device_ids=true | all-gather | bytes 655360 | tf_op jit(solution)/shard_map/all_gather | solution.py:195
  216.1 7.3 %all-gather.2 = f32[4,1,8,4096]{3,2,1,0:T(8,128)S(1)} all-gather(f32[1,1,8,4096]{3,2,1,0:T(8,128)S(1)} %get-tuple-element.115), channel_id=4, replica_groups=mesh['lat'=64,'depth'=4] {'depth'}, dimensions={0}, use_global_device_ids=true | all-gather | bytes 655360 | tf_op jit(solution)/shard_map/all_gather | solution.py:197
  223.4 7.3 %all-gather.3 = f32[4,1,8,4096]{3,2,1,0:T(8,128)S(1)} all-gather(f32[1,1,8,4096]{3,2,1,0:T(8,128)S(1)} %get-tuple-element.114), channel_id=5, replica_groups=mesh['lat'=64,'depth'=4] {'depth'}, dimensions={0}, use_global_device_ids=true | all-gather | bytes 655360 | tf_op jit(solution)/shard_map/all_gather | solution.py:194
  230.7 7.3 %all-gather.4 = f32[4,1,8,4096]{3,2,1,0:T(8,128)S(1)} all-gather(f32[1,1,8,4096]{3,2,1,0:T(8,128)S(1)} %get-tuple-element.113), channel_id=6, replica_groups=mesh['lat'=64,'depth'=4] {'depth'}, dimensions={0}, use_global_device_ids=true | all-gather | bytes 655360 | tf_op jit(solution)/shard_map/all_gather | solution.py:196
  238.0 7.3 %all-gather.5 = f32[4,1,8,4096]{3,2,1,0:T(8,128)S(1)} all-gather(f32[1,1,8,4096]{3,2,1,0:T(8,128)S(1)} %get-tuple-element.112), channel_id=7, replica_groups=mesh['lat'=64,'depth'=4] {'depth'}, dimensions={0}, use_global_device_ids=true | all-gather | bytes 655360 | tf_op jit(solution)/shard_map/all_gather | solution.py:198
  246.6 2.1 fusion.11
  (127 shorter events, 10.0 us)
Async XLA Ops:
  7.2 84.7 %all-reduce.17.cloned.1.call-start = ((), (), s32[]{:S(2)}) async-start(), calls=%async_computation | async-start | bytes 262144 | tf_op jit(solution)/shard_map/psum | solution.py:32
  10.8 24.7 %copy-start = (f32[16,8,4096]{2,1,0:T(8,128)S(1)}, f32[16,8,4096]{2,1,0:T(8,128)}, u32[]{:S(2)}) copy-start(f32[16,8,4096]{2,1,0:T(8,128)} %param.10) | copy-start | bytes 6291460
  10.8 24.7 %copy-start.15 = (f32[8,4096]{1,0:T(8,128)S(1)}, f32[8,4096]{1,0:T(8,128)}, u32[]{:S(2)}) copy-start(f32[8,4096]{1,0:T(8,128)} %param.16) | copy-start | bytes 393220
  10.8 24.7 %copy-start.23 = (s32[8,4096]{1,0:T(8,128)S(1)}, s32[8,4096]{1,0:T(8,128)}, u32[]{:S(2)}) copy-start(s32[8,4096]{1,0:T(8,128)} %param.18) | copy-start | bytes 393220
  10.8 25.5 %copy-start.22 = (s32[8,4096]{1,0:T(8,128)S(1)}, s32[8,4096]{1,0:T(8,128)}, u32[]{:S(2)}) copy-start(s32[8,4096]{1,0:T(8,128)} %param.19) | copy-start | bytes 393220
  10.8 38.6 %copy-start.17 = (f32[8,4096]{1,0:T(8,128)S(1)}, f32[8,4096]{1,0:T(8,128)}, u32[]{:S(2)}) copy-start(f32[8,4096]{1,0:T(8,128)} %param.17) | copy-start | bytes 393220
  34.2 1.3 copy-start.1
  36.3 34.4 %copy-start.2 = (f32[16,8,4096]{2,1,0:T(8,128)S(1)}, f32[16,8,4096]{2,1,0:T(8,128)}, u32[]{:S(2)}) copy-start(f32[16,8,4096]{2,1,0:T(8,128)} %copy-done.1) | copy-start | bytes 6291460
  36.4 28.7 %copy-start.18 = (f32[8,4096]{1,0:T(8,128)}, f32[8,4096]{1,0:T(8,128)S(1)}, u32[]{:S(2)}) copy-start(f32[8,4096]{1,0:T(8,128)S(1)} %multiply_add_fusion) | copy-start | bytes 393220
  37.0 35.7 %collective-permute-start.12 = (f32[1,4096]{1,0:T(1,128)S(1)}, f32[1,4096]{1,0:T(1,128)S(1)}, u32[]{:S(2)}, u32[]{:S(2)}) collective-permute-start(f32[1,4096]{1,0:T(1,128)S(1)} %get-tuple-element.137), channel_id=1, source_target_pairs={{4,0},{8,4},{12,8},{16,12},{20,16},{24,20},{28,24},{32,28},{36,32}... | collective-permute-start | bytes 49160 | tf_op jit(solution)/shard_map/ppermute | solution.py:25
  47.5 28.4 %collective-permute-start.9 = (f32[1,4096]{1,0:T(1,128)}, f32[1,4096]{1,0:T(1,128)}, u32[]{:S(2)}, u32[]{:S(2)}) collective-permute-start(f32[1,4096]{1,0:T(1,128)} %get-tuple-element.138), channel_id=1, source_target_pairs={{0,4},{4,8},{8,12},{12,16},{16,20},{20,24},{24,28},{28,32},{32,36}... | collective-permute-start | bytes 49160 | tf_op jit(solution)/shard_map/ppermute | solution.py:24
  50.0 27.8 %collective-permute-start.10 = (f32[1,4096]{1,0:T(1,128)}, f32[1,4096]{1,0:T(1,128)S(1)}, u32[]{:S(2)}, u32[]{:S(2)}) collective-permute-start(f32[1,4096]{1,0:T(1,128)} %get-tuple-element.140), channel_id=1, source_target_pairs={{0,4},{4,8},{8,12},{12,16},{16,20},{20,24},{24,28},{28,32},{32,36}... | collective-permute-start | bytes 49160 | tf_op jit(solution)/shard_map/ppermute | solution.py:24
  52.6 34.4 %collective-permute-start.11 = (f32[1,4096]{1,0:T(1,128)}, f32[1,4096]{1,0:T(1,128)}, u32[]{:S(2)}, u32[]{:S(2)}) collective-permute-start(f32[1,4096]{1,0:T(1,128)} %get-tuple-element.135), channel_id=1, source_target_pairs={{4,0},{8,4},{12,8},{16,12},{20,16},{24,20},{28,24},{32,28},{36,32}... | collective-permute-start | bytes 49160 | tf_op jit(solution)/shard_map/ppermute | solution.py:25
  61.7 27.2 %collective-permute-start.13 = (f32[1,4096]{1,0:T(1,128)}, f32[1,4096]{1,0:T(1,128)}, u32[]{:S(2)}, u32[]{:S(2)}) collective-permute-start(f32[1,4096]{1,0:T(1,128)} %get-tuple-element.139), channel_id=1, source_target_pairs={{4,0},{8,4},{12,8},{16,12},{20,16},{24,20},{28,24},{32,28},{36,32}... | collective-permute-start | bytes 49160 | tf_op jit(solution)/shard_map/ppermute | solution.py:25
  70.7 4.5 %copy-start.24 = (f32[12]{0:T(128)S(1)}, f32[12]{0:T(128)}, u32[]{:S(2)}) copy-start(f32[12]{0:T(128)} %param.15) | copy-start | bytes 148
  73.3 15.6 %collective-permute-start.8 = (f32[1,4096]{1,0:T(1,128)}, f32[1,4096]{1,0:T(1,128)S(1)}, u32[]{:S(2)}, u32[]{:S(2)}) collective-permute-start(f32[1,4096]{1,0:T(1,128)} %get-tuple-element.136), channel_id=1, source_target_pairs={{0,4},{4,8},{8,12},{12,16},{16,20},{20,24},{24,28},{28,32},{32,36}... | collective-permute-start | bytes 49160 | tf_op jit(solution)/shard_map/ppermute | solution.py:24
  75.9 58.6 %collective-permute-start = (f32[16,1,4096]{2,1,0:T(1,128)}, f32[16,1,4096]{2,1,0:T(1,128)}, u32[]{:S(2)}, u32[]{:S(2)}) collective-permute-start(f32[16,1,4096]{2,1,0:T(1,128)} %get-tuple-element.108), channel_id=1, source_target_pairs={{0,4},{4,8},{8,12},{12,16},{16,20},{20,24},{24,28},{28,32},{32,36}... | collective-permute-start | bytes 786440 | tf_op jit(solution)/shard_map/ppermute | solution.py:24
  77.8 56.6 %collective-permute-start.1 = (f32[16,1,4096]{2,1,0:T(1,128)}, f32[16,1,4096]{2,1,0:T(1,128)}, u32[]{:S(2)}, u32[]{:S(2)}) collective-permute-start(f32[16,1,4096]{2,1,0:T(1,128)} %get-tuple-element.109), channel_id=1, source_target_pairs={{4,0},{8,4},{12,8},{16,12},{20,16},{24,20},{28,24},{32,28},{36,32}... | collective-permute-start | bytes 786440 | tf_op jit(solution)/shard_map/ppermute | solution.py:25
  86.9 58.2 %collective-permute-start.4 = (f32[16,1,4096]{2,1,0:T(1,128)}, f32[16,1,4096]{2,1,0:T(1,128)}, u32[]{:S(2)}, u32[]{:S(2)}) collective-permute-start(f32[16,1,4096]{2,1,0:T(1,128)} %get-tuple-element.110), channel_id=1, source_target_pairs={{0,4},{4,8},{8,12},{12,16},{16,20},{20,24},{24,28},{28,32},{32,36}... | collective-permute-start | bytes 786440 | tf_op jit(solution)/shard_map/ppermute | solution.py:24
  88.9 0.6 copy-start.25
  91.9 13.7 %copy-start.16 = (f32[8,4096]{1,0:T(8,128)S(1)}, f32[8,4096]{1,0:T(8,128)}, u32[]{:S(2)}) copy-start(f32[8,4096]{1,0:T(8,128)} %get-tuple-element.4) | copy-start | bytes 393220
  93.5 36.1 %copy-start.21 = (f32[16,1,4096]{2,1,0:T(1,128)S(1)}, f32[16,1,4096]{2,1,0:T(1,128)}, u32[]{:S(2)}) copy-start(f32[16,1,4096]{2,1,0:T(1,128)} %get-tuple-element.111) | copy-start | bytes 786436
  93.5 11.3 %collective-permute-start.14 = (f32[1,4096]{1,0:T(1,128)S(1)}, f32[1,4096]{1,0:T(1,128)S(1)}, u32[]{:S(2)}, u32[]{:S(2)}) collective-permute-start(f32[1,4096]{1,0:T(1,128)S(1)} %get-tuple-element.128), channel_id=1, source_target_pairs={{0,4},{4,8},{8,12},{12,16},{16,20},{20,24},{24,28},{28,32},{32,36}... | collective-permute-start | bytes 49160 | tf_op jit(solution)/shard_map/ppermute | solution.py:24
  95.6 9.9 %collective-permute-start.15 = (f32[1,4096]{1,0:T(1,128)S(1)}, f32[1,4096]{1,0:T(1,128)S(1)}, u32[]{:S(2)}, u32[]{:S(2)}) collective-permute-start(f32[1,4096]{1,0:T(1,128)S(1)} %get-tuple-element.129), channel_id=1, source_target_pairs={{4,0},{8,4},{12,8},{16,12},{20,16},{24,20},{28,24},{32,28},{36,32}... | collective-permute-start | bytes 49160 | tf_op jit(solution)/shard_map/ppermute | solution.py:25
  104.8 29.7 %copy-start.3 = (f32[16,8,4096]{2,1,0:T(8,128)S(1)}, f32[16,8,4096]{2,1,0:T(8,128)}, u32[]{:S(2)}) copy-start(f32[16,8,4096]{2,1,0:T(8,128)} %copy-done.1) | copy-start | bytes 6291460
  105.7 11.4 %collective-permute-start.16 = (f32[1,4096]{1,0:T(1,128)S(1)}, f32[1,4096]{1,0:T(1,128)S(1)}, u32[]{:S(2)}, u32[]{:S(2)}) collective-permute-start(f32[1,4096]{1,0:T(1,128)S(1)} %get-tuple-element.124), channel_id=1, source_target_pairs={{0,4},{4,8},{8,12},{12,16},{16,20},{20,24},{24,28},{28,32},{32,36}... | collective-permute-start | bytes 49160 | tf_op jit(solution)/shard_map/ppermute | solution.py:24
  107.7 10.2 %collective-permute-start.17 = (f32[1,4096]{1,0:T(1,128)S(1)}, f32[1,4096]{1,0:T(1,128)S(1)}, u32[]{:S(2)}, u32[]{:S(2)}) collective-permute-start(f32[1,4096]{1,0:T(1,128)S(1)} %get-tuple-element.125), channel_id=1, source_target_pairs={{4,0},{8,4},{12,8},{16,12},{20,16},{24,20},{28,24},{32,28},{36,32}... | collective-permute-start | bytes 49160 | tf_op jit(solution)/shard_map/ppermute | solution.py:25
  118.1 11.5 %collective-permute-start.18 = (f32[1,4096]{1,0:T(1,128)S(1)}, f32[1,4096]{1,0:T(1,128)S(1)}, u32[]{:S(2)}, u32[]{:S(2)}) collective-permute-start(f32[1,4096]{1,0:T(1,128)S(1)} %get-tuple-element.119), channel_id=1, source_target_pairs={{0,4},{4,8},{8,12},{12,16},{16,20},{20,24},{24,28},{28,32},{32,36}... | collective-permute-start | bytes 49160 | tf_op jit(solution)/shard_map/ppermute | solution.py:24
  120.0 13.0 %collective-permute-start.19 = (f32[1,4096]{1,0:T(1,128)S(1)}, f32[1,4096]{1,0:T(1,128)S(1)}, u32[]{:S(2)}, u32[]{:S(2)}) collective-permute-start(f32[1,4096]{1,0:T(1,128)S(1)} %get-tuple-element.118), channel_id=1, source_target_pairs={{4,0},{8,4},{12,8},{16,12},{20,16},{24,20},{28,24},{32,28},{36,32}... | collective-permute-start | bytes 49160 | tf_op jit(solution)/shard_map/ppermute | solution.py:25
  129.6 15.6 %collective-permute-start.5 = (f32[16,1,4096]{2,1,0:T(1,128)S(1)}, f32[16,1,4096]{2,1,0:T(1,128)S(1)}, u32[]{:S(2)}, u32[]{:S(2)}) collective-permute-start(f32[16,1,4096]{2,1,0:T(1,128)S(1)} %copy-done.21), channel_id=1, source_target_pairs={{4,0},{8,4},{12,8},{16,12},{20,16},{24,20},{28,24},{32,28},{36,32}... | collective-permute-start | bytes 786440 | tf_op jit(solution)/shard_map/ppermute | solution.py:25
  135.3 18.9 %collective-permute-start.2 = (f32[1,10,4096]{2,1,0:T(8,128)S(1)}, f32[1,10,4096]{2,1,0:T(8,128)S(1)}, u32[]{:S(2)}, u32[]{:S(2)}) collective-permute-start(f32[1,10,4096]{2,1,0:T(8,128)S(1)} %get-tuple-element.77), channel_id=1, source_target_pairs={{0,1},{1,2},{2,3},{4,5},{5,6},{6,7},{8,9},{9,10},{10,11},{12,13},{... | collective-permute-start | bytes 491528 | tf_op jit(solution)/shard_map/ppermute | solution.py:24
  136.6 17.6 %collective-permute-start.3 = (f32[1,10,4096]{2,1,0:T(8,128)S(1)}, f32[1,10,4096]{2,1,0:T(8,128)S(1)}, u32[]{:S(2)}, u32[]{:S(2)}) collective-permute-start(f32[1,10,4096]{2,1,0:T(8,128)S(1)} %get-tuple-element.78), channel_id=1, source_target_pairs={{1,0},{2,1},{3,2},{5,4},{6,5},{7,6},{9,8},{10,9},{11,10},{13,12},{... | collective-permute-start | bytes 491528 | tf_op jit(solution)/shard_map/ppermute | solution.py:25
  146.0 8.3 %collective-permute-start.6 = (f32[1,10,4096]{2,1,0:T(8,128)S(1)}, f32[1,10,4096]{2,1,0:T(8,128)S(1)}, u32[]{:S(2)}, u32[]{:S(2)}) collective-permute-start(f32[1,10,4096]{2,1,0:T(8,128)S(1)} %get-tuple-element.79), channel_id=1, source_target_pairs={{0,1},{1,2},{2,3},{4,5},{5,6},{6,7},{8,9},{9,10},{10,11},{12,13},{... | collective-permute-start | bytes 491528 | tf_op jit(solution)/shard_map/ppermute | solution.py:24
  147.3 7.0 %collective-permute-start.7 = (f32[1,10,4096]{2,1,0:T(8,128)S(1)}, f32[1,10,4096]{2,1,0:T(8,128)S(1)}, u32[]{:S(2)}, u32[]{:S(2)}) collective-permute-start(f32[1,10,4096]{2,1,0:T(8,128)S(1)} %get-tuple-element.80), channel_id=1, source_target_pairs={{1,0},{2,1},{3,2},{5,4},{6,5},{7,6},{9,8},{10,9},{11,10},{13,12},{... | collective-permute-start | bytes 491528 | tf_op jit(solution)/shard_map/ppermute | solution.py:25
  154.3 4.1 %copy-start.20 = (f32[8,4096]{1,0:T(8,128)S(1)}, f32[8,4096]{1,0:T(8,128)}, u32[]{:S(2)}) copy-start(f32[8,4096]{1,0:T(8,128)} %get-tuple-element.8) | copy-start | bytes 393220
  154.3 4.1 %copy-start.10 = (pred[16,8,4096]{2,1,0:T(8,128)(4,1)S(1)}, pred[16,8,4096]{2,1,0:T(8,128)(4,1)}, u32[]{:S(2)}) copy-start(pred[16,8,4096]{2,1,0:T(8,128)(4,1)} %get-tuple-element.71) | copy-start | bytes 1572868
  154.3 4.1 %copy-start.11 = (pred[16,8,4096]{2,1,0:T(8,128)(4,1)S(1)}, pred[16,8,4096]{2,1,0:T(8,128)(4,1)}, u32[]{:S(2)}) copy-start(pred[16,8,4096]{2,1,0:T(8,128)(4,1)} %get-tuple-element.72) | copy-start | bytes 1572868
  154.3 4.1 %copy-start.12 = (pred[16,8,4096]{2,1,0:T(8,128)(4,1)S(1)}, pred[16,8,4096]{2,1,0:T(8,128)(4,1)}, u32[]{:S(2)}) copy-start(pred[16,8,4096]{2,1,0:T(8,128)(4,1)} %get-tuple-element.73) | copy-start | bytes 1572868
  154.3 4.1 %copy-start.13 = (pred[16,8,4096]{2,1,0:T(8,128)(4,1)S(1)}, pred[16,8,4096]{2,1,0:T(8,128)(4,1)}, u32[]{:S(2)}) copy-start(pred[16,8,4096]{2,1,0:T(8,128)(4,1)} %get-tuple-element.74) | copy-start | bytes 1572868
  154.3 4.1 %copy-start.14 = (pred[16,8,4096]{2,1,0:T(8,128)(4,1)S(1)}, pred[16,8,4096]{2,1,0:T(8,128)(4,1)}, u32[]{:S(2)}) copy-start(pred[16,8,4096]{2,1,0:T(8,128)(4,1)} %get-tuple-element.75) | copy-start | bytes 1572868
  154.3 4.1 %copy-start.19 = (f32[16,8,4096]{2,1,0:T(8,128)S(1)}, f32[16,8,4096]{2,1,0:T(8,128)}, u32[]{:S(2)}) copy-start(f32[16,8,4096]{2,1,0:T(8,128)} %param.11) | copy-start | bytes 6291460
  158.1 1.6 copy-start.4
  158.1 1.7 copy-start.5
  158.1 1.8 copy-start.6
  158.2 2.0 copy-start.7
  158.2 2.1 copy-start.8
  158.2 2.3 copy-start.9
  183.7 10.9 %copy-start.27 = (pred[16]{0:T(512)(128)(4,1)S(1)}, pred[16]{0:T(512)(128)(4,1)}, u32[]{:S(2)}) copy-start(pred[16]{0:T(512)(128)(4,1)} %constant.43.clone.1) | copy-start | bytes 52
  (1 other events, 0.6 us)
Sparse Core Ops, SparseCore 0:
  36.4 43.3 all-reduce.16
where the time goes:
time: 257 us; the launch traced here: 255 us
  starting transfers between devices  94.3 us (37%)
  other arithmetic  81.6 us (32%)
  blocking collectives  46.6 us (18%)
  local copies, waits for them, and re-layouts  16.5 us (6%)
  between operations  15 us (6%)
    ppermute x10, starting transfers between devices, with_halo(): after = lax.ppermute(initial, axis, down)  76.2 us
    another operation x3, other arithmetic, per_device(): stacked_rhs = jnp.stack([-residual, coupling_up, coupling_down], axis=1)  24.6 us
    mul x1, other arithmetic, soil_state(): conductivity = saturated * wetness  23.3 us
    ppermute x10, starting transfers between devices, with_halo(): before = lax.ppermute(last, axis, up)  18.1 us
    add x1, other arithmetic, newton_system(): diagonal = capacity / TIME_STEP + vface[:-1] + vface[1:]  10.9 us
    all_gather x1, blocking collectives, per_device(): lax.all_gather(pieces[0][None], 'depth', axis=0, tiled=True)  10.2 us
    all_gather x1, blocking collectives, per_device(): lax.all_gather(pieces[1][None], 'depth', axis=0, tiled=True)  7.29 us
    all_gather x1, blocking collectives, per_device(): lax.all_gather(pieces[3][None], 'depth', axis=0, tiled=True)  7.28 us
  transfers between devices with their start and end apart: 21, of which 2 were waited for; matrix products, arithmetic and copies ran while one was open for 8% of the time, Pallas kernels for 0%

commit v1 on v0

v1 whole, which is shorter than its diff:
```python
import jax
import jax.numpy as jnp
from jax import lax
from jax.experimental import pallas as pl
from jax.experimental.pallas import tpu as pltpu
from jax.sharding import PartitionSpec as P

SWEEPS = 4

TIME_STEP = 20.0
SURFACE_STEP = 2.0
SPECIFIC_STORAGE = 0.01
LAND_CONVEYANCE = 3.0
RIVER_CONVEYANCE = 10.0
SLOPE_FLOOR = 0.01

LOG2E = 1.4426950408889634
LN2 = 0.6931471805599453
CLOSED = 1e37

LANES = 128
ROWS = 8
CHUNK = 512
VMEM_LIMIT = 40 * 1024 * 1024

VMEM = pl.BlockSpec(memory_space=pltpu.VMEM)
SMEM = pl.BlockSpec(memory_space=pltpu.SMEM)
ANY = pl.BlockSpec(memory_space=pl.ANY)


def f32(*shape):
    return pltpu.VMEM(shape, jnp.float32)


def in_vmem(x):
    return pltpu.with_memory_space_constraint(x, pltpu.VMEM)


def params():
    return pltpu.CompilerParams(vmem_limit_bytes=VMEM_LIMIT)


def cost(flops, bytes_accessed=0):
    return pl.CostEstimate(flops=flops, bytes_accessed=bytes_accessed, transcendentals=0)


def rcp(x):
    r = pl.reciprocal(x, approx=True)
    return r * (2.0 - x * r)


def table_registers(*tables):
    lane = lax.broadcasted_iota(jnp.int32, (ROWS, LANES), 1)
    result = []
    for table in tables:
        value = jnp.ones((ROWS, LANES), jnp.float32)
        for soil_kind in range(table.shape[0]):
            value = jnp.where(lane == soil_kind, table[soil_kind], value)
        result.append(value)
    return result


def lookup(table, soil):
    parts = []
    for start in range(0, soil.shape[1], LANES):
        index = soil[:, start : start + LANES]
        parts.append(
            jnp.take_along_axis(table, index, axis=1, mode="promise_in_bounds")
        )
    return jnp.concatenate(parts, axis=1) if len(parts) > 1 else parts[0]


def lookup_rows(table, soil):
    return jnp.concatenate(
        [lookup(table, soil[start : start + ROWS]) for start in range(0, soil.shape[0], ROWS)], axis=0
    )


def window_start(quarter, width, window):
    return jnp.clip(quarter * width - LANES, 0, 4 * width - window)


def pack_kernel(
    cond_ref, shape_ref, head_ref, soil_ref, pond_ref, ground_ref, ponded_ref, river_ref,
    up_ref, down_ref, exfil_ref, soil_rows, soil_top, head_top, sem,
):
    nz = head_ref.shape[0]
    width = pond_ref.shape[1]
    quarter = width // 4
    window = quarter + 2 * LANES
    copies = [
        pltpu.make_async_copy(soil_ref.at[0], soil_top, sem.at[0]),
        pltpu.make_async_copy(head_ref.at[0], head_top, sem.at[1]),
        pltpu.make_async_copy(soil_ref.at[:, ROWS - 1, :], soil_rows.at[0], sem.at[2]),
        pltpu.make_async_copy(soil_ref.at[:, 0, :], soil_rows.at[1], sem.at[3]),
        pltpu.make_async_copy(head_ref.at[:, ROWS - 1, :], up_ref.at[pl.ds(0, nz)], sem.at[4]),
        pltpu.make_async_copy(head_ref.at[:, 0, :], down_ref.at[pl.ds(0, nz)], sem.at[5]),
    ]
    for copy in copies:
        copy.start()
    start = window_start(lax.axis_index("depth"), quarter, window)
    start = pl.multiple_of(start, LANES)
    lower_half = lax.broadcasted_iota(jnp.int32, (ROWS, window), 0) >= 4
    cut = pl.ds(start, window)
    conv = LAND_CONVEYANCE + (RIVER_CONVEYANCE - LAND_CONVEYANCE) * river_ref[:, cut].astype(jnp.float32)
    fields = [pond_ref[:, cut], ground_ref[:, cut], conv]
    cond_table, shape_table = table_registers(cond_ref, shape_ref)
    copies[0].wait()
    copies[1].wait()
    conductivity = lookup(cond_table, soil_top[...]) * jnp.exp(
        lookup(shape_table, soil_top[...]) * jnp.minimum(head_top[...], 0.0)
    )
    wet_pond = ponded_ref[...].astype(jnp.float32) * pond_ref[...]
    exfil = -conductivity * (2.0 * (wet_pond - head_top[...]) + 1.0)
    exfil_ref[...] = exfil
    tail = pl.ds(2 * nz, ROWS)
    up_ref[tail, :] = pltpu.roll(exfil, 4, 0)
    down_ref[tail, :] = exfil
    for place, field in enumerate(fields):
        lanes = pl.ds(place * window, window)
        up_ref[tail, lanes] = jnp.where(lower_half, field, up_ref[tail, lanes])
        down_ref[tail, lanes] = jnp.where(lower_half, pltpu.roll(field, 4, 0), down_ref[tail, lanes])
    copies[2].wait()
    up_ref[pl.ds(nz, nz), :] = soil_rows[0].astype(jnp.float32)
    copies[3].wait()
    down_ref[pl.ds(nz, nz), :] = soil_rows[1].astype(jnp.float32)
    copies[4].wait()
    copies[5].wait()


def state_chunk(chunk, tables, head_ref, old_ref, soil_ref, sigma, headx, base, diag):
    nz = head_ref.shape[0]
    half_res, steep, porosity, porosity_steep = tables
    lanes = pl.ds(pl.multiple_of(chunk * CHUNK, CHUNK), CHUNK)
    for z in range(nz):
        head = head_ref[z, :, lanes]
        old = old_ref[z, :, lanes]
        soil = soil_ref[z, :, lanes]
        alpha = lookup(steep, soil)
        pore = lookup(porosity, soil)
        power = alpha * jnp.minimum(head, 0.0)
        wet = jnp.exp2(power)
        wet_old = jnp.exp2(alpha * jnp.minimum(old, 0.0))
        sigma[z, :, lanes] = lookup(half_res, soil) * jnp.exp2(-power)
        headx[z, :, lanes] = head
        base[z, :, lanes] = pore * (wet_old - wet) + (SPECIFIC_STORAGE / TIME_STEP) * (old - head)
        diag[z, :, lanes] = SPECIFIC_STORAGE / TIME_STEP + lookup(porosity_steep, soil) * wet


def solve_chunk(
    chunk, flags, pond_ref, ponded_ref, sigma, headx, diag, last_flux,
    base, ratio, inv, top_col, bottom_col, resist_ref, sums_ref,
):
    nz = base.shape[0]
    is_top, is_bottom = flags
    start = pl.multiple_of(chunk * CHUNK, CHUNK)
    lanes = pl.ds(start, CHUNK)
    wide = pl.ds(start, CHUNK + LANES)
    sublane = lax.broadcasted_iota(jnp.int32, (ROWS, CHUNK), 0)
    inner = sublane < ROWS - 1
    face_above = flux_above = ratio_above = column = None
    for z in range(nz):
        sw, hw = sigma[z, :, wide], headx[z, :, wide]
        s, h = sw[:, :CHUNK], hw[:, :CHUNK]
        s_right = pltpu.roll(sw, CHUNK + LANES - 1, 1)[:, :CHUNK]
        h_right = pltpu.roll(hw, CHUNK + LANES - 1, 1)[:, :CHUNK]
        flux_y = rcp(s + s_right) * (h_right - h)
        shifted = jnp.concatenate([last_flux[z], flux_y], axis=1)
        flux_left = pltpu.roll(shifted, 1, 1)[:, LANES:]
        last_flux[z] = flux_y[:, CHUNK - LANES :]
        flux_x = rcp(s + pltpu.roll(s, ROWS - 1, 0)) * (pltpu.roll(h, ROWS - 1, 0) - h)
        flux_x = jnp.where(inner, flux_x, 0.0)
        b = base[z, :, lanes] + (flux_y - flux_left) + (flux_x - pltpu.roll(flux_x, 1, 0))
        d = diag[z, :, lanes]
        if z == 0:
            cond_top = 0.5 * rcp(s) * is_top
            wet_pond = ponded_ref[:, lanes].astype(jnp.float32) * pond_ref[:, lanes]
            b = b + cond_top * (2.0 * (wet_pond - h) + 1.0)
            d = d + 2.0 * cond_top
        else:
            b = b + flux_above
            d = d + face_above * (1.0 - ratio_above)
        if z == nz - 1:
            b = b - 0.5 * rcp(s) * is_bottom
        else:
            face = rcp(s + sigma[z + 1, :, lanes])
            flux = face * (h - headx[z + 1, :, lanes] + 1.0)
            b = b - flux
            d = d + face
        pivot_inv = rcp(d)
        base[z, :, lanes] = b
        inv[z, :, lanes] = pivot_inv
        column = pivot_inv if z == 0 else column * pivot_inv
        if z < nz - 1:
            ratio_above = face * pivot_inv
            ratio[z, :, lanes] = ratio_above
            top_col[z, :, lanes] = column
            column = column * face
            face_above, flux_above = face, flux
    first, last = column, pivot_inv
    top_col[nz - 1, :, lanes] = first
    bottom_col[nz - 1, :, lanes] = last
    corner = first
    resist_ref[pl.ds(2 * ROWS, ROWS), lanes] = corner
    resist_ref[pl.ds(ROWS, ROWS), lanes] = sigma[nz - 1, :, lanes] + last
    top_sum = first * b
    bottom_sum = last * b
    for z in reversed(range(nz - 1)):
        m = ratio[z, :, lanes]
        b = base[z, :, lanes]
        first = top_col[z, :, lanes] + m * first
        last = m * last
        top_col[z, :, lanes] = first
        bottom_col[z, :, lanes] = last
        top_sum = top_sum + first * b
        bottom_sum = bottom_sum + last * b
    resist_ref[pl.ds(0, ROWS), lanes] = sigma[0, :, lanes] + first
    sums_ref[pl.ds(0, ROWS), lanes] = top_sum + headx[0, :, lanes]
    sums_ref[pl.ds(ROWS, ROWS), lanes] = bottom_sum + headx[nz - 1, :, lanes]


def cells_kernel(
    cond_ref, shape_ref, pore_ref, head_ref, old_ref, soil_ref, pond_ref, ponded_ref,
    base, ratio, inv, top_col, bottom_col, resist_ref, sums_ref, rows_ref,
    sigma, headx, last_flux, sem,
):
    nz, _, width = head_ref.shape
    depth = lax.axis_index("depth")
    is_top = jnp.where(depth == 0, 1.0, 0.0)
    is_bottom = jnp.where(depth == 3, 1.0, 0.0)
    cond, shape, pore = table_registers(cond_ref, shape_ref, pore_ref)
    pore = pore * (1.0 / TIME_STEP)
    tables = (0.5 / cond, shape * LOG2E, pore, pore * shape)
    last_flux[...] = jnp.zeros_like(last_flux)
    sigma[:, :, pl.ds(width, LANES)] = jnp.full((nz, ROWS, LANES), CLOSED, jnp.float32)
    headx[:, :, pl.ds(width, LANES)] = jnp.zeros((nz, ROWS, LANES), jnp.float32)
    diag = inv

    @pl.loop(0, width // CHUNK)
    def _(chunk):
        state_chunk(chunk, tables, head_ref, old_ref, soil_ref, sigma, headx, base, diag)

    @pl.loop(0, width // CHUNK)
    def _(chunk):
        solve_chunk(
            chunk, (is_top, is_bottom), pond_ref, ponded_ref, sigma, headx, diag, last_flux,
            base, ratio, inv, top_col, bottom_col, resist_ref, sums_ref,
        )

    full = pl.ds(0, width)
    copies = []
    for place, array in enumerate((sigma, top_col, bottom_col)):
        for side, row in enumerate((ROWS - 1, 0)):
            source = array.at[:, row, full] if array is sigma else array.at[:, row, :]
            index = 2 * place + side
            copies.append(pltpu.make_async_copy(source, rows_ref.at[index], sem.at[index]))
    for copy in copies:
        copy.start()
    for copy in copies:
        copy.wait()


def halo_kernel(
    cond_ref, shape_ref, own_up, own_down, from_above, from_below, rows_ref, sums_ref, exfil_ref,
    ends_ref, flux_ref, sent_ref, kept_ref,
):
    nz = flux_ref.shape[1]
    width = own_up.shape[1]
    quarter = width // 4
    window = quarter + 2 * LANES
    lat = lax.axis_index("lat")
    has_above = jnp.where(lat == 0, 0.0, 1.0)
    has_below = jnp.where(lat == lax.axis_size("lat") - 1, 0.0, 1.0)
    is_even = lax.rem(lax.axis_index("depth"), 2) == 0
    cond, shape = table_registers(cond_ref, shape_ref)
    half_res, steep = 0.5 / cond, shape * LOG2E
    sublane = lax.broadcasted_iota(jnp.int32, (ROWS, CHUNK), 0)

    @pl.loop(0, width // CHUNK)
    def _(chunk):
        lanes = pl.ds(pl.multiple_of(chunk * CHUNK, CHUNK), CHUNK)
        totals = []
        for side, other, own, scale in ((0, from_below, own_up, has_below), (1, from_above, own_down, has_above)):
            total = None
            for start in range(0, nz, ROWS):
                here = pl.ds(start, ROWS)
                head = other[here, lanes]
                soil = other[pl.ds(nz + start, ROWS), lanes].astype(jnp.int32)
                res = lookup(half_res, soil) * jnp.exp2(-lookup(steep, soil) * jnp.minimum(head, 0.0))
                flux = rcp(res + rows_ref[side, here, lanes]) * (head - own[here, lanes]) * scale
                flux_ref[side, here, lanes] = flux
                part = (flux * rows_ref[2 + side, here, lanes], flux * rows_ref[4 + side, here, lanes])
                total = part if total is None else tuple(a + b for a, b in zip(total, part))
            totals.append([jnp.sum(part, axis=0, keepdims=True) for part in total])
        ends = []
        for place in range(2):
            added = jnp.where(sublane == 0, totals[1][place], 0.0)
            added = jnp.where(sublane == ROWS - 1, totals[0][place], added)
            ends.append(sums_ref[pl.ds(place * ROWS, ROWS), lanes] + added)
        ends_ref[pl.ds(0, ROWS), lanes] = jnp.where(is_even, ends[1], ends[0])
        ends_ref[pl.ds(ROWS, ROWS), lanes] = jnp.where(is_even, ends[0], ends[1])

    upper_half = lax.broadcasted_iota(jnp.int32, (ROWS, window), 0) < 4
    for place in range(4):
        lanes = pl.ds(min(max(place * quarter - LANES, 0), width - window), window)
        own = pltpu.roll(exfil_ref[:, lanes], 4, 0)
        above = from_above[pl.ds(2 * nz, ROWS), lanes]
        below = pltpu.roll(from_below[pl.ds(2 * nz, ROWS), lanes], 4, 0)
        target = (kept_ref, sent_ref)[place % 2]
        into = pl.ds((place // 2) * window, window)
        target[pl.ds(0, ROWS), into] = jnp.where(upper_half, above, own)
        target[pl.ds(ROWS, ROWS), into] = jnp.where(upper_half, own, below)


def local_kernel(flux_ref, base, ratio, inv, head_ref, out_ref):
    nz, _, width = base.shape
    sublane = lax.broadcasted_iota(jnp.int32, (ROWS, CHUNK), 0)

    @pl.loop(0, width // CHUNK)
    def _(chunk):
        lanes = pl.ds(pl.multiple_of(chunk * CHUNK, CHUNK), CHUNK)
        y = None
        for z in range(nz):
            below = flux_ref[0, pl.ds(z, 1), lanes]
            above = flux_ref[1, pl.ds(z, 1), lanes]
            added = jnp.where(sublane == 0, above, 0.0)
            added = jnp.where(sublane == ROWS - 1, below, added)
            rhs = base[z, :, lanes] + added
            y = rhs if z == 0 else rhs + ratio[z - 1, :, lanes] * y
            if z < nz - 1:
                out_ref[z, :, lanes] = y
        x = y * inv[nz - 1, :, lanes]
        out_ref[nz - 1, :, lanes] = x + head_ref[nz - 1, :, lanes]
        for z in reversed(range(nz - 1)):
            x = out_ref[z, :, lanes] * inv[z, :, lanes] + ratio[z, :, lanes] * x
            out_ref[z, :, lanes] = x + head_ref[z, :, lanes]


def final_kernel(local_ref, top_col, bottom_col, flow_in, flow_out, out_ref):
    nz, _, width = local_ref.shape

    @pl.loop(0, width // CHUNK)
    def _(chunk):
        lanes = pl.ds(pl.multiple_of(chunk * CHUNK, CHUNK), CHUNK)
        j_in, j_out = flow_in[:, lanes], flow_out[:, lanes]
        for z in range(nz):
            out_ref[z, :, lanes] = (
                local_ref[z, :, lanes] + top_col[z, :, lanes] * j_in - bottom_col[z, :, lanes] * j_out
            )


def shift_rows(x, by):
    return pltpu.roll(x, by % x.shape[0], 0)


def shift_lanes(x, by):
    return pltpu.roll(x, by % x.shape[1], 1)


def harmonic(first, second):
    total = first + second
    return 2.0 * first * second * rcp(jnp.where(total > 0.0, total, 1.0))


def face_k(pond, ground, conv, shift):
    pond_two, ground_two, conv_two = shift(pond), shift(ground), shift(conv)
    depth_face = 0.5 * (pond + pond_two)
    slope = pond_two + ground_two - (pond + ground)
    return (
        jnp.exp2((5.0 / 3.0 * LOG2E) * jnp.log(depth_face))
        * harmonic(conv, conv_two)
        * lax.rsqrt(jnp.abs(slope) + SLOPE_FLOOR)
    )


def surface_kernel(
    pond_ref, ground_ref, river_ref, from_above, from_below, level_ref, terms_ref,
):
    width = pond_ref.shape[1]
    quarter = width // 4
    window = quarter + 2 * LANES
    tail = pl.ds(from_above.shape[0] - ROWS, ROWS)
    lat = lax.axis_index("lat")
    start = pl.multiple_of(window_start(lax.axis_index("depth"), quarter, window), LANES)
    cut = pl.ds(start, window)
    upper_half = lax.broadcasted_iota(jnp.int32, (ROWS, window), 0) < 4
    conv_own = LAND_CONVEYANCE + (RIVER_CONVEYANCE - LAND_CONVEYANCE) * river_ref[:, cut].astype(jnp.float32)

    def extended(place, own):
        lanes = pl.ds(place * window, window)
        own = pltpu.roll(own, 4, 0)
        above = pltpu.roll(from_above[tail, lanes], 4, 0)
        below = from_below[tail, lanes]
        return jnp.concatenate(
            [jnp.where(upper_half, above, own), jnp.where(upper_half, own, below)], axis=0
        )

    pond = extended(0, pond_ref[:, cut])
    ground = extended(1, ground_ref[:, cut])
    conv = extended(2, conv_own)
    row = lax.broadcasted_iota(jnp.int32, conv.shape, 0)
    outside = ((row < 4) & (lat == 0)) | ((row >= 12) & (lat == lax.axis_size("lat") - 1))
    conv = jnp.where(outside, 0.0, conv)
    k_down = face_k(pond, ground, conv, lambda x: shift_rows(x, -1))
    k_up = shift_rows(k_down, 1)
    k_right = face_k(pond, ground, conv, lambda x: shift_lanes(x, -1))
    lane = lax.broadcasted_iota(jnp.int32, conv.shape, 1)
    k_right = jnp.where(lane < window - 1, k_right, 0.0)
    k_left = shift_lanes(k_right, 1)
    diag = 1.0 / SURFACE_STEP + k_up + k_down + k_left + k_right
    rhs = pond * (1.0 / SURFACE_STEP)
    rhs = rhs + k_up * (shift_rows(ground, 1) - ground) + k_down * (shift_rows(ground, -1) - ground)
    rhs = rhs + k_left * (shift_lanes(ground, 1) - ground) + k_right * (shift_lanes(ground, -1) - ground)
    inv = rcp(diag)
    level_ref[...] = pond
    for place, value in enumerate((k_up * inv, k_down * inv, k_left * inv, k_right * inv, rhs * inv, inv)):
        terms_ref[place] = value


def sweep_kernel(level_ref, terms_ref, exfil_ref, out_ref, last):
    quarter = out_ref.shape[1]
    k_up, k_down, k_left, k_right = (terms_ref[place] for place in range(4))
    rhs = terms_ref[4] + terms_ref[5] * exfil_ref[...]
    level = level_ref[...]
    for _ in range(SWEEPS):
        level = (
            rhs
            + k_up * shift_rows(level, 1)
            + k_down * shift_rows(level, -1)
            + k_left * shift_lanes(level, 1)
            + k_right * shift_lanes(level, -1)
        )
    last[...] = level
    depth = lax.axis_index("depth")
    start = pl.multiple_of(
        depth * quarter - window_start(depth, quarter, quarter + 2 * LANES), LANES
    )
    cut = pl.ds(start, quarter)
    lower_half = lax.broadcasted_iota(jnp.int32, (ROWS, quarter), 0) >= 4
    upper = pltpu.roll(last[pl.ds(0, ROWS), cut], 4, 0)
    lower = pltpu.roll(last[pl.ds(ROWS, ROWS), cut], 4, 0)
    out_ref[...] = jnp.where(lower_half, lower, upper)


def per_device(
    head, head_old, soil, cond_table, shape_table, pore_table, pond, ground, ponded, river
):
    nz, rows, width = head.shape
    window = width // 4 + 2 * LANES
    cells = nz * rows * width
    lat_count = lax.axis_size("lat")
    depth = lax.axis_index("depth")
    up = [(i, (i + 1) % lat_count) for i in range(lat_count)]
    down = [(j, i) for i, j in up]
    core = [(0, 1), (1, 0), (2, 3), (3, 2)]
    chip = [(0, 2), (2, 0), (1, 3), (3, 1)]

    own_up, own_down, exfil = pl.pallas_call(
        pack_kernel,
        out_shape=[f32(2 * nz + ROWS, width), f32(2 * nz + ROWS, width), f32(rows, width)],
        in_specs=[SMEM, SMEM, ANY, ANY, VMEM, VMEM, VMEM, VMEM],
        out_specs=[VMEM] * 3,
        scratch_shapes=[
            pltpu.VMEM((2, nz, width), jnp.int32),
            pltpu.VMEM((rows, width), jnp.int32),
            pltpu.VMEM((rows, width), jnp.float32),
            pltpu.SemaphoreType.DMA((6,)),
        ],
        compiler_params=params(),
        cost_estimate=cost(cells // 4),
        name="pack",
    )(cond_table, shape_table, head, soil, pond, ground, ponded, river)
    from_above = lax.ppermute(own_up, "lat", up)
    from_below = lax.ppermute(own_down, "lat", down)

    block = f32(nz, rows, width)
    head_v = in_vmem(head)
    base, ratio, inv, top_col, bottom_col, resist, sums, row_values = pl.pallas_call(
        cells_kernel,
        out_shape=[block] * 5 + [f32(3 * rows, width), f32(2 * rows, width), f32(6, nz, width)],
        in_specs=[SMEM] * 3 + [VMEM] * 5,
        out_specs=[VMEM] * 8,
        scratch_shapes=[
            pltpu.VMEM((nz, rows, width + LANES), jnp.float32),
            pltpu.VMEM((nz, rows, width + LANES), jnp.float32),
            pltpu.VMEM((nz, rows, LANES), jnp.float32),
            pltpu.SemaphoreType.DMA((6,)),
        ],
        compiler_params=params(),
        cost_estimate=cost(cells * 150, 20 * cells),
        name="cells",
    )(cond_table, shape_table, pore_table, head_v, in_vmem(head_old), in_vmem(soil), pond, ponded)

    even = depth % 2 == 0
    inner = (depth == 1) | (depth == 2)
    sign = jnp.where(depth < 2, 1.0, -1.0)
    r_top, r_bottom, corner = (resist[i * rows : (i + 1) * rows] for i in range(3))
    mine = jnp.concatenate([jnp.where(even, r_bottom, r_top), jnp.where(even, r_top, r_bottom), corner], 0)
    partner = lax.ppermute(mine, "depth", core)
    pair_inv = 1.0 / (mine[:rows] + partner[:rows])
    inner_corner = jnp.where(inner, mine[2 * rows :], partner[2 * rows :])
    gain = inner_corner * pair_inv
    chip_res = jnp.where(inner, mine[rows : 2 * rows], partner[rows : 2 * rows]) - inner_corner * gain
    chip_res_other = lax.ppermute(chip_res, "depth", chip)

    ends, flux, sent, kept = pl.pallas_call(
        halo_kernel,
        out_shape=[f32(2 * rows, width), f32(2, nz, width), f32(2 * rows, 2 * window), f32(2 * rows, 2 * window)],
        in_specs=[SMEM] * 2 + [VMEM] * 7,
        out_specs=[VMEM] * 4,
        compiler_params=params(),
        cost_estimate=cost(cells * 8),
        name="halo",
    )(
        cond_table, shape_table, in_vmem(own_up), in_vmem(own_down), in_vmem(from_above), in_vmem(from_below),
        in_vmem(row_values), in_vmem(sums), in_vmem(exfil),
    )
    ends_other = lax.ppermute(ends, "depth", core)
    exfil_core = lax.ppermute(sent, "depth", core)
    local = pl.pallas_call(
        local_kernel,
        out_shape=block,
        in_specs=[VMEM] * 5,
        out_specs=VMEM,
        compiler_params=params(),
        cost_estimate=cost(cells * 10),
        name="local",
    )(in_vmem(flux), in_vmem(base), in_vmem(ratio), in_vmem(inv), head_v)

    gap = sign * jnp.where(inner, ends_other[:rows] - ends[:rows], ends[:rows] - ends_other[:rows]) + 1.0
    chip_end = jnp.where(inner, ends[rows:], ends_other[rows:]) + sign * gain * gap
    chip_end_other = lax.ppermute(chip_end, "depth", chip)
    exfil_chip = lax.ppermute(
        jnp.where(depth == 0, kept[:, window:], exfil_core[:, window:]), "depth", chip
    )
    level, terms = pl.pallas_call(
        surface_kernel,
        out_shape=[f32(2 * rows, window), f32(6, 2 * rows, window)],
        in_specs=[VMEM] * 5,
        out_specs=[VMEM] * 2,
        compiler_params=params(),
        cost_estimate=cost(cells * 10),
        name="surface",
    )(pond, ground, river, in_vmem(from_above), in_vmem(from_below))

    flow_chip = (sign * (chip_end - chip_end_other) + 1.0) / (chip_res + chip_res_other)
    flow_core = gap * pair_inv + gain * flow_chip
    flow_in = jnp.where(depth == 0, 0.0, jnp.where(depth == 2, flow_chip, flow_core))
    flow_out = jnp.where(depth == 3, 0.0, jnp.where(depth == 1, flow_chip, flow_core))
    head_new = pl.pallas_call(
        final_kernel,
        out_shape=jax.ShapeDtypeStruct((nz, rows, width), jnp.float32),
        in_specs=[VMEM] * 5,
        out_specs=VMEM,
        compiler_params=params(),
        cost_estimate=cost(cells * 4),
        name="final",
    )(in_vmem(local), in_vmem(top_col), in_vmem(bottom_col), flow_in, flow_out)

    exfil_near = jnp.where(depth == 0, kept[:, :window], exfil_core[:, :window])
    exfil_window = jnp.where(depth < 2, exfil_near, exfil_chip)
    surface_new = pl.pallas_call(
        sweep_kernel,
        out_shape=jax.ShapeDtypeStruct((rows, width // 4), jnp.float32),
        in_specs=[VMEM] * 3,
        out_specs=VMEM,
        scratch_shapes=[pltpu.VMEM((2 * rows, window), jnp.float32)],
        compiler_params=params(),
        cost_estimate=cost(cells),
        name="sweep",
    )(in_vmem(level), in_vmem(terms), exfil_window)
    return (head_new, surface_new)


def solution(mesh):
    placed = (
        P("depth", "lat", None),
        P("depth", "lat", None),
        P("depth", "lat", None),
        P(),
        P(),
        P(),
        P("lat", None),
        P("lat", None),
        P("lat", None),
        P("lat", None),
    )
    return jax.shard_map(
        per_device,
        mesh=mesh,
        in_specs=placed,
        out_specs=(P("depth", "lat", None), P("lat", "depth")),
        check_vma=False,
    )
```

time: 257 us -> 75.5 us (0.29)
  the two profiles are of different devices: /device:TPU:25 before, /device:TPU:1 now
where the time goes in v1:
time: 75.5 us; the launch traced here: 74.8 us
  Pallas kernels  25.4 us (34%)
  local copies, waits for them, and re-layouts  23.6 us (31%)
  starting transfers between devices  14.9 us (20%)
  other arithmetic  5.89 us (8%)
  waiting for transfers between devices  4.08 us (5%)
  between operations  0.88 us (1%)
    unnamed x76, local copies, waits for them, and re-layouts  23.6 us
    pallas_call x1, Pallas kernels, per_device(): pl.pallas_call(cells_kernel, out_shape=[block] * 5 + [f32(3 * rows, width...  14.3 us
    ppermute x1, starting transfers between devices, per_device(): from_below = lax.ppermute(own_down, 'lat', down)  8.85 us
    pallas_call x1, Pallas kernels, per_device(): pl.pallas_call(halo_kernel, out_shape=[f32(2 * rows, width), f32(2, nz, w...  4.42 us
    pallas_call x1, Pallas kernels, per_device(): pl.pallas_call(pack_kernel, out_shape=[f32(2 * nz + ROWS, width), f32(2 *...  3.02 us
    ppermute x1, waiting for transfers between devices, per_device(): chip_end_other = lax.ppermute(chip_end, 'depth', chip)  2.81 us
    ppermute x1, starting transfers between devices, per_device(): from_above = lax.ppermute(own_up, 'lat', up)  2.54 us
    pallas_call x1, Pallas kernels, per_device(): pl.pallas_call(final_kernel, out_shape=jax.ShapeDtypeStruct((nz, rows, wi...  1.65 us
  transfers between devices with their start and end apart: 8, of which 2 were waited for; matrix products, arithmetic and copies ran while one was open for 7% of the time, Pallas kernels for 22%

profile of v1, /device:TPU:1, one launch (start us, length us, event | category | flops | bytes accessed | tf_op | source)
XLA Modules:
  0.0 74.8 jit_solution(12472990497118750940)
XLA Ops:
  0.6 1.6 %copy-done = f32[16,8,4096]{2,1,0:T(8,128)S(1)} copy-done((f32[16,8,4096]{2,1,0:T(8,128)S(1)}, f32[16,8,4096]{2,1,0:T(8,128)}, u32[]{:S(2)}) %copy-start) | copy-done | bytes 2097176
  2.2 1.6 %copy-done.2 = s32[16,8,4096]{2,1,0:T(8,128)S(1)} copy-done((s32[16,8,4096]{2,1,0:T(8,128)S(1)}, s32[16,8,4096]{2,1,0:T(8,128)}, u32[]{:S(2)}) %copy-start.2) | copy-done | bytes 2097176
  3.8 0.9 %copy-done.15 = f32[8,4096]{1,0:T(8,128)S(1)} copy-done((f32[8,4096]{1,0:T(8,128)S(1)}, f32[8,4096]{1,0:T(8,128)}, u32[]{:S(2)}) %copy-start.15) | copy-done | bytes 131096
  4.7 0.9 %copy-done.21 = s32[8,4096]{1,0:T(8,128)S(1)} copy-done((s32[8,4096]{1,0:T(8,128)S(1)}, s32[8,4096]{1,0:T(8,128)}, u32[]{:S(2)}) %copy-start.21) | copy-done | bytes 131096
  5.6 0.9 %copy-done.22 = f32[8,4096]{1,0:T(8,128)S(1)} copy-done((f32[8,4096]{1,0:T(8,128)S(1)}, f32[8,4096]{1,0:T(8,128)}, u32[]{:S(2)}) %copy-start.22) | copy-done | bytes 131096
  6.5 0.9 %copy-done.24 = s32[8,4096]{1,0:T(8,128)S(1)} copy-done((s32[8,4096]{1,0:T(8,128)S(1)}, s32[8,4096]{1,0:T(8,128)}, u32[]{:S(2)}) %copy-start.24) | copy-done | bytes 131096
  7.4 0.7 copy-done.30
  8.1 0.7 copy-done.32
  8.7 3.0 %pack.1 = (f32[40,4096]{1,0:T(8,128)}, f32[40,4096]{1,0:T(8,128)}, f32[8,4096]{1,0:T(8,128)S(1)}) custom-call(f32[12]{0:T(128)S(1)} %copy-done.30, f32[12]{0:T(128)S(1)} %copy-done.32, f32[16,8,4096]{2,1,0:T(8,128)S(1)} %copy-done, s32[16,8,4096]{2,1,0:T(8,128)S(1)} %copy-done.2, f32[8,4096]{1,0:T(8,128)S(1)} %copy-done.15, f32[8,4096]{1,0:T(8,128)S(1)} %copy-done.22, ...), custom_call_target="tpu_custom_call" | custom-call | flops 131072 | tf_op jit(solution)/shard_map/pack/pallas_call | solution.py:458
  11.8 2.5 %collective-permute-start = (f32[40,4096]{1,0:T(8,128)}, f32[40,4096]{1,0:T(8,128)S(1)}, u32[]{:S(2)}, u32[]{:S(2)}) collective-permute-start(f32[40,4096]{1,0:T(8,128)} %get-tuple-element.19.own_up), channel_id=1, source_target_pairs={{0,4},{4,8},{8,12},{12,16},{16,20},{20,24},{24,28},{28,32},{32,36}... | collective-permute-start | bytes 1966088 | tf_op jit(solution)/shard_map/ppermute | solution.py:473
  14.3 8.9 %collective-permute-start.1 = (f32[40,4096]{1,0:T(8,128)}, f32[40,4096]{1,0:T(8,128)S(1)}, u32[]{:S(2)}, u32[]{:S(2)}) collective-permute-start(f32[40,4096]{1,0:T(8,128)} %get-tuple-element.20.own_down), channel_id=1, source_target_pairs={{4,0},{8,4},{12,8},{16,12},{20,16},{24,20},{28,24},{32,28},{36,32}... | collective-permute-start | bytes 1966088 | tf_op jit(solution)/shard_map/ppermute | solution.py:474
  23.2 1.6 %copy-done.3 = s32[16,8,4096]{2,1,0:T(8,128)S(1)} copy-done((s32[16,8,4096]{2,1,0:T(8,128)S(1)}, s32[16,8,4096]{2,1,0:T(8,128)}, u32[]{:S(2)}) %copy-start.3) | copy-done | bytes 2097176
  24.8 1.6 %copy-done.4 = f32[16,8,4096]{2,1,0:T(8,128)S(1)} copy-done((f32[16,8,4096]{2,1,0:T(8,128)S(1)}, f32[16,8,4096]{2,1,0:T(8,128)}, u32[]{:S(2)}) %copy-start.4) | copy-done | bytes 2097176
  26.4 14.3 %cells.1 = (f32[16,8,4096]{2,1,0:T(8,128)S(1)}, f32[16,8,4096]{2,1,0:T(8,128)S(1)}, f32[16,8,4096]{2,1,0:T(8,128)S(1)}, f32[16,8,4096]{2,1,0:T(8,128)S(1)}, f32[...) custom-call(f32[12]{0:T(128)} %cond_ref.5, ...), custom_call_target="tpu_custom_call" | custom-call | flops 78643200 | bytes 10485760 | tf_op jit(solution)/shard_map/cells/pallas_call | solution.py:478
  40.6 0.0 copy-start.9
  40.6 1.3 %copy-done.9 = f32[16,8,4096]{2,1,0:T(8,128)} copy-done((f32[16,8,4096]{2,1,0:T(8,128)}, f32[16,8,4096]{2,1,0:T(8,128)S(1)}, u32[]{:S(2)}) %copy-start.9) | copy-done | bytes 2097176
  42.0 1.4 %copy-done.11 = f32[16,8,4096]{2,1,0:T(8,128)} copy-done((f32[16,8,4096]{2,1,0:T(8,128)}, f32[16,8,4096]{2,1,0:T(8,128)S(1)}, u32[]{:S(2)}) %copy-start.11) | copy-done | bytes 2097176
  43.3 1.4 %copy-done.13 = f32[16,8,4096]{2,1,0:T(8,128)} copy-done((f32[16,8,4096]{2,1,0:T(8,128)}, f32[16,8,4096]{2,1,0:T(8,128)S(1)}, u32[]{:S(2)}) %copy-start.13) | copy-done | bytes 2097176
  44.8 0.0 collective-permute-done.1.from_below
  44.8 4.4 %halo.1 = (f32[16,4096]{1,0:T(8,128)S(1)}, f32[2,16,4096]{2,1,0:T(8,128)S(1)}, f32[16,2560]{1,0:T(8,128)}, f32[16,2560]{1,0:T(8,128)S(1)}) custom-call(f32[12]{0:T(128)S(1)} %copy-done.31, f32[12]{0:T(128)S(1)} %copy-done.33, f32[40,4096]{1,0:T(8,128)} %get-tuple-element.19.own_up, f32[40,4096]{1,0:T(8,128)} %get-tuple-element.20.own_down, ...), custom_call_target="tpu_custom_call" | custom-call | flops 4194304 | tf_op jit(solution)/shard_map/halo/pallas_call | solution.py:506
  49.3 0.7 copy-done.19
  50.0 0.8 %copy-done.26 = f32[2,16,4096]{2,1,0:T(8,128)} copy-done((f32[2,16,4096]{2,1,0:T(8,128)}, f32[2,16,4096]{2,1,0:T(8,128)S(1)}, u32[]{:S(2)}) %copy-start.26) | copy-done | bytes 524312
  50.8 0.7 copy-done.28
  51.4 1.0 %collective-permute-start.6 = (f32[16,2560]{1,0:T(8,128)}, f32[16,2560]{1,0:T(8,128)}, u32[]{:S(2)}, u32[]{:S(2)}) collective-permute-start(f32[16,2560]{1,0:T(8,128)} %get-tuple-element.35), channel_id=1, source_target_pairs={{0,1},{1,0},{2,3},{3,2},{4,5},{5,4},{6,7},{7,6},{8,9},{9,8},{10,11... | collective-permute-start | bytes 491528 | tf_op jit(solution)/shard_map/ppermute | solution.py:519
  52.4 0.8 %pad_maximum_fusion = f32[24,4096]{1,0:T(8,128)} fusion(f32[8,4096]{1,0:T(8,128)S(1)} %get-tuple-element.42, f32[8,4096]{1,0:T(8,128)S(1)} %get-tuple-element.40, f32[8,4096]{1,0:T(8,128)S(1)} %get-tuple-element.41), kind=kLoop, calls=%fused_computation | loop fusion | flops 196608 | bytes 786432 | tf_op jit(solution)/shard_map/concatenate | solution.py:498
  53.2 0.0 collective-permute-start.3
  53.2 0.5 collective-permute-start.2
  53.7 1.6 %copy-done.10 = f32[16,8,4096]{2,1,0:T(8,128)S(1)} copy-done((f32[16,8,4096]{2,1,0:T(8,128)S(1)}, f32[16,8,4096]{2,1,0:T(8,128)}, u32[]{:S(2)}) %copy-start.10) | copy-done | bytes 2097176
  55.3 1.6 %copy-done.12 = f32[16,8,4096]{2,1,0:T(8,128)S(1)} copy-done((f32[16,8,4096]{2,1,0:T(8,128)S(1)}, f32[16,8,4096]{2,1,0:T(8,128)}, u32[]{:S(2)}) %copy-start.12) | copy-done | bytes 2097176
  56.9 1.6 %copy-done.14 = f32[16,8,4096]{2,1,0:T(8,128)S(1)} copy-done((f32[16,8,4096]{2,1,0:T(8,128)S(1)}, f32[16,8,4096]{2,1,0:T(8,128)}, u32[]{:S(2)}) %copy-start.14) | copy-done | bytes 2097176
  58.4 1.0 %copy-done.27 = f32[2,16,4096]{2,1,0:T(8,128)S(1)} copy-done((f32[2,16,4096]{2,1,0:T(8,128)S(1)}, f32[2,16,4096]{2,1,0:T(8,128)}, u32[]{:S(2)}) %copy-start.27) | copy-done | bytes 524312
  59.5 0.8 %local.1.local_ref = f32[16,8,4096]{2,1,0:T(8,128)S(1)} custom-call(f32[2,16,4096]{2,1,0:T(8,128)S(1)} %copy-done.27, f32[16,8,4096]{2,1,0:T(8,128)S(1)} %copy-done.10, f32[16,8,4096]{2,1,0:T(8,128)S(1)} %copy-done.12, f32[16,8,4096]{2,1,0:T(8,128)S(1)} %copy-done.14, f32[16,8,4096]{2,1,0:T(8,128)S(1)} %copy-done.1), custom_call_target="tpu_custom_call" | custom-call | flops 5242880 | tf_op jit(solution)/shard_map/local/pallas_call | solution.py:520
  60.3 0.1 copy-done.16
  60.4 0.1 copy-done.23
  60.5 0.1 copy-done.25
  60.5 0.3 surface.1
  60.8 0.9 %slice_select_fusion.5 = f32[16,1280]{1,0:T(8,128)S(1)} fusion(f32[16,2560]{1,0:T(8,128)} %collective-permute-done.6, f32[16,2560]{1,0:T(8,128)S(1)} %copy-done.29, pred[]{:T(512)S(6)} %eq.21), kind=kLoop, calls=%fused_computation.15 | loop fusion | flops 20480 | bytes 245761 | tf_op jit(solution)/shard_map/jit(_where)/select_n | solution.py:534
  61.8 0.5 collective-permute-start.7
  62.3 1.3 %fusion.2 = (f32[8,4096]{1,0:T(8,128)S(1)}, f32[8,4096]{1,0:T(8,128)S(1)}) fusion(f32[16,4096]{1,0:T(8,128)S(1)} %collective-permute-done.2, f32[16,4096]{1,0:T(8,128)S(1)} %copy-done.20, f32[]{:T(128)S(6)} %select_n.87, pred[]{:T(512)S(6)} %or.3, f32[8,4096]{1,0:T(8,128)S(1)} %copy-done.35, f32[24,4096]{1,0:T(8,128)} %collective-permute-done.3, ...), kind=kLoop, calls=%fused_computation.7 | loop fusion | flops 425984 | bytes 1310725 | tf_op jit(solution)/shard_map/add | solution.py:531
  63.6 1.0 %fusion = f32[8,4096]{1,0:T(8,128)S(1)} fusion(f32[8,4096]{1,0:T(8,128)S(1)} %copy-done.37, f32[24,4096]{1,0:T(8,128)} %collective-permute-done.3, f32[8,4096]{1,0:T(8,128)S(1)} %get-tuple-element.37, pred[]{:T(512)S(6)} %or.3, f32[24,4096]{1,0:T(8,128)S(1)} %copy-done.18), kind=kLoop, calls=%fused_computation.2 | loop fusion | flops 131072 | bytes 786433 | tf_op jit(solution)/shard_map/sub | solution.py:503
  64.6 0.9 %collective-permute-start.5 = (f32[8,4096]{1,0:T(8,128)S(1)}, f32[8,4096]{1,0:T(8,128)S(1)}, u32[]{:S(2)}, u32[]{:S(2)}) collective-permute-start(f32[8,4096]{1,0:T(8,128)S(1)} %fusion), channel_id=1, source_target_pairs={{0,2},{2,0},{1,3},{3,1},{4,6},{6,4},{5,7},{7,5},{8,10},{10,8},{9,1... | collective-permute-start | bytes 393224 | tf_op jit(solution)/shard_map/ppermute | solution.py:504
  65.5 0.6 collective-permute-start.4
  66.2 0.9 %fusion.3.exfil_ref = f32[16,1280]{1,0:T(8,128)S(1)} fusion(f32[16,1280]{1,0:T(8,128)S(1)} %collective-permute-done.7, f32[16,2560]{1,0:T(8,128)} %collective-permute-done.6, f32[16,2560]{1,0:T(8,128)S(1)} %copy-done.29, pred[]{:T(512)S(6)} %eq.21, pred[]{:T(512)S(6)} %lt.10), kind=kLoop, calls=%fused_computation.17 | loop fusion | flops 40960 | bytes 327682 | tf_op jit(solution)/shard_map/jit(_where)/select_n | solution.py:561
  67.1 1.0 %sweep.1 = f32[8,1024]{1,0:T(8,128)} custom-call(f32[16,1280]{1,0:T(8,128)S(1)} %get-tuple-element.32.level_ref, f32[6,16,1280]{2,1,0:T(8,128)S(1)} %get-tuple-element.33.terms_ref, f32[16,1280]{1,0:T(8,128)S(1)} %fusion.3.exfil_ref), custom_call_target="tpu_custom_call" | custom-call | flops 524288 | tf_op jit(solution)/shard_map/sweep/pallas_call | solution.py:562
  68.1 1.3 %collective-permute-done.5 = f32[8,4096]{1,0:T(8,128)S(1)} collective-permute-done((f32[8,4096]{1,0:T(8,128)S(1)}, f32[8,4096]{1,0:T(8,128)S(1)}, u32[]{:S(2)}, u32[]{:S(2)}) %collective-permute-start.5) | collective-permute-done | bytes 131104 | tf_op jit(solution)/shard_map/ppermute | solution.py:504
  69.3 2.8 %collective-permute-done.4 = f32[8,4096]{1,0:T(8,128)S(1)} collective-permute-done((f32[8,4096]{1,0:T(8,128)S(1)}, f32[8,4096]{1,0:T(8,128)S(1)}, u32[]{:S(2)}, u32[]{:S(2)}) %collective-permute-start.4) | collective-permute-done | bytes 131104 | tf_op jit(solution)/shard_map/ppermute | solution.py:532
  72.1 1.0 %select_select_fusion = (f32[8,4096]{1,0:T(8,128)S(1)}, f32[8,4096]{1,0:T(8,128)S(1)}) fusion(pred[]{:T(512)S(6)} %eq.23, pred[]{:T(512)S(6)} %eq.25, f32[8,4096]{1,0:T(8,128)S(1)} %get-tuple-element.37, f32[8,4096]{1,0:T(8,128)S(1)} %fusion, f32[8,4096]{1,0:T(8,128)S(1)} %collective-permute-done.5, f32[8,4096]{1,0:T(8,128)S(1)} %get-tuple-element.36, ...), kind=kLoop, calls=%fused_computation.8 | loop fusion | flops 622592 | bytes 1441801 | tf_op jit(solution)/shard_map/jit(_where)/select_n | solution.py:549
  73.2 1.7 %final.1 = f32[16,8,4096]{2,1,0:T(8,128)} custom-call(f32[16,8,4096]{2,1,0:T(8,128)S(1)} %local.1.local_ref, f32[16,8,4096]{2,1,0:T(8,128)S(1)} %copy-done.6, f32[16,8,4096]{2,1,0:T(8,128)S(1)} %copy-done.8, f32[8,4096]{1,0:T(8,128)S(1)} %get-tuple-element.39.flow_in, f32[8,4096]{1,0:T(8,128)S(1)} %get-tuple-element.38.flow_out), custom_call_target="tpu_custom_call" | custom-call | flops 2097152 | tf_op jit(solution)/shard_map/final/pallas_call | solution.py:550
  (58 shorter events, 0.1 us)
Async XLA Ops:
  0.6 1.6 %copy-start = (f32[16,8,4096]{2,1,0:T(8,128)S(1)}, f32[16,8,4096]{2,1,0:T(8,128)}, u32[]{:S(2)}) copy-start(f32[16,8,4096]{2,1,0:T(8,128)} %head_ref.5) | copy-start | bytes 6291460
  2.2 1.6 %copy-start.2 = (s32[16,8,4096]{2,1,0:T(8,128)S(1)}, s32[16,8,4096]{2,1,0:T(8,128)}, u32[]{:S(2)}) copy-start(s32[16,8,4096]{2,1,0:T(8,128)} %soil_ref.3) | copy-start | bytes 6291460
  3.8 0.9 %copy-start.15 = (f32[8,4096]{1,0:T(8,128)S(1)}, f32[8,4096]{1,0:T(8,128)}, u32[]{:S(2)}) copy-start(f32[8,4096]{1,0:T(8,128)} %pond_ref.5) | copy-start | bytes 393220
  4.7 0.9 %copy-start.21 = (s32[8,4096]{1,0:T(8,128)S(1)}, s32[8,4096]{1,0:T(8,128)}, u32[]{:S(2)}) copy-start(s32[8,4096]{1,0:T(8,128)} %ponded_ref.3) | copy-start | bytes 393220
  5.6 0.9 %copy-start.22 = (f32[8,4096]{1,0:T(8,128)S(1)}, f32[8,4096]{1,0:T(8,128)}, u32[]{:S(2)}) copy-start(f32[8,4096]{1,0:T(8,128)} %ground_ref.3) | copy-start | bytes 393220
  6.5 0.9 %copy-start.24 = (s32[8,4096]{1,0:T(8,128)S(1)}, s32[8,4096]{1,0:T(8,128)}, u32[]{:S(2)}) copy-start(s32[8,4096]{1,0:T(8,128)} %river_ref.3) | copy-start | bytes 393220
  7.4 0.7 copy-start.30
  8.1 0.7 copy-start.32
  8.7 14.4 %copy-start.1 = (f32[16,8,4096]{2,1,0:T(8,128)S(1)}, f32[16,8,4096]{2,1,0:T(8,128)}, u32[]{:S(2)}) copy-start(f32[16,8,4096]{2,1,0:T(8,128)} %head_ref.5) | copy-start | bytes 6291460
  11.8 33.0 %collective-permute-start = (f32[40,4096]{1,0:T(8,128)}, f32[40,4096]{1,0:T(8,128)S(1)}, u32[]{:S(2)}, u32[]{:S(2)}) collective-permute-start(f32[40,4096]{1,0:T(8,128)} %get-tuple-element.19.own_up), channel_id=1, source_target_pairs={{0,4},{4,8},{8,12},{12,16},{16,20},{20,24},{24,28},{28,32},{32,36}... | collective-permute-start | bytes 1966088 | tf_op jit(solution)/shard_map/ppermute | solution.py:473
  14.3 30.5 %collective-permute-start.1 = (f32[40,4096]{1,0:T(8,128)}, f32[40,4096]{1,0:T(8,128)S(1)}, u32[]{:S(2)}, u32[]{:S(2)}) collective-permute-start(f32[40,4096]{1,0:T(8,128)} %get-tuple-element.20.own_down), channel_id=1, source_target_pairs={{4,0},{8,4},{12,8},{16,12},{20,16},{24,20},{28,24},{32,28},{36,32}... | collective-permute-start | bytes 1966088 | tf_op jit(solution)/shard_map/ppermute | solution.py:474
  23.2 1.6 %copy-start.3 = (s32[16,8,4096]{2,1,0:T(8,128)S(1)}, s32[16,8,4096]{2,1,0:T(8,128)}, u32[]{:S(2)}) copy-start(s32[16,8,4096]{2,1,0:T(8,128)} %soil_ref.3) | copy-start | bytes 6291460
  24.8 1.6 %copy-start.4 = (f32[16,8,4096]{2,1,0:T(8,128)S(1)}, f32[16,8,4096]{2,1,0:T(8,128)}, u32[]{:S(2)}) copy-start(f32[16,8,4096]{2,1,0:T(8,128)} %old_ref.1) | copy-start | bytes 6291460
  26.4 18.4 %copy-start.31 = (f32[12]{0:T(128)S(1)}, f32[12]{0:T(128)}, u32[]{:S(2)}) copy-start(f32[12]{0:T(128)} %cond_ref.5) | copy-start | bytes 148
  26.4 18.4 %copy-start.33 = (f32[12]{0:T(128)S(1)}, f32[12]{0:T(128)}, u32[]{:S(2)}) copy-start(f32[12]{0:T(128)} %shape_ref.5) | copy-start | bytes 148
  40.6 1.3 %copy-start.9 = (f32[16,8,4096]{2,1,0:T(8,128)}, f32[16,8,4096]{2,1,0:T(8,128)S(1)}, u32[]{:S(2)}) copy-start(f32[16,8,4096]{2,1,0:T(8,128)S(1)} %get-tuple-element.25.base) | copy-start | bytes 6291460
  42.0 1.4 %copy-start.11 = (f32[16,8,4096]{2,1,0:T(8,128)}, f32[16,8,4096]{2,1,0:T(8,128)S(1)}, u32[]{:S(2)}) copy-start(f32[16,8,4096]{2,1,0:T(8,128)S(1)} %get-tuple-element.26.ratio) | copy-start | bytes 6291460
  43.3 1.4 %copy-start.13 = (f32[16,8,4096]{2,1,0:T(8,128)}, f32[16,8,4096]{2,1,0:T(8,128)S(1)}, u32[]{:S(2)}) copy-start(f32[16,8,4096]{2,1,0:T(8,128)S(1)} %get-tuple-element.27.inv) | copy-start | bytes 6291460
  44.7 4.5 %copy-start.5 = (f32[16,8,4096]{2,1,0:T(8,128)}, f32[16,8,4096]{2,1,0:T(8,128)S(1)}, u32[]{:S(2)}) copy-start(f32[16,8,4096]{2,1,0:T(8,128)S(1)} %get-tuple-element.28.top_col) | copy-start | bytes 6291460
  44.7 4.5 %copy-start.7 = (f32[16,8,4096]{2,1,0:T(8,128)}, f32[16,8,4096]{2,1,0:T(8,128)S(1)}, u32[]{:S(2)}) copy-start(f32[16,8,4096]{2,1,0:T(8,128)S(1)} %get-tuple-element.29.bottom_col) | copy-start | bytes 6291460
  44.7 4.5 %copy-start.17 = (f32[24,4096]{1,0:T(8,128)}, f32[24,4096]{1,0:T(8,128)S(1)}, u32[]{:S(2)}) copy-start(f32[24,4096]{1,0:T(8,128)S(1)} %get-tuple-element.31) | copy-start | bytes 1179652
  44.8 7.6 %copy-start.34 = (f32[8,4096]{1,0:T(8,128)}, f32[8,4096]{1,0:T(8,128)S(1)}, u32[]{:S(2)}) copy-start(f32[8,4096]{1,0:T(8,128)S(1)} %get-tuple-element.41) | copy-start | bytes 393220
  44.8 7.6 %copy-start.36 = (f32[8,4096]{1,0:T(8,128)}, f32[8,4096]{1,0:T(8,128)S(1)}, u32[]{:S(2)}) copy-start(f32[8,4096]{1,0:T(8,128)S(1)} %get-tuple-element.40) | copy-start | bytes 393220
  49.2 0.7 copy-start.19
  50.0 0.8 %copy-start.26 = (f32[2,16,4096]{2,1,0:T(8,128)}, f32[2,16,4096]{2,1,0:T(8,128)S(1)}, u32[]{:S(2)}) copy-start(f32[2,16,4096]{2,1,0:T(8,128)S(1)} %get-tuple-element.24.flux_ref) | copy-start | bytes 1572868
  50.8 0.7 copy-start.28
  51.4 9.4 %collective-permute-start.6 = (f32[16,2560]{1,0:T(8,128)}, f32[16,2560]{1,0:T(8,128)}, u32[]{:S(2)}, u32[]{:S(2)}) collective-permute-start(f32[16,2560]{1,0:T(8,128)} %get-tuple-element.35), channel_id=1, source_target_pairs={{0,1},{1,0},{2,3},{3,2},{4,5},{5,4},{6,7},{7,6},{8,9},{9,8},{10,11... | collective-permute-start | bytes 491528 | tf_op jit(solution)/shard_map/ppermute | solution.py:519
  53.2 9.1 %collective-permute-start.3 = (f32[24,4096]{1,0:T(8,128)}, f32[24,4096]{1,0:T(8,128)}, u32[]{:S(2)}, u32[]{:S(2)}) collective-permute-start(f32[24,4096]{1,0:T(8,128)} %pad_maximum_fusion), channel_id=1, source_target_pairs={{0,1},{1,0},{2,3},{3,2},{4,5},{5,4},{6,7},{7,6},{8,9},{9,8},{10,11... | collective-permute-start | bytes 1179656 | tf_op jit(solution)/shard_map/ppermute | solution.py:499
  53.2 9.1 %collective-permute-start.2 = (f32[16,4096]{1,0:T(8,128)}, f32[16,4096]{1,0:T(8,128)S(1)}, u32[]{:S(2)}, u32[]{:S(2)}) collective-permute-start(f32[16,4096]{1,0:T(8,128)} %copy-done.19), channel_id=1, source_target_pairs={{0,1},{1,0},{2,3},{3,2},{4,5},{5,4},{6,7},{7,6},{8,9},{9,8},{10,11... | collective-permute-start | bytes 786440 | tf_op jit(solution)/shard_map/ppermute | solution.py:518
  53.7 1.6 %copy-start.10 = (f32[16,8,4096]{2,1,0:T(8,128)S(1)}, f32[16,8,4096]{2,1,0:T(8,128)}, u32[]{:S(2)}) copy-start(f32[16,8,4096]{2,1,0:T(8,128)} %copy-done.9) | copy-start | bytes 6291460
  55.3 1.6 %copy-start.12 = (f32[16,8,4096]{2,1,0:T(8,128)S(1)}, f32[16,8,4096]{2,1,0:T(8,128)}, u32[]{:S(2)}) copy-start(f32[16,8,4096]{2,1,0:T(8,128)} %copy-done.11) | copy-start | bytes 6291460
  56.9 1.6 %copy-start.14 = (f32[16,8,4096]{2,1,0:T(8,128)S(1)}, f32[16,8,4096]{2,1,0:T(8,128)}, u32[]{:S(2)}) copy-start(f32[16,8,4096]{2,1,0:T(8,128)} %copy-done.13) | copy-start | bytes 6291460
  58.4 1.0 %copy-start.27 = (f32[2,16,4096]{2,1,0:T(8,128)S(1)}, f32[2,16,4096]{2,1,0:T(8,128)}, u32[]{:S(2)}) copy-start(f32[2,16,4096]{2,1,0:T(8,128)} %copy-done.26) | copy-start | bytes 1572868
  59.5 0.9 %copy-start.16 = (f32[8,4096]{1,0:T(8,128)S(1)}, f32[8,4096]{1,0:T(8,128)}, u32[]{:S(2)}) copy-start(f32[8,4096]{1,0:T(8,128)} %pond_ref.5) | copy-start | bytes 393220
  59.5 1.0 %copy-start.23 = (f32[8,4096]{1,0:T(8,128)S(1)}, f32[8,4096]{1,0:T(8,128)}, u32[]{:S(2)}) copy-start(f32[8,4096]{1,0:T(8,128)} %ground_ref.3) | copy-start | bytes 393220
  59.5 1.0 %copy-start.25 = (s32[8,4096]{1,0:T(8,128)S(1)}, s32[8,4096]{1,0:T(8,128)}, u32[]{:S(2)}) copy-start(s32[8,4096]{1,0:T(8,128)} %river_ref.3) | copy-start | bytes 393220
  59.5 1.3 %copy-start.29 = (f32[16,2560]{1,0:T(8,128)S(1)}, f32[16,2560]{1,0:T(8,128)}, u32[]{:S(2)}) copy-start(f32[16,2560]{1,0:T(8,128)} %copy-done.28) | copy-start | bytes 491524
  59.5 2.8 %copy-start.18 = (f32[24,4096]{1,0:T(8,128)S(1)}, f32[24,4096]{1,0:T(8,128)}, u32[]{:S(2)}) copy-start(f32[24,4096]{1,0:T(8,128)} %copy-done.17) | copy-start | bytes 1179652
  59.5 2.8 %copy-start.35 = (f32[8,4096]{1,0:T(8,128)S(1)}, f32[8,4096]{1,0:T(8,128)}, u32[]{:S(2)}) copy-start(f32[8,4096]{1,0:T(8,128)} %copy-done.34) | copy-start | bytes 393220
  60.5 1.8 %copy-start.20 = (f32[16,4096]{1,0:T(8,128)S(1)}, f32[16,4096]{1,0:T(8,128)}, u32[]{:S(2)}) copy-start(f32[16,4096]{1,0:T(8,128)} %copy-done.19) | copy-start | bytes 786436
  60.5 3.1 %copy-start.37 = (f32[8,4096]{1,0:T(8,128)S(1)}, f32[8,4096]{1,0:T(8,128)}, u32[]{:S(2)}) copy-start(f32[8,4096]{1,0:T(8,128)} %copy-done.36) | copy-start | bytes 393220
  61.7 11.4 %copy-start.6 = (f32[16,8,4096]{2,1,0:T(8,128)S(1)}, f32[16,8,4096]{2,1,0:T(8,128)}, u32[]{:S(2)}) copy-start(f32[16,8,4096]{2,1,0:T(8,128)} %copy-done.5) | copy-start | bytes 6291460
  61.8 11.4 %copy-start.8 = (f32[16,8,4096]{2,1,0:T(8,128)S(1)}, f32[16,8,4096]{2,1,0:T(8,128)}, u32[]{:S(2)}) copy-start(f32[16,8,4096]{2,1,0:T(8,128)} %copy-done.7) | copy-start | bytes 6291460
  61.8 4.4 %collective-permute-start.7 = (f32[16,1280]{1,0:T(8,128)S(1)}, f32[16,1280]{1,0:T(8,128)S(1)}, u32[]{:S(2)}, u32[]{:S(2)}) collective-permute-start(f32[16,1280]{1,0:T(8,128)S(1)} %slice_select_fusion.5), channel_id=1, source_target_pairs={{0,2},{2,0},{1,3},{3,1},{4,6},{6,4},{5,7},{7,5},{8,10},{10,8},{9,1... | collective-permute-start | bytes 245768 | tf_op jit(solution)/shard_map/ppermute | solution.py:533
  64.6 4.7 %collective-permute-start.5 = (f32[8,4096]{1,0:T(8,128)S(1)}, f32[8,4096]{1,0:T(8,128)S(1)}, u32[]{:S(2)}, u32[]{:S(2)}) collective-permute-start(f32[8,4096]{1,0:T(8,128)S(1)} %fusion), channel_id=1, source_target_pairs={{0,2},{2,0},{1,3},{3,1},{4,6},{6,4},{5,7},{7,5},{8,10},{10,8},{9,1... | collective-permute-start | bytes 393224 | tf_op jit(solution)/shard_map/ppermute | solution.py:504
  65.5 6.6 %collective-permute-start.4 = (f32[8,4096]{1,0:T(8,128)S(1)}, f32[8,4096]{1,0:T(8,128)S(1)}, u32[]{:S(2)}, u32[]{:S(2)}) collective-permute-start(f32[8,4096]{1,0:T(8,128)S(1)} %get-tuple-element.36), channel_id=1, source_target_pairs={{0,2},{2,0},{1,3},{3,1},{4,6},{6,4},{5,7},{7,5},{8,10},{10,8},{9,1... | collective-permute-start | bytes 393224 | tf_op jit(solution)/shard_map/ppermute | solution.py:532

commit v2 on v1

v2 whole, which is shorter than its diff:
```python
import jax
import jax.numpy as jnp
from jax import lax
from jax.experimental import pallas as pl
from jax.experimental.pallas import tpu as pltpu
from jax.sharding import PartitionSpec as P

SWEEPS = 4

TIME_STEP = 20.0
SURFACE_STEP = 2.0
SPECIFIC_STORAGE = 0.01
LAND_CONVEYANCE = 3.0
RIVER_CONVEYANCE = 10.0
SLOPE_FLOOR = 0.01

LOG2E = 1.4426950408889634
LN2 = 0.6931471805599453
CLOSED = 1e37

LANES = 128
ROWS = 8
CHUNK = 512
VMEM_LIMIT = 6 * 1024 * 1024

VMEM = pl.BlockSpec(memory_space=pltpu.VMEM)
ANY = pl.BlockSpec(memory_space=pl.ANY)


def f32(*shape):
    return pltpu.VMEM(shape, jnp.float32)


def in_vmem(x):
    return pltpu.with_memory_space_constraint(x, pltpu.VMEM)


def in_hbm(x):
    return pltpu.with_memory_space_constraint(x, pltpu.HBM)


def call(kernel, name, args, out_shape, time, out_specs=None, scratch=()):
    from_program = kernel is pack_kernel
    return pl.pallas_call(
        kernel,
        out_shape=out_shape,
        in_specs=[ANY if from_program else VMEM] * len(args),
        out_specs=out_specs or [VMEM] * len(out_shape),
        scratch_shapes=list(scratch),
        compiler_params=pltpu.CompilerParams(vmem_limit_bytes=VMEM_LIMIT),
        cost_estimate=pl.CostEstimate(flops=0, bytes_accessed=int(time * 3e6), transcendentals=0),
        name=name,
    )(*(args if from_program else map(in_vmem, args)))


def rcp(x):
    r = pl.reciprocal(x, approx=True)
    return r * (2.0 - x * r)


def lookup(table, soil):
    blocks = []
    for top in range(0, soil.shape[0], ROWS):
        parts = []
        for start in range(0, soil.shape[1], LANES):
            index = soil[top : top + ROWS, start : start + LANES]
            parts.append(jnp.take_along_axis(table, index, axis=1, mode="promise_in_bounds"))
        blocks.append(jnp.concatenate(parts, axis=1) if len(parts) > 1 else parts[0])
    return jnp.concatenate(blocks, axis=0) if len(blocks) > 1 else blocks[0]


def window_start(quarter, width, window):
    return jnp.clip(quarter * width - LANES, 0, 4 * width - window)


def pack_kernel(
    cond_ref, shape_ref, pore_ref, head_ref, old_ref, soil_ref, pond_ref, ground_ref, ponded_ref, river_ref,
    up_ref, down_ref, exfil_ref, table_ref, head_out, old_out, soil_out,
    small, pond, ground, ponded, river, sem,
):
    nz = head_ref.shape[0]
    width = pond_ref.shape[1]
    quarter = width // 4
    window = quarter + 2 * LANES
    start = pl.multiple_of(window_start(lax.axis_index("depth"), quarter, window), LANES)
    cut = pl.ds(start, window)
    pieces = 4
    piece = width // pieces
    pairs = [
        (cond_ref, small.at[0]),
        (shape_ref, small.at[1]),
        (pore_ref, small.at[2]),
        (pond_ref, pond),
        (ponded_ref, ponded),
        (ground_ref.at[:, cut], ground),
        (river_ref.at[:, cut], river),
    ]
    for part in range(pieces):
        lanes = pl.ds(part * piece, piece)
        pairs.append((soil_ref.at[:, :, lanes], soil_out.at[:, :, lanes]))
        pairs.append((head_ref.at[:, :, lanes], head_out.at[:, :, lanes]))
    pairs.append((old_ref, old_out))
    copies = [pltpu.make_async_copy(source, target, sem.at[i]) for i, (source, target) in enumerate(pairs)]
    for copy in copies:
        copy.start()
    head_out[:, :, pl.ds(width, LANES)] = jnp.zeros((nz, ROWS, LANES), jnp.float32)

    for copy in copies[:3]:
        copy.wait()
    lane = lax.broadcasted_iota(jnp.int32, (ROWS, LANES), 1)
    registers = []
    for place in range(3):
        value = jnp.ones((ROWS, LANES), jnp.float32)
        for soil_kind in range(cond_ref.shape[0]):
            value = jnp.where(lane == soil_kind, small[place, soil_kind], value)
        registers.append(value)
    cond_table, shape_table, pore_table = registers
    half_res = 0.5 / cond_table
    steep = shape_table * LOG2E
    pore_table = pore_table * (1.0 / TIME_STEP)
    for place, value in enumerate((half_res, steep, pore_table, pore_table * shape_table)):
        table_ref[place] = value

    for copy in copies[3:7]:
        copy.wait()
    tail = pl.ds(2 * nz, ROWS)
    sublane = lax.broadcasted_iota(jnp.int32, (ROWS, piece), 0)
    for part in range(pieces):
        copies[7 + 2 * part].wait()
        copies[8 + 2 * part].wait()
        lanes = pl.ds(part * piece, piece)
        soil, head = soil_out[0, :, lanes], head_out[0, :, lanes]
        conductivity = lookup(cond_table, soil) * jnp.exp2(lookup(steep, soil) * jnp.minimum(head, 0.0))
        wet_pond = ponded[:, lanes].astype(jnp.float32) * pond[:, lanes]
        exfil = -conductivity * (2.0 * (wet_pond - head) + 1.0)
        exfil_ref[:, lanes] = exfil
        up_ref[tail, lanes] = pltpu.roll(exfil, 4, 0)
        down_ref[tail, lanes] = exfil
        for target, row in ((up_ref, ROWS - 1), (down_ref, 0)):
            for top in range(0, nz, ROWS):
                head = jnp.zeros((ROWS, piece), jnp.float32)
                soil = jnp.zeros((ROWS, piece), jnp.int32)
                for z in range(ROWS):
                    head = jnp.where(sublane == z, head_out[top + z, pl.ds(row, 1), lanes], head)
                    soil = jnp.where(sublane == z, soil_out[top + z, pl.ds(row, 1), lanes], soil)
                target[pl.ds(top, ROWS), lanes] = head
                target[pl.ds(nz + top, ROWS), lanes] = lookup(half_res, soil) * jnp.exp2(
                    -lookup(steep, soil) * jnp.minimum(head, 0.0)
                )
    lower_half = lax.broadcasted_iota(jnp.int32, (ROWS, window), 0) >= 4
    conv = LAND_CONVEYANCE + (RIVER_CONVEYANCE - LAND_CONVEYANCE) * river[...].astype(jnp.float32)
    for place, field in enumerate((pond[:, cut], ground[...], conv)):
        lanes = pl.ds(place * window, window)
        up_ref[tail, lanes] = jnp.where(lower_half, field, up_ref[tail, lanes])
        down_ref[tail, lanes] = jnp.where(lower_half, pltpu.roll(field, 4, 0), down_ref[tail, lanes])
    copies[-1].wait()


def factor_kernel(
    table_ref, head_ref, old_ref, soil_ref, exfil_ref,
    sigma, base, ratio, inv, top_col, bottom_col, resist_ref,
):
    nz, _, width = base.shape
    depth = lax.axis_index("depth")
    is_top = jnp.where(depth == 0, 1.0, 0.0)
    is_bottom = jnp.where(depth == 3, 1.0, 0.0)
    is_even = lax.rem(depth, 2) == 0
    half_res, steep, porosity, porosity_steep = (table_ref[place] for place in range(4))
    sigma[:, :, pl.ds(width, LANES)] = jnp.full((nz, ROWS, LANES), CLOSED, jnp.float32)

    @pl.loop(0, width // CHUNK)
    def _(chunk):
        lanes = pl.ds(pl.multiple_of(chunk * CHUNK, CHUNK), CHUNK)

        def state(z):
            head = head_ref[z, :, lanes]
            old = old_ref[z, :, lanes]
            soil = soil_ref[z, :, lanes]
            alpha = lookup(steep, soil)
            power = alpha * jnp.minimum(head, 0.0)
            wet = jnp.exp2(power)
            wet_old = jnp.exp2(alpha * jnp.minimum(old, 0.0))
            res = lookup(half_res, soil) * jnp.exp2(-power)
            sigma[z, :, lanes] = res
            storage = lookup(porosity, soil) * (wet_old - wet) + (SPECIFIC_STORAGE / TIME_STEP) * (old - head)
            capacity = SPECIFIC_STORAGE / TIME_STEP + lookup(porosity_steep, soil) * wet
            return head, res, storage, capacity

        now = state(0)
        sigma_top = now[1]
        face_above = flux_above = ratio_above = column = None
        for z in range(nz):
            head, res, b, d = now
            if z == 0:
                b = b - exfil_ref[:, lanes] * is_top
                d = d + rcp(res) * is_top
            else:
                b = b + flux_above
                d = d + face_above * (1.0 - ratio_above)
            if z == nz - 1:
                b = b - 0.5 * rcp(res) * is_bottom
            else:
                after = state(z + 1)
                face = rcp(res + after[1])
                flux = face * (head - after[0] + 1.0)
                b = b - flux
                d = d + face
            pivot_inv = rcp(d)
            base[z, :, lanes] = b
            inv[z, :, lanes] = pivot_inv
            column = pivot_inv if z == 0 else column * pivot_inv
            if z < nz - 1:
                ratio_above = face * pivot_inv
                ratio[z, :, lanes] = ratio_above
                top_col[z, :, lanes] = column
                column = column * face
                face_above, flux_above = face, flux
                now = after
        first, last = column, pivot_inv
        top_col[nz - 1, :, lanes] = first
        bottom_col[nz - 1, :, lanes] = last
        corner = first
        r_bottom = res + last
        for z in reversed(range(nz - 1)):
            m = ratio[z, :, lanes]
            first = top_col[z, :, lanes] + m * first
            last = m * last
            top_col[z, :, lanes] = first
            bottom_col[z, :, lanes] = last
        r_top = sigma_top + first
        resist_ref[pl.ds(0, ROWS), lanes] = jnp.where(is_even, r_bottom, r_top)
        resist_ref[pl.ds(ROWS, ROWS), lanes] = jnp.where(is_even, r_top, r_bottom)
        resist_ref[pl.ds(2 * ROWS, ROWS), lanes] = corner


def lateral_kernel(
    head_ref, sigma, base_in, top_col, bottom_col, base, sums_ref, last_flux,
):
    nz, _, width = base.shape
    last_flux[...] = jnp.zeros_like(last_flux)
    sublane = lax.broadcasted_iota(jnp.int32, (ROWS, CHUNK), 0)
    inner = sublane < ROWS - 1

    @pl.loop(0, width // CHUNK)
    def _(chunk):
        start = pl.multiple_of(chunk * CHUNK, CHUNK)
        lanes = pl.ds(start, CHUNK)
        wide = pl.ds(start, CHUNK + LANES)
        top_sum = bottom_sum = None
        for z in range(nz):
            sw, hw = sigma[z, :, wide], head_ref[z, :, wide]
            s, h = sw[:, :CHUNK], hw[:, :CHUNK]
            s_right = pltpu.roll(sw, CHUNK + LANES - 1, 1)[:, :CHUNK]
            h_right = pltpu.roll(hw, CHUNK + LANES - 1, 1)[:, :CHUNK]
            flux_y = rcp(s + s_right) * (h_right - h)
            shifted = jnp.concatenate([last_flux[z], flux_y], axis=1)
            flux_left = pltpu.roll(shifted, 1, 1)[:, LANES:]
            last_flux[z] = flux_y[:, CHUNK - LANES :]
            flux_x = rcp(s + pltpu.roll(s, ROWS - 1, 0)) * (pltpu.roll(h, ROWS - 1, 0) - h)
            flux_x = jnp.where(inner, flux_x, 0.0)
            b = base_in[z, :, lanes] + (flux_y - flux_left) + (flux_x - pltpu.roll(flux_x, 1, 0))
            base[z, :, lanes] = b
            first = top_col[z, :, lanes] * b
            last = bottom_col[z, :, lanes] * b
            top_sum = first if z == 0 else top_sum + first
            bottom_sum = last if z == 0 else bottom_sum + last
        sums_ref[pl.ds(0, ROWS), lanes] = top_sum + head_ref[0, :, lanes]
        sums_ref[pl.ds(ROWS, ROWS), lanes] = bottom_sum + head_ref[nz - 1, :, lanes]


def pair_kernel(mine, other, pair_inv_ref, gain_ref, chip_res_ref):
    depth = lax.axis_index("depth")
    inner = (depth == 1) | (depth == 2)
    near, far, corner = (pl.ds(place * ROWS, ROWS) for place in range(3))
    pair_inv = rcp(mine[near, :] + other[near, :])
    inner_corner = jnp.where(inner, mine[corner, :], other[corner, :])
    gain = inner_corner * pair_inv
    pair_inv_ref[...] = pair_inv
    gain_ref[...] = gain
    chip_res_ref[...] = jnp.where(inner, mine[far, :], other[far, :]) - inner_corner * gain


def halo_kernel(
    own_up, own_down, from_above, from_below, top_col, bottom_col, sums_ref, exfil_ref,
    flux_ref, sent_ref, kept_ref,
):
    nz = top_col.shape[0]
    width = own_up.shape[1]
    quarter = width // 4
    window = quarter + 2 * LANES
    lat = lax.axis_index("lat")
    has_above = jnp.where(lat == 0, 0.0, 1.0)
    has_below = jnp.where(lat == lax.axis_size("lat") - 1, 0.0, 1.0)
    is_even = lax.rem(lax.axis_index("depth"), 2) == 0
    heads, sigmas = pl.ds(0, nz), pl.ds(nz, nz)
    sublane = lax.broadcasted_iota(jnp.int32, (ROWS, CHUNK), 0)
    for side, other, own, scale in ((0, from_below, own_up, has_below), (1, from_above, own_down, has_above)):
        flux_ref[side] = rcp(other[sigmas, :] + own[sigmas, :]) * ((other[heads, :] - own[heads, :]) * scale)

    @pl.loop(0, width // CHUNK)
    def _(chunk):
        lanes = pl.ds(pl.multiple_of(chunk * CHUNK, CHUNK), CHUNK)
        top_sum = sums_ref[pl.ds(0, ROWS), lanes]
        bottom_sum = sums_ref[pl.ds(ROWS, ROWS), lanes]
        for z in range(nz):
            added = jnp.where(sublane == 0, flux_ref[1, pl.ds(z, 1), lanes], 0.0)
            added = jnp.where(sublane == ROWS - 1, flux_ref[0, pl.ds(z, 1), lanes], added)
            top_sum = top_sum + top_col[z, :, lanes] * added
            bottom_sum = bottom_sum + bottom_col[z, :, lanes] * added
        sent_ref[pl.ds(0, ROWS), lanes] = jnp.where(is_even, bottom_sum, top_sum)
        sent_ref[pl.ds(ROWS, ROWS), lanes] = jnp.where(is_even, top_sum, bottom_sum)

    upper_half = lax.broadcasted_iota(jnp.int32, (ROWS, window), 0) < 4
    tail = pl.ds(2 * nz, ROWS)
    for place in range(4):
        lanes = pl.ds(min(max(place * quarter - LANES, 0), width - window), window)
        own = pltpu.roll(exfil_ref[:, lanes], 4, 0)
        above = from_above[tail, lanes]
        below = pltpu.roll(from_below[tail, lanes], 4, 0)
        if place % 2:
            target, into = sent_ref, pl.ds(width + (place // 2) * window, window)
        else:
            target, into = kept_ref, pl.ds((place // 2) * window, window)
        target[pl.ds(0, ROWS), into] = jnp.where(upper_half, above, own)
        target[pl.ds(ROWS, ROWS), into] = jnp.where(upper_half, own, below)


def local_kernel(flux_ref, base, ratio, inv, head_ref, out_ref):
    nz, _, width = base.shape
    sublane = lax.broadcasted_iota(jnp.int32, (ROWS, CHUNK), 0)

    @pl.loop(0, width // CHUNK)
    def _(chunk):
        lanes = pl.ds(pl.multiple_of(chunk * CHUNK, CHUNK), CHUNK)
        y = None
        for z in range(nz):
            added = jnp.where(sublane == 0, flux_ref[1, pl.ds(z, 1), lanes], 0.0)
            added = jnp.where(sublane == ROWS - 1, flux_ref[0, pl.ds(z, 1), lanes], added)
            rhs = base[z, :, lanes] + added
            y = rhs if z == 0 else rhs + ratio[z - 1, :, lanes] * y
            if z < nz - 1:
                out_ref[z, :, lanes] = y
        x = y * inv[nz - 1, :, lanes]
        out_ref[nz - 1, :, lanes] = x + head_ref[nz - 1, :, lanes]
        for z in reversed(range(nz - 1)):
            x = out_ref[z, :, lanes] * inv[z, :, lanes] + ratio[z, :, lanes] * x
            out_ref[z, :, lanes] = x + head_ref[z, :, lanes]


def ends_kernel(mine, other, kept, pair_inv_ref, gain_ref, gap_ref, chip_end_ref, exfil_ref):
    width = gap_ref.shape[1]
    window = exfil_ref.shape[1]
    depth = lax.axis_index("depth")
    inner = (depth == 1) | (depth == 2)
    sign = jnp.where(depth < 2, 1.0, -1.0)
    lanes = pl.ds(0, width)
    near, far = pl.ds(0, ROWS), pl.ds(ROWS, ROWS)
    own, others = mine[near, lanes], other[near, lanes]
    gap = sign * jnp.where(inner, others - own, own - others) + 1.0
    gap_ref[...] = gap * pair_inv_ref[...]
    chip_end_ref[...] = jnp.where(inner, mine[far, lanes], other[far, lanes]) + sign * gain_ref[...] * gap
    exfil_ref[...] = jnp.where(
        depth == 0, kept[:, pl.ds(window, window)], other[:, pl.ds(width + window, window)]
    )


def final_kernel(
    local_ref, top_col, bottom_col, gap_ref, gain_ref, res_ref, res_other, end_ref, end_other, out_ref, held, sem
):
    nz, _, width = local_ref.shape
    depth = lax.axis_index("depth")
    sign = jnp.where(depth < 2, 1.0, -1.0)

    def out_copy(chunk):
        lanes = pl.ds(pl.multiple_of(chunk * CHUNK, CHUNK), CHUNK)
        return pltpu.make_async_copy(held.at[:, :, lanes], out_ref.at[:, :, lanes], sem.at[chunk])

    @pl.loop(0, width // CHUNK)
    def _(chunk):
        lanes = pl.ds(pl.multiple_of(chunk * CHUNK, CHUNK), CHUNK)
        flow_chip = (sign * (end_ref[:, lanes] - end_other[:, lanes]) + 1.0) * rcp(
            res_ref[:, lanes] + res_other[:, lanes]
        )
        flow_core = gap_ref[:, lanes] + gain_ref[:, lanes] * flow_chip
        j_in = jnp.where(depth == 0, 0.0, jnp.where(depth == 2, flow_chip, flow_core))
        j_out = jnp.where(depth == 3, 0.0, jnp.where(depth == 1, flow_chip, flow_core))
        for z in range(nz):
            held[z, :, lanes] = (
                local_ref[z, :, lanes] + top_col[z, :, lanes] * j_in - bottom_col[z, :, lanes] * j_out
            )
        out_copy(chunk).start()

    @pl.loop(0, width // CHUNK)
    def _(chunk):
        out_copy(chunk).wait()


def shift_rows(x, by):
    return pltpu.roll(x, by % x.shape[0], 0)


def shift_lanes(x, by):
    return pltpu.roll(x, by % x.shape[1], 1)


def harmonic(first, second):
    total = first + second
    return 2.0 * first * second * rcp(jnp.where(total > 0.0, total, 1.0))


def face_k(pond, ground, conv, shift):
    pond_two, ground_two, conv_two = shift(pond), shift(ground), shift(conv)
    depth_face = 0.5 * (pond + pond_two)
    slope = pond_two + ground_two - (pond + ground)
    return (
        jnp.exp2((5.0 / 3.0 * LOG2E) * jnp.log(depth_face))
        * harmonic(conv, conv_two)
        * lax.rsqrt(jnp.abs(slope) + SLOPE_FLOOR)
    )


def surface_kernel(
    own_up, own_down, from_above, from_below, level_ref, terms_ref,
):
    window = level_ref.shape[1]
    tail = pl.ds(from_above.shape[0] - ROWS, ROWS)
    lat = lax.axis_index("lat")
    upper_half = lax.broadcasted_iota(jnp.int32, (ROWS, window), 0) < 4

    def extended(place):
        lanes = pl.ds(place * window, window)
        above = pltpu.roll(from_above[tail, lanes], 4, 0)
        first = own_down[tail, lanes]
        last = pltpu.roll(own_up[tail, lanes], 4, 0)
        below = from_below[tail, lanes]
        return jnp.concatenate(
            [jnp.where(upper_half, above, first), jnp.where(upper_half, last, below)], axis=0
        )

    pond, ground, conv = extended(0), extended(1), extended(2)
    row = lax.broadcasted_iota(jnp.int32, conv.shape, 0)
    outside = ((row < 4) & (lat == 0)) | ((row >= 12) & (lat == lax.axis_size("lat") - 1))
    conv = jnp.where(outside, 0.0, conv)
    k_down = face_k(pond, ground, conv, lambda x: shift_rows(x, -1))
    k_up = shift_rows(k_down, 1)
    k_right = face_k(pond, ground, conv, lambda x: shift_lanes(x, -1))
    lane = lax.broadcasted_iota(jnp.int32, conv.shape, 1)
    k_right = jnp.where(lane < window - 1, k_right, 0.0)
    k_left = shift_lanes(k_right, 1)
    diag = 1.0 / SURFACE_STEP + k_up + k_down + k_left + k_right
    rhs = pond * (1.0 / SURFACE_STEP)
    rhs = rhs + k_up * (shift_rows(ground, 1) - ground) + k_down * (shift_rows(ground, -1) - ground)
    rhs = rhs + k_left * (shift_lanes(ground, 1) - ground) + k_right * (shift_lanes(ground, -1) - ground)
    inv = rcp(diag)
    level_ref[...] = pond
    for place, value in enumerate((k_up * inv, k_down * inv, k_left * inv, k_right * inv, rhs * inv, inv)):
        terms_ref[place] = value


def sweep_kernel(level_ref, terms_ref, kept, from_core, from_chip, out_ref, last):
    quarter = out_ref.shape[1]
    window = level_ref.shape[1]
    depth = lax.axis_index("depth")
    k_up, k_down, k_left, k_right = (terms_ref[place] for place in range(4))
    near = from_core[:, pl.ds(from_core.shape[1] - 2 * window, window)]
    exfil = jnp.where(depth == 0, kept[:, pl.ds(0, window)], jnp.where(depth == 1, near, from_chip[...]))
    rhs = terms_ref[4] + terms_ref[5] * exfil
    level = level_ref[...]
    for _ in range(SWEEPS):
        level = (
            rhs
            + k_up * shift_rows(level, 1)
            + k_down * shift_rows(level, -1)
            + k_left * shift_lanes(level, 1)
            + k_right * shift_lanes(level, -1)
        )
    last[...] = level
    start = pl.multiple_of(
        depth * quarter - window_start(depth, quarter, quarter + 2 * LANES), LANES
    )
    cut = pl.ds(start, quarter)
    lower_half = lax.broadcasted_iota(jnp.int32, (ROWS, quarter), 0) >= 4
    upper = pltpu.roll(last[pl.ds(0, ROWS), cut], 4, 0)
    lower = pltpu.roll(last[pl.ds(ROWS, ROWS), cut], 4, 0)
    out_ref[...] = jnp.where(lower_half, lower, upper)


def per_device(
    head, head_old, soil, cond_table, shape_table, pore_table, pond, ground, ponded, river
):
    nz, rows, width = head.shape
    window = width // 4 + 2 * LANES
    lat_count = lax.axis_size("lat")
    up = [(i, (i + 1) % lat_count) for i in range(lat_count)]
    down = [(j, i) for i, j in up]
    core = [(0, 1), (1, 0), (2, 3), (3, 2)]
    chip = [(0, 2), (2, 0), (1, 3), (3, 1)]
    block = f32(nz, rows, width)
    padded = f32(nz, rows, width + LANES)
    plane = f32(rows, width)

    own_up, own_down, exfil, tables, head_v, old_v, soil_v = call(
        pack_kernel,
        "pack",
        [in_hbm(x) for x in (cond_table, shape_table, pore_table, head, head_old, soil, pond, ground, ponded, river)],
        [f32(2 * nz + rows, width)] * 2
        + [plane, f32(4, ROWS, LANES), padded, block, pltpu.VMEM((nz, rows, width), jnp.int32)],
        scratch=[
            pltpu.SMEM((3, cond_table.shape[0]), jnp.float32),
            pltpu.VMEM((rows, width), jnp.float32),
            pltpu.VMEM((rows, window), jnp.float32),
            pltpu.VMEM((rows, width), jnp.int32),
            pltpu.VMEM((rows, window), jnp.int32),
            pltpu.SemaphoreType.DMA((16,)),
        ],
        time=3,
    )
    from_above = lax.ppermute(own_up, "lat", up)
    from_below = lax.ppermute(own_down, "lat", down)

    sigma, base, ratio, inv, top_col, bottom_col, resist = call(
        factor_kernel,
        "factor",
        [tables, head_v, old_v, soil_v, exfil],
        [padded] + [block] * 5 + [f32(3 * rows, width)],
        time=8,
    )
    resist_other = lax.ppermute(resist, "depth", core)
    base, sums = call(
        lateral_kernel,
        "lateral",
        [head_v, sigma, base, top_col, bottom_col],
        [block, f32(2 * rows, width)],
        scratch=[pltpu.VMEM((nz, rows, LANES), jnp.float32)],
        time=6,
    )
    pair_inv, gain, chip_res = call(pair_kernel, "pair", [resist, resist_other], [plane] * 3, time=0.3)
    chip_res_other = lax.ppermute(chip_res, "depth", chip)

    flux, sent, kept = call(
        halo_kernel,
        "halo",
        [own_up, own_down, from_above, from_below, top_col, bottom_col, sums, exfil],
        [f32(2, nz, width), f32(2 * rows, width + 2 * window), f32(2 * rows, 2 * window)],
        time=2,
    )
    sent_other = lax.ppermute(sent, "depth", core)
    local = call(local_kernel, "local", [flux, base, ratio, inv, head_v], [block], time=1)[0]
    level, terms = call(
        surface_kernel,
        "surface",
        [own_up, own_down, from_above, from_below],
        [f32(2 * rows, window), f32(6, 2 * rows, window)],
        time=0.3,
    )
    gap, chip_end, exfil_out = call(
        ends_kernel, "ends", [sent, sent_other, kept, pair_inv, gain], [plane, plane, f32(2 * rows, window)], time=0.3
    )
    chip_end_other = lax.ppermute(chip_end, "depth", chip)
    exfil_chip = lax.ppermute(exfil_out, "depth", chip)
    head_new = call(
        final_kernel,
        "final",
        [local, top_col, bottom_col, gap, gain, chip_res, chip_res_other, chip_end, chip_end_other],
        [jax.ShapeDtypeStruct((nz, rows, width), jnp.float32)],
        out_specs=[ANY],
        scratch=[pltpu.VMEM((nz, rows, width), jnp.float32), pltpu.SemaphoreType.DMA((width // CHUNK,))],
        time=1.5,
    )[0]
    surface_new = call(
        sweep_kernel,
        "sweep",
        [level, terms, kept, sent_other, exfil_chip],
        [jax.ShapeDtypeStruct((rows, width // 4), jnp.float32)],
        scratch=[pltpu.VMEM((2 * rows, window), jnp.float32)],
        time=1,
    )[0]
    return (head_new, surface_new)


def solution(mesh):
    placed = (
        P("depth", "lat", None),
        P("depth", "lat", None),
        P("depth", "lat", None),
        P(),
        P(),
        P(),
        P("lat", None),
        P("lat", None),
        P("lat", None),
        P("lat", None),
    )
    return jax.shard_map(
        per_device,
        mesh=mesh,
        in_specs=placed,
        out_specs=(P("depth", "lat", None), P("lat", "depth")),
        check_vma=False,
    )
```

time: 75.5 us -> 45.7 us (0.61)
  local copies, waits for them, and re-layouts: 23.6 us -> 0 us
  waiting for transfers between devices: 4.08 us -> 10 us
  other arithmetic: 5.89 us -> 0 us
  Pallas kernels: 25.4 us -> 20 us
    unnamed x76 -> x0, local copies, waits for them, and re-layouts: 23.6 us -> none
    ppermute x4 -> x3, waiting for transfers between devices: 0.01 us -> 8.04 us  [the longest x1 6.18 us: per_device(): exfil_chip = lax.ppermute(exfil_out, 'depth', chip)]
    pallas_call x7 -> x10, Pallas kernels: 25.4 us -> 20 us  [call(): pl.pallas_call(kernel, out_shape=out_shape, in_specs=[ANY if from_program...]
    select_n x4 -> x0, other arithmetic: 2.83 us -> none  [the longest x1 1 us: per_device(): jnp.where(depth == 3, 0.0, jnp.where(depth == 1, flow_chip, flow_core))]
    ppermute x1, waiting for transfers between devices: 2.81 us -> 0.01 us  [per_device(): chip_end_other = lax.ppermute(chip_end, 'depth', chip)]
    ppermute x1, waiting for transfers between devices: 0.01 us -> 1.99 us  [per_device(): from_above = lax.ppermute(own_up, 'lat', up)]
    add x1 -> x0, other arithmetic: 1.3 us -> none  [per_device(): jnp.where(inner, ends[rows:], ends_other[rows:]) + sign * gain * gap]
    ppermute x1, waiting for transfers between devices: 1.26 us -> 0.01 us  [per_device(): chip_res_other = lax.ppermute(chip_res, 'depth', chip)]
  transfers between devices with their start and end apart: 8 -> 7, of which waited for: 2 -> 3; matrix products, arithmetic and copies ran while one was open for 7% -> 0% of each run, Pallas kernels for 22% -> 32%
where the time goes in v2:
time: 45.7 us; the launch traced here: 45.6 us
  Pallas kernels  20 us (44%)
  starting transfers between devices  14.8 us (32%)
  waiting for transfers between devices  10 us (22%)
  between operations  0.7 us (2%)
    pallas_call x10, Pallas kernels, call(): pl.pallas_call(kernel, out_shape=out_shape, in_specs=[ANY if from_program...  20 us
    ppermute x1, starting transfers between devices, per_device(): from_below = lax.ppermute(own_down, 'lat', down)  8.85 us
    ppermute x1, waiting for transfers between devices, per_device(): exfil_chip = lax.ppermute(exfil_out, 'depth', chip)  6.18 us
    ppermute x1, starting transfers between devices, per_device(): from_above = lax.ppermute(own_up, 'lat', up)  2.54 us
    ppermute x1, waiting for transfers between devices, per_device(): from_above = lax.ppermute(own_up, 'lat', up)  1.99 us
    ppermute x1, waiting for transfers between devices, per_device(): resist_other = lax.ppermute(resist, 'depth', core)  1.86 us
    ppermute x1, starting transfers between devices, per_device(): sent_other = lax.ppermute(sent, 'depth', core)  1.32 us
    ppermute x1, starting transfers between devices, per_device(): chip_end_other = lax.ppermute(chip_end, 'depth', chip)  1.16 us
  transfers between devices with their start and end apart: 7, of which 3 were waited for; matrix products, arithmetic and copies ran while one was open for 0% of the time, Pallas kernels for 32%

profile of v2, /device:TPU:1, one launch (start us, length us, event | category | flops | bytes accessed | tf_op | source)
XLA Modules:
  0.0 45.6 jit_solution(5130501627804784569)
XLA Ops:
  0.6 3.2 %pack.1 = (f32[40,4096]{1,0:T(8,128)S(1)}, f32[40,4096]{1,0:T(8,128)S(1)}, f32[8,4096]{1,0:T(8,128)S(1)}, f32[4,8,128]{2,1,0:T(8,128)S(1)}, f32[16,8,4224]{2,1,0...) custom-call(f32[12]{0:T(128)} %cond_ref.1, f32[12]{0:T(128)} %shape_ref.1, f32[12]{0:T(128)} %pore_ref.1, ...), custom_call_target="tpu_custom_call" | custom-call | bytes 9000000 | tf_op jit(solution)/shard_map/pack/pallas_call | solution.py:44
  3.9 2.5 %collective-permute-start = (f32[40,4096]{1,0:T(8,128)S(1)}, f32[40,4096]{1,0:T(8,128)S(1)}, u32[]{:S(2)}, u32[]{:S(2)}) collective-permute-start(f32[40,4096]{1,0:T(8,128)S(1)} %get-tuple-element.29.own_up), channel_id=1, source_target_pairs={{0,4},{4,8},{8,12},{12,16},{16,20},{20,24},{24,28},{28,32},{32,36}... | collective-permute-start | bytes 1966088 | tf_op jit(solution)/shard_map/ppermute | solution.py:518
  6.4 8.9 %collective-permute-start.1 = (f32[40,4096]{1,0:T(8,128)S(1)}, f32[40,4096]{1,0:T(8,128)S(1)}, u32[]{:S(2)}, u32[]{:S(2)}) collective-permute-start(f32[40,4096]{1,0:T(8,128)S(1)} %get-tuple-element.30.own_down), channel_id=1, source_target_pairs={{4,0},{8,4},{12,8},{16,12},{20,16},{24,20},{28,24},{32,28},{36,32}... | collective-permute-start | bytes 1966088 | tf_op jit(solution)/shard_map/ppermute | solution.py:519
  15.3 6.3 %factor.1 = (f32[16,8,4224]{2,1,0:T(8,128)S(1)}, f32[16,8,4096]{2,1,0:T(8,128)S(1)}, f32[16,8,4096]{2,1,0:T(8,128)S(1)}, f32[16,8,4096]{2,1,0:T(8,128)S(1)}, f32...) custom-call(f32[4,8,128]{2,1,0:T(8,128)S(1)} %get-tuple-element.31.table_ref, ...), custom_call_target="tpu_custom_call" | custom-call | bytes 24000000 | tf_op jit(solution)/shard_map/factor/pallas_call | solution.py:44
  21.6 6.0 %lateral.1 = (f32[16,8,4096]{2,1,0:T(8,128)S(1)}, f32[16,4096]{1,0:T(8,128)S(1)}) custom-call(f32[16,8,4224]{2,1,0:T(8,128)S(1)} %get-tuple-element.32.head_ref, f32[16,8,4224]{2,1,0:T(8,128)S(1)} %get-tuple-element.38.sigma, f32[16,8,4096]{2,1,0:T(8,128)S(1)} %get-tuple-element.39.base_in, f32[16,8,4096]{2,1,0:T(8,128)S(1)} %get-tuple-element.36.top_col, ...), custom_call_target="tpu_custom_call" | custom-call | bytes 18000000 | tf_op jit(solution)/shard_map/lateral/pallas_call | solution.py:44
  27.6 2.0 %collective-permute-done.from_above = f32[40,4096]{1,0:T(8,128)S(1)} collective-permute-done((f32[40,4096]{1,0:T(8,128)S(1)}, f32[40,4096]{1,0:T(8,128)S(1)}, u32[]{:S(2)}, u32[]{:S(2)}) %collective-permute-start) | collective-permute-done | bytes 655392 | tf_op jit(solution)/shard_map/ppermute | solution.py:518
  29.6 0.0 collective-permute-done.1.from_below
  29.6 0.8 %halo.1 = (f32[2,16,4096]{2,1,0:T(8,128)S(1)}, f32[16,6656]{1,0:T(8,128)S(1)}, f32[16,2560]{1,0:T(8,128)S(1)}) custom-call(f32[40,4096]{1,0:T(8,128)S(1)} %get-tuple-element.29.own_up, f32[40,4096]{1,0:T(8,128)S(1)} %get-tuple-element.30.own_down, f32[40,4096]{1,0:T(8,128)S(1)} %collective-permute-done.from_above, ...), custom_call_target="tpu_custom_call" | custom-call | bytes 6000000 | tf_op jit(solution)/shard_map/halo/pallas_call | solution.py:44
  30.4 1.3 %collective-permute-start.2 = (f32[16,6656]{1,0:T(8,128)S(1)}, f32[16,6656]{1,0:T(8,128)S(1)}, u32[]{:S(2)}, u32[]{:S(2)}) collective-permute-start(f32[16,6656]{1,0:T(8,128)S(1)} %get-tuple-element.45.mine), channel_id=1, source_target_pairs={{0,1},{1,0},{2,3},{3,2},{4,5},{5,4},{6,7},{7,6},{8,9},{9,8},{10,11... | collective-permute-start | bytes 1277960 | tf_op jit(solution)/shard_map/ppermute | solution.py:547
  31.7 0.1 collective-permute-start.3
  31.8 1.9 %collective-permute-done.3.other = f32[24,4096]{1,0:T(8,128)S(1)} collective-permute-done((f32[24,4096]{1,0:T(8,128)S(1)}, f32[24,4096]{1,0:T(8,128)S(1)}, u32[]{:S(2)}, u32[]{:S(2)}) %collective-permute-start.3) | collective-permute-done | bytes 393248 | tf_op jit(solution)/shard_map/ppermute | solution.py:528
  33.7 0.1 pair.1
  33.8 0.5 %collective-permute-start.4 = (f32[8,4096]{1,0:T(8,128)S(1)}, f32[8,4096]{1,0:T(8,128)S(1)}, u32[]{:S(2)}, u32[]{:S(2)}) collective-permute-start(f32[8,4096]{1,0:T(8,128)S(1)} %get-tuple-element.51.res_ref), channel_id=1, source_target_pairs={{0,2},{2,0},{1,3},{3,1},{4,6},{6,4},{5,7},{7,5},{8,10},{10,8},{9,1... | collective-permute-start | bytes 393224 | tf_op jit(solution)/shard_map/ppermute | solution.py:538
  34.2 0.0 collective-permute-done.2.other.from_core
  34.2 0.1 ends.1
  34.3 1.2 %collective-permute-start.5 = (f32[8,4096]{1,0:T(8,128)S(1)}, f32[8,4096]{1,0:T(8,128)S(1)}, u32[]{:S(2)}, u32[]{:S(2)}) collective-permute-start(f32[8,4096]{1,0:T(8,128)S(1)} %get-tuple-element.52.end_ref), channel_id=1, source_target_pairs={{0,2},{2,0},{1,3},{3,1},{4,6},{6,4},{5,7},{7,5},{8,10},{10,8},{9,1... | collective-permute-start | bytes 393224 | tf_op jit(solution)/shard_map/ppermute | solution.py:559
  35.5 0.4 collective-permute-start.6
  35.9 0.8 %local.1.local_ref = f32[16,8,4096]{2,1,0:T(8,128)S(1)} custom-call(f32[2,16,4096]{2,1,0:T(8,128)S(1)} %get-tuple-element.41.flux_ref, f32[16,8,4096]{2,1,0:T(8,128)S(1)} %get-tuple-element.42.base, f32[16,8,4096]{2,1,0:T(8,128)S(1)} %get-tuple-element.43.ratio, f32[16,8,4096]{2,1,0:T(8,128)S(1)} %get-tuple-element.44.inv, ...), custom_call_target="tpu_custom_call" | custom-call | bytes 3000000 | tf_op jit(solution)/shard_map/local/pallas_call | solution.py:44
  36.6 0.3 surface.1
  36.9 6.2 %collective-permute-done.6.from_chip = f32[16,1280]{1,0:T(8,128)S(1)} collective-permute-done((f32[16,1280]{1,0:T(8,128)S(1)}, f32[16,1280]{1,0:T(8,128)S(1)}, u32[]{:S(2)}, u32[]{:S(2)}) %collective-permute-start.6) | collective-permute-done | bytes 81952 | tf_op jit(solution)/shard_map/ppermute | solution.py:560
  43.1 1.0 %sweep.1 = f32[8,1024]{1,0:T(8,128)} custom-call(f32[16,1280]{1,0:T(8,128)S(1)} %get-tuple-element.53.level_ref, f32[6,16,1280]{2,1,0:T(8,128)S(1)} %get-tuple-element.54.terms_ref, f32[16,2560]{1,0:T(8,128)S(1)} %get-tuple-element.46.kept, f32[16,6656]{1,0:T(8,128)S(1)} %collective-permute-done.2.other.from_core, ...), custom_call_target="tpu_custom_call" | custom-call | bytes 3000000 | tf_op jit(solution)/shard_map/sweep/pallas_call | solution.py:44
  44.1 0.0 collective-permute-done.4.res_other
  44.1 0.0 collective-permute-done.5.end_other
  44.1 1.4 %final.1 = f32[16,8,4096]{2,1,0:T(8,128)} custom-call(f32[16,8,4096]{2,1,0:T(8,128)S(1)} %local.1.local_ref, f32[16,8,4096]{2,1,0:T(8,128)S(1)} %get-tuple-element.36.top_col, f32[16,8,4096]{2,1,0:T(8,128)S(1)} %get-tuple-element.37.bottom_col, f32[8,4096]{1,0:T(8,128)S(1)} %get-tuple-element.50.gap_ref, f32[8,4096]{1,0:T(8,128)S(1)} %get-tuple-element.49.gain_ref, ...), custom_call_target="tpu_custom_call" | custom-call | bytes 4500000 | tf_op jit(solution)/shard_map/final/pallas_call | solution.py:44
Async XLA Ops:
  3.9 25.8 %collective-permute-start = (f32[40,4096]{1,0:T(8,128)S(1)}, f32[40,4096]{1,0:T(8,128)S(1)}, u32[]{:S(2)}, u32[]{:S(2)}) collective-permute-start(f32[40,4096]{1,0:T(8,128)S(1)} %get-tuple-element.29.own_up), channel_id=1, source_target_pairs={{0,4},{4,8},{8,12},{12,16},{16,20},{20,24},{24,28},{28,32},{32,36}... | collective-permute-start | bytes 1966088 | tf_op jit(solution)/shard_map/ppermute | solution.py:518
  6.4 23.2 %collective-permute-start.1 = (f32[40,4096]{1,0:T(8,128)S(1)}, f32[40,4096]{1,0:T(8,128)S(1)}, u32[]{:S(2)}, u32[]{:S(2)}) collective-permute-start(f32[40,4096]{1,0:T(8,128)S(1)} %get-tuple-element.30.own_down), channel_id=1, source_target_pairs={{4,0},{8,4},{12,8},{16,12},{20,16},{24,20},{28,24},{32,28},{36,32}... | collective-permute-start | bytes 1966088 | tf_op jit(solution)/shard_map/ppermute | solution.py:519
  30.4 3.8 %collective-permute-start.2 = (f32[16,6656]{1,0:T(8,128)S(1)}, f32[16,6656]{1,0:T(8,128)S(1)}, u32[]{:S(2)}, u32[]{:S(2)}) collective-permute-start(f32[16,6656]{1,0:T(8,128)S(1)} %get-tuple-element.45.mine), channel_id=1, source_target_pairs={{0,1},{1,0},{2,3},{3,2},{4,5},{5,4},{6,7},{7,6},{8,9},{9,8},{10,11... | collective-permute-start | bytes 1277960 | tf_op jit(solution)/shard_map/ppermute | solution.py:547
  31.7 2.0 %collective-permute-start.3 = (f32[24,4096]{1,0:T(8,128)S(1)}, f32[24,4096]{1,0:T(8,128)S(1)}, u32[]{:S(2)}, u32[]{:S(2)}) collective-permute-start(f32[24,4096]{1,0:T(8,128)S(1)} %get-tuple-element.47.mine), channel_id=1, source_target_pairs={{0,1},{1,0},{2,3},{3,2},{4,5},{5,4},{6,7},{7,6},{8,9},{9,8},{10,11... | collective-permute-start | bytes 1179656 | tf_op jit(solution)/shard_map/ppermute | solution.py:528
  33.8 10.4 %collective-permute-start.4 = (f32[8,4096]{1,0:T(8,128)S(1)}, f32[8,4096]{1,0:T(8,128)S(1)}, u32[]{:S(2)}, u32[]{:S(2)}) collective-permute-start(f32[8,4096]{1,0:T(8,128)S(1)} %get-tuple-element.51.res_ref), channel_id=1, source_target_pairs={{0,2},{2,0},{1,3},{3,1},{4,6},{6,4},{5,7},{7,5},{8,10},{10,8},{9,1... | collective-permute-start | bytes 393224 | tf_op jit(solution)/shard_map/ppermute | solution.py:538
  34.3 9.8 %collective-permute-start.5 = (f32[8,4096]{1,0:T(8,128)S(1)}, f32[8,4096]{1,0:T(8,128)S(1)}, u32[]{:S(2)}, u32[]{:S(2)}) collective-permute-start(f32[8,4096]{1,0:T(8,128)S(1)} %get-tuple-element.52.end_ref), channel_id=1, source_target_pairs={{0,2},{2,0},{1,3},{3,1},{4,6},{6,4},{5,7},{7,5},{8,10},{10,8},{9,1... | collective-permute-start | bytes 393224 | tf_op jit(solution)/shard_map/ppermute | solution.py:559
  35.5 7.7 %collective-permute-start.6 = (f32[16,1280]{1,0:T(8,128)S(1)}, f32[16,1280]{1,0:T(8,128)S(1)}, u32[]{:S(2)}, u32[]{:S(2)}) collective-permute-start(f32[16,1280]{1,0:T(8,128)S(1)} %get-tuple-element.55), channel_id=1, source_target_pairs={{0,2},{2,0},{1,3},{3,1},{4,6},{6,4},{5,7},{7,5},{8,10},{10,8},{9,1... | collective-permute-start | bytes 245768 | tf_op jit(solution)/shard_map/ppermute | solution.py:560

commit v3 on v2

v3 whole, which is shorter than its diff:
```python
import jax
import jax.numpy as jnp
from jax import lax
from jax.experimental import pallas as pl
from jax.experimental.pallas import tpu as pltpu
from jax.sharding import PartitionSpec as P

SWEEPS = 4

TIME_STEP = 20.0
SURFACE_STEP = 2.0
SPECIFIC_STORAGE = 0.01
LAND_CONVEYANCE = 3.0
RIVER_CONVEYANCE = 10.0
SLOPE_FLOOR = 0.01

LOG2E = 1.4426950408889634
LN2 = 0.6931471805599453
CLOSED = 1e37

LANES = 128
ROWS = 8
CHUNK = 512
AHEAD = 3
VMEM_LIMIT = 8 * 1024 * 1024

VMEM = pl.BlockSpec(memory_space=pltpu.VMEM)
ANY = pl.BlockSpec(memory_space=pl.ANY)


def f32(*shape):
    return pltpu.VMEM(shape, jnp.float32)


def in_vmem(x):
    return (VMEM, pltpu.with_memory_space_constraint(x, pltpu.VMEM))


def in_hbm(x):
    return (ANY, pltpu.with_memory_space_constraint(x, pltpu.HBM))


FLOPS = {}


def call(kernel, name, args, out_shape, out_specs=None, scratch=()):
    return pl.pallas_call(
        kernel,
        out_shape=out_shape,
        in_specs=[spec for spec, _ in args],
        out_specs=out_specs or [VMEM] * len(out_shape),
        scratch_shapes=list(scratch),
        compiler_params=pltpu.CompilerParams(vmem_limit_bytes=VMEM_LIMIT),
        cost_estimate=pl.CostEstimate(flops=FLOPS.get(name, 1), bytes_accessed=1, transcendentals=0),
        name=name,
    )(*(x for _, x in args))


def rcp(x):
    return pl.reciprocal(x, approx=True)


def lookup(table, soil):
    numbers = lax.GatherDimensionNumbers(
        offset_dims=(),
        collapsed_slice_dims=(0,),
        start_index_map=(0,),
        operand_batching_dims=(1,),
        start_indices_batching_dims=(1,),
    )
    low, high = table
    blocks = []
    for top in range(0, soil.shape[0], ROWS):
        parts = []
        for start in range(0, soil.shape[1], LANES):
            kind = soil[top : top + ROWS, start : start + LANES]
            index = (kind & (ROWS - 1))[..., None]
            found = [
                lax.gather(half, index, numbers, (1, 1), mode=lax.GatherScatterMode.PROMISE_IN_BOUNDS)
                for half in table
            ]
            parts.append(jnp.where(kind < ROWS, *found))
        blocks.append(jnp.concatenate(parts, axis=1) if len(parts) > 1 else parts[0])
    return jnp.concatenate(blocks, axis=0) if len(blocks) > 1 else blocks[0]


def window_start(quarter, width, window):
    return jnp.clip(quarter * width - LANES, 0, 4 * width - window)


def static_window(quarter, width, window):
    return pl.ds(min(max(quarter * width - LANES, 0), 4 * width - window), window)


def pack_kernel(
    cond_ref, shape_ref, pore_ref, head_ref, soil_ref, pond_ref, ground_ref, ponded_ref, river_ref,
    up_ref, down_ref, table_ref, exfil_ref, own_ref,
    small, soils, head_top, soil_top, pond, ground, ponded, river, sem,
):
    nz, _, width = head_ref.shape
    groups = nz // ROWS
    quarter = width // 4
    window = quarter + 2 * LANES
    half = width // 2
    depth = lax.axis_index("depth")
    sides = (up_ref, down_ref)
    pairs = [(cond_ref, small.at[0]), (shape_ref, small.at[1]), (pore_ref, small.at[2])]
    for group in range(groups):
        layers = pl.ds(group * ROWS, ROWS)
        for side, (target, row) in enumerate(zip(sides, (ROWS - 1, 0))):
            pairs.append((soil_ref.at[layers, row, :], soils.at[side, group]))
            pairs.append((head_ref.at[layers, row, :], target.at[:, pl.ds(group * width, width)]))
    pairs += [
        (head_ref.at[0], head_top),
        (soil_ref.at[0], soil_top),
        (pond_ref, pond),
        (ponded_ref, ponded),
        (ground_ref, ground),
        (river_ref, river),
    ]
    copies = [pltpu.make_async_copy(source, target, sem.at[i]) for i, (source, target) in enumerate(pairs)]
    for copy in copies:
        copy.start()

    for copy in copies[:3]:
        copy.wait()
    row = lax.broadcasted_iota(jnp.int32, (ROWS, LANES), 0)
    registers = []
    for place in range(3):
        halves = []
        for top in (0, ROWS):
            value = jnp.ones((ROWS, LANES), jnp.float32)
            for soil_kind in range(top, min(top + ROWS, cond_ref.shape[0])):
                value = jnp.where(row == soil_kind - top, small[place, soil_kind], value)
            halves.append(value)
        registers.append(halves)
    cond_table, shape_table, pore_table = registers
    half_res = [0.5 / value for value in cond_table]
    steep = [value * LOG2E for value in shape_table]
    pore_table = [value * (1.0 / TIME_STEP) for value in pore_table]
    for place, halves in enumerate((half_res, steep, pore_table)):
        table_ref[2 * place] = halves[0]
        table_ref[2 * place + 1] = halves[1]

    following = iter(copies[3:])
    for group in range(groups):
        for side, target in enumerate(sides):
            next(following).wait()
            next(following).wait()
            head = target[:, pl.ds(group * width, width)]
            soil = soils[side, group]
            target[:, pl.ds((groups + group) * width, width)] = lookup(half_res, soil) * jnp.exp2(
                -lookup(steep, soil) * jnp.minimum(head, 0.0)
            )
    for copy in following:
        copy.wait()
    wet_pond = ponded[...].astype(jnp.float32) * pond[...]
    conductivity = lookup(cond_table, soil_top[...]) * jnp.exp2(
        lookup(steep, soil_top[...]) * jnp.minimum(head_top[...], 0.0)
    )
    exfil = -conductivity * (2.0 * (wet_pond - head_top[...]) + 1.0)
    exfil_ref[...] = exfil
    conv = LAND_CONVEYANCE + (RIVER_CONVEYANCE - LAND_CONVEYANCE) * river[...].astype(jnp.float32)
    field = jnp.where(
        depth < 2, jnp.where(depth == 0, exfil, pond[...]), jnp.where(depth == 2, ground[...], conv)
    )
    upper = lax.broadcasted_iota(jnp.int32, (ROWS, half), 0) < 4
    into = pl.ds(2 * groups * width, half)
    left, right = field[:, :half], field[:, half:]
    up_ref[:, into] = jnp.where(upper, pltpu.roll(left, 4, 0), right)
    down_ref[:, into] = jnp.where(upper, left, pltpu.roll(right, 4, 0))
    cut = pl.ds(pl.multiple_of(window_start(depth, quarter, window), LANES), window)
    own_ref[0] = pond[:, cut]
    own_ref[1] = ground[:, cut]
    own_ref[2] = LAND_CONVEYANCE + (RIVER_CONVEYANCE - LAND_CONVEYANCE) * river[:, cut].astype(jnp.float32)


def factor_kernel(
    table_ref, exfil_ref, head_hbm, old_hbm, soil_hbm,
    head_ref, sigma, base, ratio, inv, top_col, bottom_col, resist_ref, old_ref, soil_ref, sem,
):
    nz, _, width = base.shape
    depth = lax.axis_index("depth")
    is_top = jnp.where(depth == 0, 1.0, 0.0)
    is_bottom = jnp.where(depth == 3, 1.0, 0.0)
    is_even = lax.rem(depth, 2) == 0
    chunks = width // CHUNK
    quarter = width // 4
    window = quarter + 2 * LANES
    for place in range(2):
        resist_ref[:, pl.ds(3 * width + place * window, window)] = exfil_ref[
            :, static_window(2 * place + 1, quarter, window)
        ]

    def fetch(chunk):
        lanes = pl.ds(pl.multiple_of(chunk * CHUNK, CHUNK), CHUNK)
        return [
            pltpu.make_async_copy(source.at[:, :, lanes], target.at[:, :, lanes], sem.at[i, chunk])
            for i, (source, target) in enumerate(((head_hbm, head_ref), (soil_hbm, soil_ref), (old_hbm, old_ref)))
        ]

    for chunk in range(AHEAD):
        for copy in fetch(chunk):
            copy.start()
    half_res, steep, porosity = ((table_ref[2 * place], table_ref[2 * place + 1]) for place in range(3))
    sigma[:, :, pl.ds(width, LANES)] = jnp.full((nz, ROWS, LANES), CLOSED, jnp.float32)
    head_ref[:, :, pl.ds(width, LANES)] = jnp.zeros((nz, ROWS, LANES), jnp.float32)

    @pl.loop(0, chunks)
    def _(chunk):
        lanes = pl.ds(pl.multiple_of(chunk * CHUNK, CHUNK), CHUNK)
        for copy in fetch(chunk):
            copy.wait()

        @pl.when(chunk + AHEAD < chunks)
        def _():
            for copy in fetch(chunk + AHEAD):
                copy.start()

        def state(z):
            head = head_ref[z, :, lanes]
            old = old_ref[z, :, lanes]
            soil = soil_ref[z, :, lanes]
            alpha = lookup(steep, soil)
            power = alpha * jnp.minimum(head, 0.0)
            wet = jnp.exp2(power)
            wet_old = jnp.exp2(alpha * jnp.minimum(old, 0.0))
            res = lookup(half_res, soil) * rcp(wet)
            sigma[z, :, lanes] = res
            pore = lookup(porosity, soil)
            pore_wet = pore * wet
            storage = pore * wet_old - pore_wet + (SPECIFIC_STORAGE / TIME_STEP) * (old - head)
            capacity = SPECIFIC_STORAGE / TIME_STEP + (alpha * LN2) * pore_wet
            return head, res, storage, capacity

        now = state(0)
        sigma_top = now[1]
        face_above = flux_above = ratio_above = column = None
        for z in range(nz):
            head, res, b, d = now
            if z == 0:
                b = b - exfil_ref[:, lanes] * is_top
                d = d + rcp(res) * is_top
            else:
                b = b + flux_above
                d = d + face_above * (1.0 - ratio_above)
            if z == nz - 1:
                b = b - 0.5 * rcp(res) * is_bottom
            else:
                after = state(z + 1)
                face = rcp(res + after[1])
                flux = face * (head - after[0] + 1.0)
                b = b - flux
                d = d + face
            pivot_inv = rcp(d)
            base[z, :, lanes] = b
            inv[z, :, lanes] = pivot_inv
            column = pivot_inv if z == 0 else column * pivot_inv
            if z < nz - 1:
                ratio_above = face * pivot_inv
                ratio[z, :, lanes] = ratio_above
                top_col[z, :, lanes] = column
                column = column * face
                face_above, flux_above = face, flux
                now = after
        first, last = column, pivot_inv
        top_col[nz - 1, :, lanes] = first
        bottom_col[nz - 1, :, lanes] = last
        corner = first
        r_bottom = res + last
        for z in reversed(range(nz - 1)):
            m = ratio[z, :, lanes]
            first = top_col[z, :, lanes] + m * first
            last = m * last
            top_col[z, :, lanes] = first
            bottom_col[z, :, lanes] = last
        r_top = sigma_top + first
        resist_ref[:, lanes] = jnp.where(is_even, r_bottom, r_top)
        resist_ref[:, pl.ds(pl.multiple_of(width + chunk * CHUNK, CHUNK), CHUNK)] = jnp.where(is_even, r_top, r_bottom)
        resist_ref[:, pl.ds(pl.multiple_of(2 * width + chunk * CHUNK, CHUNK), CHUNK)] = corner


def lateral_kernel(
    head_ref, sigma, base_in, top_col, bottom_col, base, sums_ref, carried,
):
    nz, _, width = base.shape
    sublane = lax.broadcasted_iota(jnp.int32, (ROWS, CHUNK), 0)
    inner = sublane < ROWS - 1
    lane = lax.broadcasted_iota(jnp.int32, (ROWS, LANES), 1)
    is_first, is_last = lane == 0, lane == LANES - 1
    count = CHUNK // LANES

    def left(x):
        return pltpu.roll(x, LANES - 1, 1)

    def registers(x):
        return [x[:, k * LANES : (k + 1) * LANES] for k in range(x.shape[1] // LANES)]

    for z in range(nz):
        carried[0, z] = left(sigma[z, :, pl.ds(0, LANES)])
        carried[1, z] = left(head_ref[z, :, pl.ds(0, LANES)])
        carried[2, z] = jnp.zeros((ROWS, LANES), jnp.float32)

    @pl.loop(0, width // CHUNK)
    def _(chunk):
        start = pl.multiple_of(chunk * CHUNK, CHUNK)
        lanes = pl.ds(start, CHUNK)
        after = pl.ds(pl.multiple_of(start + LANES, LANES), CHUNK)
        top_sum = bottom_sum = None
        for z in range(nz):
            s, h = sigma[z, :, lanes], head_ref[z, :, lanes]
            moved = []
            for place, array in ((0, sigma), (1, head_ref)):
                found = [carried[place, z]] + [left(x) for x in registers(array[z, :, after])]
                carried[place, z] = found[count]
                moved.append(
                    jnp.concatenate(
                        [jnp.where(is_last, found[k + 1], found[k]) for k in range(count)], axis=1
                    )
                )
            s_right, h_right = moved
            flux_y = rcp(s + s_right) * (h_right - h)
            found = [carried[2, z]] + [pltpu.roll(x, 1, 1) for x in registers(flux_y)]
            carried[2, z] = found[count]
            flux_left = jnp.concatenate(
                [jnp.where(is_first, found[k], found[k + 1]) for k in range(count)], axis=1
            )
            flux_x = rcp(s + pltpu.roll(s, ROWS - 1, 0)) * (pltpu.roll(h, ROWS - 1, 0) - h)
            flux_x = jnp.where(inner, flux_x, 0.0)
            b = base_in[z, :, lanes] + (flux_y - flux_left) + (flux_x - pltpu.roll(flux_x, 1, 0))
            base[z, :, lanes] = b
            first = top_col[z, :, lanes] * b
            last = bottom_col[z, :, lanes] * b
            top_sum = first if z == 0 else top_sum + first
            bottom_sum = last if z == 0 else bottom_sum + last
        sums_ref[pl.ds(0, ROWS), lanes] = top_sum + head_ref[0, :, lanes]
        sums_ref[pl.ds(ROWS, ROWS), lanes] = bottom_sum + head_ref[nz - 1, :, lanes]


def pair_kernel(mine, other, exfil_ref, _, pair_inv_ref, gain_ref, sent_ref):
    width = gain_ref.shape[1]
    window = sent_ref.shape[1] - width
    depth = lax.axis_index("depth")
    inner = (depth == 1) | (depth == 2)
    near, far, corner = (pl.ds(place * width, width) for place in range(3))
    pair_inv = rcp(mine[:, near] + other[:, near])
    inner_corner = jnp.where(inner, mine[:, corner], other[:, corner])
    gain = inner_corner * pair_inv
    pair_inv_ref[...] = pair_inv
    gain_ref[...] = gain
    sent_ref[:, pl.ds(0, width)] = jnp.where(inner, mine[:, far], other[:, far]) - inner_corner * gain
    sent_ref[:, pl.ds(width, window)] = jnp.where(
        depth == 0, exfil_ref[:, static_window(2, width // 4, window)], other[:, pl.ds(3 * width + window, window)]
    )


def halo_kernel(
    own_up, own_down, from_above, from_below, top_col, bottom_col, sums_ref, _, flux_ref, sent_ref, rows_ref, windows_ref,
):
    nz, _, width = top_col.shape
    lat = lax.axis_index("lat")
    has_above = jnp.where(lat == 0, 0.0, 1.0)
    has_below = jnp.where(lat == lax.axis_size("lat") - 1, 0.0, 1.0)
    is_even = lax.rem(lax.axis_index("depth"), 2) == 0
    sublane = lax.broadcasted_iota(jnp.int32, (ROWS, CHUNK), 0)
    for side, other, own, scale in ((0, from_below, own_up, has_below), (1, from_above, own_down, has_above)):
        for group in range(nz // ROWS):
            heads = pl.ds(group * width, width)
            sigmas = pl.ds((nz // ROWS + group) * width, width)
            flux_ref[side, pl.ds(group * ROWS, ROWS), :] = rcp(other[:, sigmas] + own[:, sigmas]) * (
                (other[:, heads] - own[:, heads]) * scale
            )

    @pl.loop(0, width // CHUNK)
    def _(chunk):
        lanes = pl.ds(pl.multiple_of(chunk * CHUNK, CHUNK), CHUNK)
        top_sum = sums_ref[pl.ds(0, ROWS), lanes]
        bottom_sum = sums_ref[pl.ds(ROWS, ROWS), lanes]
        for z in range(nz):
            row = pl.ds(z, 1)
            added = jnp.where(sublane == 0, flux_ref[1, row, lanes], 0.0)
            added = jnp.where(sublane == ROWS - 1, flux_ref[0, row, lanes], added)
            top_sum = top_sum + top_col[z, :, lanes] * added
            bottom_sum = bottom_sum + bottom_col[z, :, lanes] * added
        sent_ref[pl.ds(0, ROWS), lanes] = jnp.where(is_even, bottom_sum, top_sum)
        sent_ref[pl.ds(ROWS, ROWS), lanes] = jnp.where(is_even, top_sum, bottom_sum)

    half = width // 2
    extra = pl.ds(own_up.shape[1] - half, half)
    upper = lax.broadcasted_iota(jnp.int32, (ROWS, half), 0) < 4
    above, below = from_above[:, extra], from_below[:, extra]
    rows_ref[:, pl.ds(0, half)] = jnp.where(upper, above, pltpu.roll(below, 4, 0))
    rows_ref[:, pl.ds(half, half)] = jnp.where(upper, pltpu.roll(above, 4, 0), below)
    quarter = width // 4
    window = windows_ref.shape[1] // 2
    depth = lax.axis_index("depth")
    for place, quarters in enumerate((depth ^ 1, depth ^ 3)):
        cut = pl.ds(pl.multiple_of(window_start(quarters, quarter, window), LANES), window)
        windows_ref[:, pl.ds(place * window, window)] = rows_ref[:, cut]


def local_kernel(flux_ref, base, ratio, inv, head_ref, out_ref):
    nz, _, width = base.shape
    sublane = lax.broadcasted_iota(jnp.int32, (ROWS, CHUNK), 0)

    @pl.loop(0, width // CHUNK)
    def _(chunk):
        lanes = pl.ds(pl.multiple_of(chunk * CHUNK, CHUNK), CHUNK)
        y = None
        for z in range(nz):
            row = pl.ds(z, 1)
            added = jnp.where(sublane == 0, flux_ref[1, row, lanes], 0.0)
            added = jnp.where(sublane == ROWS - 1, flux_ref[0, row, lanes], added)
            rhs = base[z, :, lanes] + added
            y = rhs if z == 0 else rhs + ratio[z - 1, :, lanes] * y
            if z < nz - 1:
                out_ref[z, :, lanes] = y
        x = y * inv[nz - 1, :, lanes]
        out_ref[nz - 1, :, lanes] = x + head_ref[nz - 1, :, lanes]
        for z in reversed(range(nz - 1)):
            x = out_ref[z, :, lanes] * inv[z, :, lanes] + ratio[z, :, lanes] * x
            out_ref[z, :, lanes] = x + head_ref[z, :, lanes]


def ends_kernel(mine, other, pair_inv_ref, gain_ref, gap_ref, chip_end_ref):
    depth = lax.axis_index("depth")
    inner = (depth == 1) | (depth == 2)
    sign = jnp.where(depth < 2, 1.0, -1.0)
    near, far = pl.ds(0, ROWS), pl.ds(ROWS, ROWS)
    own, others = mine[near, :], other[near, :]
    gap = sign * jnp.where(inner, others - own, own - others) + 1.0
    gap_ref[...] = gap * pair_inv_ref[...]
    chip_end_ref[...] = jnp.where(inner, mine[far, :], other[far, :]) + sign * gain_ref[...] * gap


def final_kernel(
    local_ref, top_col, bottom_col, gap_ref, gain_ref, res_ref, res_other, end_ref, end_other,
    out_ref, token_ref, held, sem,
):
    nz, _, width = local_ref.shape
    depth = lax.axis_index("depth")
    sign = jnp.where(depth < 2, 1.0, -1.0)

    token_ref[...] = jnp.zeros_like(token_ref)

    def out_copy(chunk):
        lanes = pl.ds(pl.multiple_of(chunk * CHUNK, CHUNK), CHUNK)
        return pltpu.make_async_copy(held.at[:, :, lanes], out_ref.at[:, :, lanes], sem.at[chunk])

    @pl.loop(0, width // CHUNK)
    def _(chunk):
        lanes = pl.ds(pl.multiple_of(chunk * CHUNK, CHUNK), CHUNK)
        flow_chip = (sign * (end_ref[:, lanes] - end_other[:, lanes]) + 1.0) * rcp(
            res_ref[:, lanes] + res_other[:, lanes]
        )
        flow_core = gap_ref[:, lanes] + gain_ref[:, lanes] * flow_chip
        j_in = jnp.where(depth == 0, 0.0, jnp.where(depth == 2, flow_chip, flow_core))
        j_out = jnp.where(depth == 3, 0.0, jnp.where(depth == 1, flow_chip, flow_core))
        for z in range(nz):
            held[z, :, lanes] = (
                local_ref[z, :, lanes] + top_col[z, :, lanes] * j_in - bottom_col[z, :, lanes] * j_out
            )
        out_copy(chunk).start()

    @pl.loop(0, width // CHUNK)
    def _(chunk):
        out_copy(chunk).wait()


def shift_rows(x, by):
    return pltpu.roll(x, by % x.shape[0], 0)


def shift_lanes(x, by):
    return pltpu.roll(x, by % x.shape[1], 1)


def harmonic(first, second):
    total = first + second
    return 2.0 * first * second * rcp(jnp.where(total > 0.0, total, 1.0))


def face_k(pond, ground, conv, shift):
    pond_two, ground_two, conv_two = shift(pond), shift(ground), shift(conv)
    depth_face = 0.5 * (pond + pond_two)
    slope = pond_two + ground_two - (pond + ground)
    return (
        jnp.exp2((5.0 / 3.0 * LOG2E) * jnp.log(depth_face))
        * harmonic(conv, conv_two)
        * lax.rsqrt(jnp.abs(slope) + SLOPE_FLOOR)
    )


def relay_kernel(rows_ref, from_core, _, sent_ref):
    window = sent_ref.shape[1] // 2
    depth = lax.axis_index("depth")
    is_even = lax.rem(depth, 2) == 0
    cut = pl.ds(pl.multiple_of(window_start(depth ^ 2, rows_ref.shape[1] // 4, window), LANES), window)
    own, other = rows_ref[:, cut], from_core[:, pl.ds(window, window)]
    sent_ref[:, pl.ds(0, window)] = jnp.where(is_even, own, other)
    sent_ref[:, pl.ds(window, window)] = jnp.where(is_even, other, own)


def surface_kernel(
    own_ref, exfil_ref, pair_core, pair_chip, rows_ref, from_core, from_chip, _, out_ref, last,
):
    window = last.shape[1]
    width = exfil_ref.shape[1]
    quarter = width // 4
    lat = lax.axis_index("lat")
    depth = lax.axis_index("depth")
    is_even = lax.rem(depth, 2) == 0
    upper = lax.broadcasted_iota(jnp.int32, (ROWS, window), 0) < 4
    first, second = pl.ds(0, window), pl.ds(window, window)

    cut = pl.ds(pl.multiple_of(window_start(depth, quarter, window), LANES), window)
    mine, other = rows_ref[:, cut], from_core[:, first]
    here = (jnp.where(is_even, mine, other), jnp.where(is_even, other, mine))
    there = (from_chip[:, first], from_chip[:, second])
    outer = [jnp.where(depth < 2, a, b) for a, b in zip(here + there, there + here)]
    near = jnp.where(depth == 0, exfil_ref[:, first], pair_core[:, pl.ds(3 * width, window)])
    near = jnp.where(depth < 2, near, pair_chip[:, pl.ds(width, window)])

    def extended(rows, own):
        own = pltpu.roll(own, 4, 0)
        return jnp.concatenate([jnp.where(upper, rows, own), jnp.where(upper, own, rows)], axis=0)

    exfil, pond, ground, conv = (
        extended(rows, own) for rows, own in zip(outer, (near, own_ref[0], own_ref[1], own_ref[2]))
    )
    row = lax.broadcasted_iota(jnp.int32, conv.shape, 0)
    outside = ((row < 4) & (lat == 0)) | ((row >= 12) & (lat == lax.axis_size("lat") - 1))
    conv = jnp.where(outside, 0.0, conv)
    k_down = face_k(pond, ground, conv, lambda x: shift_rows(x, -1))
    k_up = shift_rows(k_down, 1)
    k_right = face_k(pond, ground, conv, lambda x: shift_lanes(x, -1))
    lane = lax.broadcasted_iota(jnp.int32, conv.shape, 1)
    k_right = jnp.where(lane < window - 1, k_right, 0.0)
    k_left = shift_lanes(k_right, 1)
    diag = 1.0 / SURFACE_STEP + k_up + k_down + k_left + k_right
    rhs = pond * (1.0 / SURFACE_STEP)
    rhs = rhs + k_up * (shift_rows(ground, 1) - ground) + k_down * (shift_rows(ground, -1) - ground)
    rhs = rhs + k_left * (shift_lanes(ground, 1) - ground) + k_right * (shift_lanes(ground, -1) - ground)
    inv = rcp(diag)
    k_up, k_down, k_left, k_right = k_up * inv, k_down * inv, k_left * inv, k_right * inv
    rhs = (rhs + exfil) * inv
    level = pond
    for _ in range(SWEEPS):
        level = (
            rhs
            + k_up * shift_rows(level, 1)
            + k_down * shift_rows(level, -1)
            + k_left * shift_lanes(level, 1)
            + k_right * shift_lanes(level, -1)
        )
    last[...] = level
    start = pl.multiple_of(
        depth * quarter - window_start(depth, quarter, window), LANES
    )
    cut = pl.ds(start, quarter)
    lower_half = lax.broadcasted_iota(jnp.int32, (ROWS, quarter), 0) >= 4
    upper = pltpu.roll(last[pl.ds(0, ROWS), cut], 4, 0)
    lower = pltpu.roll(last[pl.ds(ROWS, ROWS), cut], 4, 0)
    out_ref[...] = jnp.where(lower_half, lower, upper)


def per_device(
    head, head_old, soil, cond_table, shape_table, pore_table, pond, ground, ponded, river
):
    nz, rows, width = head.shape
    window = width // 4 + 2 * LANES
    lat_count = lax.axis_size("lat")
    up, down = [], []
    for i in range(lat_count):
        for j in range(4):
            after, place = (i + 1, j) if i < lat_count - 1 else (0, j ^ 2)
            up.append((4 * i + j, 4 * after + place))
            down.append((4 * after + place, 4 * i + j))
    core = [(0, 1), (1, 0), (2, 3), (3, 2)]
    chip = [(0, 2), (2, 0), (1, 3), (3, 1)]
    block = f32(nz, rows, width)
    padded = f32(nz, rows, width + LANES)
    plane = f32(rows, width)

    side = f32(rows, 2 * (nz // ROWS) * width + width // 2)

    own_up, own_down, tables, exfil, own_fields = call(
        pack_kernel,
        "pack",
        [in_hbm(x) for x in (cond_table, shape_table, pore_table, head, soil, pond, ground, ponded, river)],
        [side, side, f32(6, ROWS, LANES), plane, f32(3, rows, window)],
        scratch=[
            pltpu.SMEM((3, cond_table.shape[0]), jnp.float32),
            pltpu.VMEM((2, nz // ROWS, ROWS, width), jnp.int32),
            pltpu.VMEM((rows, width), jnp.float32),
            pltpu.VMEM((rows, width), jnp.int32),
            pltpu.VMEM((rows, width), jnp.float32),
            pltpu.VMEM((rows, width), jnp.float32),
            pltpu.VMEM((rows, width), jnp.int32),
            pltpu.VMEM((rows, width), jnp.int32),
            pltpu.SemaphoreType.DMA((9 + 4 * (nz // ROWS),)),
        ],
    )
    from_above = lax.ppermute(own_up, ("lat", "depth"), up)
    from_below = lax.ppermute(own_down, ("lat", "depth"), down)

    head_v, sigma, base, ratio, inv, top_col, bottom_col, resist = call(
        factor_kernel,
        "factor",
        [in_vmem(tables), in_vmem(exfil)] + [in_hbm(x) for x in (head, head_old, soil)],
        [padded, padded] + [block] * 5 + [f32(rows, 3 * width + 2 * window)],
        scratch=[
            pltpu.VMEM((nz, rows, width), jnp.float32),
            pltpu.VMEM((nz, rows, width), jnp.int32),
            pltpu.SemaphoreType.DMA((3, width // CHUNK)),
        ],
    )
    resist_other = lax.ppermute(resist, "depth", core)
    base, sums = call(
        lateral_kernel,
        "lateral",
        [in_vmem(x) for x in (head_v, sigma, base, top_col, bottom_col)],
        [block, f32(2 * rows, width)],
        scratch=[pltpu.VMEM((3, nz, rows, LANES), jnp.float32)],
    )
    pair_inv, gain, chip_sent = call(
        pair_kernel,
        "pair",
        [in_vmem(x) for x in (resist, resist_other, exfil, sums)],
        [plane, plane, f32(rows, width + window)],
    )
    chip_other = lax.ppermute(chip_sent, "depth", chip)

    flux, ends, field_rows, windows = call(
        halo_kernel,
        "halo",
        [in_vmem(x) for x in (own_up, own_down, from_above, from_below, top_col, bottom_col, sums, gain)],
        [f32(2, nz, width), f32(2 * rows, width), plane, f32(rows, 2 * window)],
    )
    ends_other = lax.ppermute(ends, "depth", core)
    windows_core = lax.ppermute(windows, "depth", core)
    local = call(
        local_kernel, "local", [in_vmem(x) for x in (flux, base, ratio, inv, head_v)], [block]
    )[0]
    gap, chip_end = call(
        ends_kernel, "ends", [in_vmem(x) for x in (ends, ends_other, pair_inv, gain)], [plane, plane]
    )
    chip_end_other = lax.ppermute(chip_end, "depth", chip)
    relayed = call(
        relay_kernel,
        "relay",
        [in_vmem(x) for x in (field_rows, windows_core, chip_end)],
        [f32(rows, 2 * window)],
    )[0]
    windows_chip = lax.ppermute(relayed, "depth", chip)
    head_new, token = call(
        final_kernel,
        "final",
        [
            in_vmem(x)
            for x in (local, top_col, bottom_col, gap, gain, chip_sent, chip_other, chip_end, chip_end_other)
        ],
        [jax.ShapeDtypeStruct((nz, rows, width), jnp.float32), f32(ROWS, LANES)],
        out_specs=[ANY, VMEM],
        scratch=[pltpu.VMEM((nz, rows, width), jnp.float32), pltpu.SemaphoreType.DMA((width // CHUNK,))],
    )
    surface_new = call(
        surface_kernel,
        "surface",
        [
            in_vmem(x)
            for x in (own_fields, exfil, resist_other, chip_other, field_rows, windows_core, windows_chip, token)
        ],
        [jax.ShapeDtypeStruct((rows, width // 4), jnp.float32)],
        scratch=[pltpu.VMEM((2 * rows, window), jnp.float32)],
    )[0]
    return (head_new, surface_new)


def solution(mesh):
    placed = (
        P("depth", "lat", None),
        P("depth", "lat", None),
        P("depth", "lat", None),
        P(),
        P(),
        P(),
        P("lat", None),
        P("lat", None),
        P("lat", None),
        P("lat", None),
    )
    return jax.shard_map(
        per_device,
        mesh=mesh,
        in_specs=placed,
        out_specs=(P("depth", "lat", None), P("lat", "depth")),
        check_vma=False,
    )
```

time: 45.7 us -> 40.7 us (0.89)
  Pallas kernels: 20 us -> 16 us
  waiting for transfers between devices: 10 us -> 8.47 us
  starting transfers between devices: 14.8 us -> 15.4 us
    pallas_call x10, Pallas kernels: 20 us -> 16 us  [call(): pl.pallas_call(kernel, out_shape=out_shape, in_specs=[spec for spec, _ in...]
    ppermute x1, waiting for transfers between devices: 0.01 us -> 2.81 us  [per_device(): chip_end_other = lax.ppermute(chip_end, 'depth', chip)]
    ppermute x5 -> x6, waiting for transfers between devices: 8.18 us -> 5.66 us  [the longest x1 2.24 us: per_device(): from_above = lax.ppermute(own_up, ('lat', 'depth'), up)]
    ppermute x1, waiting for transfers between devices: 1.86 us -> 0.01 us  [per_device(): resist_other = lax.ppermute(resist, 'depth', core)]
    ppermute x1, starting transfers between devices: 0.1 us -> 1.04 us  [per_device(): resist_other = lax.ppermute(resist, 'depth', core)]
    ppermute x5 -> x6, starting transfers between devices: 13.6 us -> 13.6 us  [the longest x1 8.67 us: per_device(): from_below = lax.ppermute(own_down, ('lat', 'depth'), down)]
  transfers between devices with their start and end apart: 7 -> 8, of which waited for: 3 -> 5; matrix products, arithmetic and copies ran while one was open for 0% -> 0% of each run, Pallas kernels for 32% -> 30%
where the time goes in v3:
time: 40.7 us; the launch traced here: 40.6 us
  Pallas kernels  16 us (39%)
  starting transfers between devices  15.4 us (38%)
  waiting for transfers between devices  8.47 us (21%)
  between operations  0.7 us (2%)
    pallas_call x10, Pallas kernels, call(): pl.pallas_call(kernel, out_shape=out_shape, in_specs=[spec for spec, _ in...  16 us
    ppermute x1, starting transfers between devices, per_device(): from_below = lax.ppermute(own_down, ('lat', 'depth'), down)  8.67 us
    ppermute x1, waiting for transfers between devices, per_device(): chip_end_other = lax.ppermute(chip_end, 'depth', chip)  2.81 us
    ppermute x1, starting transfers between devices, per_device(): from_above = lax.ppermute(own_up, ('lat', 'depth'), up)  2.54 us
    ppermute x1, waiting for transfers between devices, per_device(): from_above = lax.ppermute(own_up, ('lat', 'depth'), up)  2.24 us
    ppermute x1, waiting for transfers between devices, per_device(): chip_other = lax.ppermute(chip_sent, 'depth', chip)  2.18 us
    ppermute x1, starting transfers between devices, per_device(): ends_other = lax.ppermute(ends, 'depth', core)  1.32 us
    ppermute x1, starting transfers between devices, per_device(): resist_other = lax.ppermute(resist, 'depth', core)  1.04 us
  transfers between devices with their start and end apart: 8, of which 5 were waited for; matrix products, arithmetic and copies ran while one was open for 0% of the time, Pallas kernels for 30%

profile of v3, /device:TPU:1, one launch (start us, length us, event | category | flops | bytes accessed | tf_op | source)
XLA Modules:
  0.0 40.6 jit_solution(16399365226670104389)
XLA Ops:
  0.6 1.9 %pack.1 = (f32[8,18432]{1,0:T(8,128)S(1)}, f32[8,18432]{1,0:T(8,128)S(1)}, f32[6,8,128]{2,1,0:T(8,128)S(1)}, f32[8,4096]{1,0:T(8,128)S(1)}, f32[3,8,1280]{2,1,0:T(8,128)S(1)}) custom-call(f32[12]{0:T(128)} %cond_ref.1, f32[12]{0:T(128)} %shape_ref.1, f32[12]{0:T(128)} %pore_ref.1, f32[16,8,4096]{2,1,0:T(8,128)} %head_hbm.1, s32[16,8,4096]{2,1,0:T(8,128)} %soil_hbm.1, ...), custom_call_target="tpu_custom_call" | custom-call | flops 1 | bytes 1 | tf_op jit(solution)/shard_map/pack/pallas_call | solution.py:47
  2.6 2.5 %collective-permute-start = (f32[8,18432]{1,0:T(8,128)S(1)}, f32[8,18432]{1,0:T(8,128)S(1)}, u32[]{:S(2)}, u32[]{:S(2)}) collective-permute-start(f32[8,18432]{1,0:T(8,128)S(1)} %get-tuple-element.28.own_up), channel_id=1, source_target_pairs={{0,4},{1,5},{2,6},{3,7},{4,8},{5,9},{6,10},{7,11},{8,12},{9,13},{1... | collective-permute-start | bytes 1769480 | tf_op jit(solution)/shard_map/ppermute | solution.py:604
  5.1 8.7 %collective-permute-start.1 = (f32[8,18432]{1,0:T(8,128)S(1)}, f32[8,18432]{1,0:T(8,128)S(1)}, u32[]{:S(2)}, u32[]{:S(2)}) collective-permute-start(f32[8,18432]{1,0:T(8,128)S(1)} %get-tuple-element.29.own_down), channel_id=1, source_target_pairs={{4,0},{5,1},{6,2},{7,3},{8,4},{9,5},{10,6},{11,7},{12,8},{13,9},{1... | collective-permute-start | bytes 1769480 | tf_op jit(solution)/shard_map/ppermute | solution.py:605
  13.8 4.9 %factor.1 = (f32[16,8,4224]{2,1,0:T(8,128)S(1)}, f32[16,8,4224]{2,1,0:T(8,128)S(1)}, f32[16,8,4096]{2,1,0:T(8,128)S(1)}, f32[16,8,4096]{2,1,0:T(8,128)S(1)}, f32...) custom-call(f32[6,8,128]{2,1,0:T(8,128)S(1)} %get-tuple-element.30.ta, ...), custom_call_target="tpu_custom_call" | custom-call | flops 1 | bytes 1 | tf_op jit(solution)/shard_map/factor/pallas_call | solution.py:47
  18.7 1.0 %collective-permute-start.2 = (f32[8,14848]{1,0:T(8,128)S(1)}, f32[8,14848]{1,0:T(8,128)S(1)}, u32[]{:S(2)}, u32[]{:S(2)}) collective-permute-start(f32[8,14848]{1,0:T(8,128)S(1)} %get-tuple-element.38.mine), channel_id=1, source_target_pairs={{0,1},{1,0},{2,3},{3,2},{4,5},{5,4},{6,7},{7,6},{8,9},{9,8},{10,11... | collective-permute-start | bytes 1425416 | tf_op jit(solution)/shard_map/ppermute | solution.py:618
  19.8 4.7 %lateral.1 = (f32[16,8,4096]{2,1,0:T(8,128)S(1)}, f32[16,4096]{1,0:T(8,128)S(1)}) custom-call(f32[16,8,4224]{2,1,0:T(8,128)S(1)} %get-tuple-element.34.head_ref, f32[16,8,4224]{2,1,0:T(8,128)S(1)} %get-tuple-element.35.sigma, f32[16,8,4096]{2,1,0:T(8,128)S(1)} %get-tuple-element.36.base_in, f32[16,8,4096]{2,1,0:T(8,128)S(1)} %get-tuple-element.32.top_col, ...), custom_call_target="tpu_custom_call" | custom-call | flops 1 | bytes 1 | tf_op jit(solution)/shard_map/lateral/pallas_call | solution.py:47
  24.5 0.0 collective-permute-done.2.other.pair_core
  24.5 0.1 pair.1
  24.5 2.2 %collective-permute-done.from_above = f32[8,18432]{1,0:T(8,128)S(1)} collective-permute-done((f32[8,18432]{1,0:T(8,128)S(1)}, f32[8,18432]{1,0:T(8,128)S(1)}, u32[]{:S(2)}, u32[]{:S(2)}) %collective-permute-start) | collective-permute-done | bytes 589856 | tf_op jit(solution)/shard_map/ppermute | solution.py:604
  26.8 0.0 collective-permute-done.1.from_below
  26.8 0.8 %halo.1 = (f32[2,16,4096]{2,1,0:T(8,128)S(1)}, f32[16,4096]{1,0:T(8,128)S(1)}, f32[8,4096]{1,0:T(8,128)S(1)}, f32[8,2560]{1,0:T(8,128)S(1)}) custom-call(f32[8,18432]{1,0:T(8,128)S(1)} %get-tuple-element.28.own_up, f32[8,18432]{1,0:T(8,128)S(1)} %get-tuple-element.29.own_down, f32[8,18432]{1,0:T(8,128)S(1)} %collective-permute-done.from_above, ...), custom_call_target="tpu_custom_call" | custom-call | flops 1 | bytes 1 | tf_op jit(solution)/shard_map/halo/pallas_call | solution.py:47
  27.5 1.3 %collective-permute-start.3 = (f32[16,4096]{1,0:T(8,128)S(1)}, f32[16,4096]{1,0:T(8,128)S(1)}, u32[]{:S(2)}, u32[]{:S(2)}) collective-permute-start(f32[16,4096]{1,0:T(8,128)S(1)} %get-tuple-element.44.mine), channel_id=1, source_target_pairs={{0,1},{1,0},{2,3},{3,2},{4,5},{5,4},{6,7},{7,6},{8,9},{9,8},{10,11... | collective-permute-start | bytes 786440 | tf_op jit(solution)/shard_map/ppermute | solution.py:640
  28.9 0.0 collective-permute-start.4
  28.9 0.2 collective-permute-start.6
  29.1 0.9 %collective-permute-done.3.other = f32[16,4096]{1,0:T(8,128)S(1)} collective-permute-done((f32[16,4096]{1,0:T(8,128)S(1)}, f32[16,4096]{1,0:T(8,128)S(1)}, u32[]{:S(2)}, u32[]{:S(2)}) %collective-permute-start.3) | collective-permute-done | bytes 262176 | tf_op jit(solution)/shard_map/ppermute | solution.py:640
  30.0 0.1 ends.1
  30.1 0.8 %collective-permute-start.5 = (f32[8,4096]{1,0:T(8,128)S(1)}, f32[8,4096]{1,0:T(8,128)S(1)}, u32[]{:S(2)}, u32[]{:S(2)}) collective-permute-start(f32[8,4096]{1,0:T(8,128)S(1)} %get-tuple-element.48.end_ref._), channel_id=1, source_target_pairs={{0,2},{2,0},{1,3},{3,1},{4,6},{6,4},{5,7},{7,5},{8,10},{10,8},{9,1... | collective-permute-start | bytes 393224 | tf_op jit(solution)/shard_map/ppermute | solution.py:648
  30.8 0.0 collective-permute-done.6.from_core
  30.9 0.9 %collective-permute-start.7 = (f32[8,2560]{1,0:T(8,128)S(1)}, f32[8,2560]{1,0:T(8,128)S(1)}, u32[]{:S(2)}, u32[]{:S(2)}) collective-permute-start(f32[8,2560]{1,0:T(8,128)S(1)} %relay.1), channel_id=1, source_target_pairs={{0,2},{2,0},{1,3},{3,1},{4,6},{6,4},{5,7},{7,5},{8,10},{10,8},{9,1... | collective-permute-start | bytes 245768 | tf_op jit(solution)/shard_map/ppermute | solution.py:655
  31.7 0.9 %local.1.local_ref = f32[16,8,4096]{2,1,0:T(8,128)S(1)} custom-call(f32[2,16,4096]{2,1,0:T(8,128)S(1)} %get-tuple-element.40.flux_ref, f32[16,8,4096]{2,1,0:T(8,128)S(1)} %get-tuple-element.41.base, f32[16,8,4096]{2,1,0:T(8,128)S(1)} %get-tuple-element.42.ratio, f32[16,8,4096]{2,1,0:T(8,128)S(1)} %get-tuple-element.43.inv, ...), custom_call_target="tpu_custom_call" | custom-call | flops 1 | bytes 1 | tf_op jit(solution)/shard_map/local/pallas_call | solution.py:47
  32.6 2.2 %collective-permute-done.4.res_other.pair_chip = f32[8,5376]{1,0:T(8,128)S(1)} collective-permute-done((f32[8,5376]{1,0:T(8,128)S(1)}, f32[8,5376]{1,0:T(8,128)S(1)}, u32[]{:S(2)}, u32[]{:S(2)}) %collective-permute-start.4) | collective-permute-done | bytes 172064 | tf_op jit(solution)/shard_map/ppermute | solution.py:632
  34.8 2.8 %collective-permute-done.5.end_other = f32[8,4096]{1,0:T(8,128)S(1)} collective-permute-done((f32[8,4096]{1,0:T(8,128)S(1)}, f32[8,4096]{1,0:T(8,128)S(1)}, u32[]{:S(2)}, u32[]{:S(2)}) %collective-permute-start.5) | collective-permute-done | bytes 131104 | tf_op jit(solution)/shard_map/ppermute | solution.py:648
  37.6 1.4 %final.1 = (f32[16,8,4096]{2,1,0:T(8,128)}, f32[8,128]{1,0:T(8,128)S(1)}) custom-call(f32[16,8,4096]{2,1,0:T(8,128)S(1)} %local.1.local_ref, f32[16,8,4096]{2,1,0:T(8,128)S(1)} %get-tuple-element.32.top_col, f32[16,8,4096]{2,1,0:T(8,128)S(1)} %get-tuple-element.33.bottom_col, f32[8,4096]{1,0:T(8,128)S(1)} %get-tuple-element.46.gap_ref, ...), custom_call_target="tpu_custom_call" | custom-call | flops 1 | bytes 1 | tf_op jit(solution)/shard_map/final/pallas_call | solution.py:47
  39.0 0.3 collective-permute-done.7.from_chip
  39.4 1.2 %surface.1 = f32[8,1024]{1,0:T(8,128)} custom-call(f32[3,8,1280]{2,1,0:T(8,128)S(1)} %get-tuple-element.50.own_ref, f32[8,4096]{1,0:T(8,128)S(1)} %get-tuple-element.31.exfil_ref, f32[8,14848]{1,0:T(8,128)S(1)} %collective-permute-done.2.other.pair_core, f32[8,5376]{1,0:T(8,128)S(1)} %collective-permute-done.4.res_other.pair_chip, ...), custom_call_target="tpu_custom_call" | custom-call | flops 1 | bytes 1 | tf_op jit(solution)/shard_map/surface/pallas_call | solution.py:47
  (1 shorter events, 0.0 us)
Async XLA Ops:
  2.6 24.2 %collective-permute-start = (f32[8,18432]{1,0:T(8,128)S(1)}, f32[8,18432]{1,0:T(8,128)S(1)}, u32[]{:S(2)}, u32[]{:S(2)}) collective-permute-start(f32[8,18432]{1,0:T(8,128)S(1)} %get-tuple-element.28.own_up), channel_id=1, source_target_pairs={{0,4},{1,5},{2,6},{3,7},{4,8},{5,9},{6,10},{7,11},{8,12},{9,13},{1... | collective-permute-start | bytes 1769480 | tf_op jit(solution)/shard_map/ppermute | solution.py:604
  5.1 21.6 %collective-permute-start.1 = (f32[8,18432]{1,0:T(8,128)S(1)}, f32[8,18432]{1,0:T(8,128)S(1)}, u32[]{:S(2)}, u32[]{:S(2)}) collective-permute-start(f32[8,18432]{1,0:T(8,128)S(1)} %get-tuple-element.29.own_down), channel_id=1, source_target_pairs={{4,0},{5,1},{6,2},{7,3},{8,4},{9,5},{10,6},{11,7},{12,8},{13,9},{1... | collective-permute-start | bytes 1769480 | tf_op jit(solution)/shard_map/ppermute | solution.py:605
  18.7 5.7 %collective-permute-start.2 = (f32[8,14848]{1,0:T(8,128)S(1)}, f32[8,14848]{1,0:T(8,128)S(1)}, u32[]{:S(2)}, u32[]{:S(2)}) collective-permute-start(f32[8,14848]{1,0:T(8,128)S(1)} %get-tuple-element.38.mine), channel_id=1, source_target_pairs={{0,1},{1,0},{2,3},{3,2},{4,5},{5,4},{6,7},{7,6},{8,9},{9,8},{10,11... | collective-permute-start | bytes 1425416 | tf_op jit(solution)/shard_map/ppermute | solution.py:618
  27.5 2.5 %collective-permute-start.3 = (f32[16,4096]{1,0:T(8,128)S(1)}, f32[16,4096]{1,0:T(8,128)S(1)}, u32[]{:S(2)}, u32[]{:S(2)}) collective-permute-start(f32[16,4096]{1,0:T(8,128)S(1)} %get-tuple-element.44.mine), channel_id=1, source_target_pairs={{0,1},{1,0},{2,3},{3,2},{4,5},{5,4},{6,7},{7,6},{8,9},{9,8},{10,11... | collective-permute-start | bytes 786440 | tf_op jit(solution)/shard_map/ppermute | solution.py:640
  28.9 5.9 %collective-permute-start.4 = (f32[8,5376]{1,0:T(8,128)S(1)}, f32[8,5376]{1,0:T(8,128)S(1)}, u32[]{:S(2)}, u32[]{:S(2)}) collective-permute-start(f32[8,5376]{1,0:T(8,128)S(1)} %get-tuple-element.47.res_ref), channel_id=1, source_target_pairs={{0,2},{2,0},{1,3},{3,1},{4,6},{6,4},{5,7},{7,5},{8,10},{10,8},{9,1... | collective-permute-start | bytes 516104 | tf_op jit(solution)/shard_map/ppermute | solution.py:632
  28.9 2.0 %collective-permute-start.6 = (f32[8,2560]{1,0:T(8,128)S(1)}, f32[8,2560]{1,0:T(8,128)S(1)}, u32[]{:S(2)}, u32[]{:S(2)}) collective-permute-start(f32[8,2560]{1,0:T(8,128)S(1)} %get-tuple-element.52), channel_id=1, source_target_pairs={{0,1},{1,0},{2,3},{3,2},{4,5},{5,4},{6,7},{7,6},{8,9},{9,8},{10,11... | collective-permute-start | bytes 245768 | tf_op jit(solution)/shard_map/ppermute | solution.py:641
  30.1 7.5 %collective-permute-start.5 = (f32[8,4096]{1,0:T(8,128)S(1)}, f32[8,4096]{1,0:T(8,128)S(1)}, u32[]{:S(2)}, u32[]{:S(2)}) collective-permute-start(f32[8,4096]{1,0:T(8,128)S(1)} %get-tuple-element.48.end_ref._), channel_id=1, source_target_pairs={{0,2},{2,0},{1,3},{3,1},{4,6},{6,4},{5,7},{7,5},{8,10},{10,8},{9,1... | collective-permute-start | bytes 393224 | tf_op jit(solution)/shard_map/ppermute | solution.py:648
  30.9 8.5 %collective-permute-start.7 = (f32[8,2560]{1,0:T(8,128)S(1)}, f32[8,2560]{1,0:T(8,128)S(1)}, u32[]{:S(2)}, u32[]{:S(2)}) collective-permute-start(f32[8,2560]{1,0:T(8,128)S(1)} %relay.1), channel_id=1, source_target_pairs={{0,2},{2,0},{1,3},{3,1},{4,6},{6,4},{5,7},{7,5},{8,10},{10,8},{9,1... | collective-permute-start | bytes 245768 | tf_op jit(solution)/shard_map/ppermute | solution.py:655

commit v4 on v3

--- a/solution.py
+++ b/solution.py
@@ -104,13 +104,10 @@
     half = width // 2
     depth = lax.axis_index("depth")
     sides = (up_ref, down_ref)
-    pairs = [(cond_ref, small.at[0]), (shape_ref, small.at[1]), (pore_ref, small.at[2])]
-    for group in range(groups):
-        layers = pl.ds(group * ROWS, ROWS)
-        for side, (target, row) in enumerate(zip(sides, (ROWS - 1, 0))):
-            pairs.append((soil_ref.at[layers, row, :], soils.at[side, group]))
-            pairs.append((head_ref.at[layers, row, :], target.at[:, pl.ds(group * width, width)]))
-    pairs += [
+    pairs = [
+        (cond_ref, small.at[0]),
+        (shape_ref, small.at[1]),
+        (pore_ref, small.at[2]),
         (head_ref.at[0], head_top),
         (soil_ref.at[0], soil_top),
         (pond_ref, pond),
@@ -118,6 +115,12 @@
         (ground_ref, ground),
         (river_ref, river),
     ]
+    fields = len(pairs)
+    for group in range(groups):
+        layers = pl.ds(group * ROWS, ROWS)
+        for side, (target, row) in enumerate(zip(sides, (ROWS - 1, 0))):
+            pairs.append((soil_ref.at[layers, row, :], soils.at[side, group]))
+            pairs.append((head_ref.at[layers, row, :], target.at[:, pl.ds(group * width, width)]))
     copies = [pltpu.make_async_copy(source, target, sem.at[i]) for i, (source, target) in enumerate(pairs)]
     for copy in copies:
         copy.start()
@@ -142,7 +145,29 @@
         table_ref[2 * place] = halves[0]
         table_ref[2 * place + 1] = halves[1]
 
-    following = iter(copies[3:])
+    for copy in copies[3:fields]:
+        copy.wait()
+    wet_pond = ponded[...].astype(jnp.float32) * pond[...]
+    conductivity = lookup(cond_table, soil_top[...]) * jnp.exp2(
+        lookup(steep, soil_top[...]) * jnp.minimum(head_top[...], 0.0)
+    )
+    exfil = -conductivity * (2.0 * (wet_pond - head_top[...]) + 1.0)
+    exfil_ref[...] = exfil
+    conv = LAND_CONVEYANCE + (RIVER_CONVEYANCE - LAND_CONVEYANCE) * river[...].astype(jnp.float32)
+    field = jnp.where(
+        depth < 2, jnp.where(depth == 0, exfil, pond[...]), jnp.where(depth == 2, ground[...], conv)
+    )
+    upper = lax.broadcasted_iota(jnp.int32, (ROWS, half), 0) < 4
+    into = pl.ds(2 * groups * width, half)
+    left, right = field[:, :half], field[:, half:]
+    up_ref[:, into] = jnp.where(upper, pltpu.roll(left, 4, 0), right)
+    down_ref[:, into] = jnp.where(upper, left, pltpu.roll(right, 4, 0))
+    cut = pl.ds(pl.multiple_of(window_start(depth, quarter, window), LANES), window)
+    own_ref[0] = pond[:, cut]
+    own_ref[1] = ground[:, cut]
+    own_ref[2] = LAND_CONVEYANCE + (RIVER_CONVEYANCE - LAND_CONVEYANCE) * river[:, cut].astype(jnp.float32)
+
+    following = iter(copies[fields:])
     for group in range(groups):
         for side, target in enumerate(sides):
             next(following).wait()
@@ -152,27 +177,6 @@
             target[:, pl.ds((groups + group) * width, width)] = lookup(half_res, soil) * jnp.exp2(
                 -lookup(steep, soil) * jnp.minimum(head, 0.0)
             )
-    for copy in following:
-        copy.wait()
-    wet_pond = ponded[...].astype(jnp.float32) * pond[...]
-    conductivity = lookup(cond_table, soil_top[...]) * jnp.exp2(
-        lookup(steep, soil_top[...]) * jnp.minimum(head_top[...], 0.0)
-    )
-    exfil = -conductivity * (2.0 * (wet_pond - head_top[...]) + 1.0)
-    exfil_ref[...] = exfil
-    conv = LAND_CONVEYANCE + (RIVER_CONVEYANCE - LAND_CONVEYANCE) * river[...].astype(jnp.float32)
-    field = jnp.where(
-        depth < 2, jnp.where(depth == 0, exfil, pond[...]), jnp.where(depth == 2, ground[...], conv)
-    )
-    upper = lax.broadcasted_iota(jnp.int32, (ROWS, half), 0) < 4
-    into = pl.ds(2 * groups * width, half)
-    left, right = field[:, :half], field[:, half:]
-    up_ref[:, into] = jnp.where(upper, pltpu.roll(left, 4, 0), right)
-    down_ref[:, into] = jnp.where(upper, left, pltpu.roll(right, 4, 0))
-    cut = pl.ds(pl.multiple_of(window_start(depth, quarter, window), LANES), window)
-    own_ref[0] = pond[:, cut]
-    own_ref[1] = ground[:, cut]
-    own_ref[2] = LAND_CONVEYANCE + (RIVER_CONVEYANCE - LAND_CONVEYANCE) * river[:, cut].astype(jnp.float32)
 
 
 def factor_kernel(
@@ -185,12 +189,6 @@
     is_bottom = jnp.where(depth == 3, 1.0, 0.0)
     is_even = lax.rem(depth, 2) == 0
     chunks = width // CHUNK
-    quarter = width // 4
-    window = quarter + 2 * LANES
-    for place in range(2):
-        resist_ref[:, pl.ds(3 * width + place * window, window)] = exfil_ref[
-            :, static_window(2 * place + 1, quarter, window)
-        ]
 
     def fetch(chunk):
         lanes = pl.ds(pl.multiple_of(chunk * CHUNK, CHUNK), CHUNK)
@@ -339,7 +337,7 @@
 
 def pair_kernel(mine, other, exfil_ref, _, pair_inv_ref, gain_ref, sent_ref):
     width = gain_ref.shape[1]
-    window = sent_ref.shape[1] - width
+    window = (sent_ref.shape[1] - width) // 2
     depth = lax.axis_index("depth")
     inner = (depth == 1) | (depth == 2)
     near, far, corner = (pl.ds(place * width, width) for place in range(3))
@@ -349,13 +347,13 @@
     pair_inv_ref[...] = pair_inv
     gain_ref[...] = gain
     sent_ref[:, pl.ds(0, width)] = jnp.where(inner, mine[:, far], other[:, far]) - inner_corner * gain
-    sent_ref[:, pl.ds(width, window)] = jnp.where(
-        depth == 0, exfil_ref[:, static_window(2, width // 4, window)], other[:, pl.ds(3 * width + window, window)]
-    )
+    for place, quarters in enumerate((depth ^ 2, depth ^ 3)):
+        cut = pl.ds(pl.multiple_of(window_start(quarters, width // 4, window), LANES), window)
+        sent_ref[:, pl.ds(width + place * window, window)] = exfil_ref[:, cut]
 
 
 def halo_kernel(
-    own_up, own_down, from_above, from_below, top_col, bottom_col, sums_ref, _, flux_ref, sent_ref, rows_ref, windows_ref,
+    own_up, own_down, from_above, from_below, top_col, bottom_col, sums_ref, _, flux_ref, near_ref, far_ref, rows_ref, windows_ref,
 ):
     nz, _, width = top_col.shape
     lat = lax.axis_index("lat")
@@ -382,8 +380,8 @@
             added = jnp.where(sublane == ROWS - 1, flux_ref[0, row, lanes], added)
             top_sum = top_sum + top_col[z, :, lanes] * added
             bottom_sum = bottom_sum + bottom_col[z, :, lanes] * added
-        sent_ref[pl.ds(0, ROWS), lanes] = jnp.where(is_even, bottom_sum, top_sum)
-        sent_ref[pl.ds(ROWS, ROWS), lanes] = jnp.where(is_even, top_sum, bottom_sum)
+        near_ref[:, lanes] = jnp.where(is_even, bottom_sum, top_sum)
+        far_ref[:, lanes] = jnp.where(is_even, top_sum, bottom_sum)
 
     half = width // 2
     extra = pl.ds(own_up.shape[1] - half, half)
@@ -394,7 +392,7 @@
     quarter = width // 4
     window = windows_ref.shape[1] // 2
     depth = lax.axis_index("depth")
-    for place, quarters in enumerate((depth ^ 1, depth ^ 3)):
+    for place, quarters in enumerate((depth ^ 2, depth ^ 3)):
         cut = pl.ds(pl.multiple_of(window_start(quarters, quarter, window), LANES), window)
         windows_ref[:, pl.ds(place * window, window)] = rows_ref[:, cut]
 
@@ -422,26 +420,24 @@
             out_ref[z, :, lanes] = x + head_ref[z, :, lanes]
 
 
-def ends_kernel(mine, other, pair_inv_ref, gain_ref, gap_ref, chip_end_ref):
+def ends_kernel(mine, other, far_mine, far_other, pair_inv_ref, gain_ref, gap_ref, chip_end_ref):
     depth = lax.axis_index("depth")
     inner = (depth == 1) | (depth == 2)
     sign = jnp.where(depth < 2, 1.0, -1.0)
-    near, far = pl.ds(0, ROWS), pl.ds(ROWS, ROWS)
-    own, others = mine[near, :], other[near, :]
+    own, others = mine[...], other[...]
     gap = sign * jnp.where(inner, others - own, own - others) + 1.0
     gap_ref[...] = gap * pair_inv_ref[...]
-    chip_end_ref[...] = jnp.where(inner, mine[far, :], other[far, :]) + sign * gain_ref[...] * gap
+    chip_end_ref[...] = jnp.where(inner, far_mine[...], far_other[...]) + sign * gain_ref[...] * gap
 
 
 def final_kernel(
     local_ref, top_col, bottom_col, gap_ref, gain_ref, res_ref, res_other, end_ref, end_other,
-    out_ref, token_ref, held, sem,
+    own_ref, exfil_ref, rows_ref, from_chip, from_core,
+    out_ref, surface_ref, held, last, sem,
 ):
     nz, _, width = local_ref.shape
     depth = lax.axis_index("depth")
     sign = jnp.where(depth < 2, 1.0, -1.0)
-
-    token_ref[...] = jnp.zeros_like(token_ref)
 
     def out_copy(chunk):
         lanes = pl.ds(pl.multiple_of(chunk * CHUNK, CHUNK), CHUNK)
@@ -462,6 +458,8 @@
             )
         out_copy(chunk).start()
 
+    surface(own_ref, exfil_ref, rows_ref, from_chip, from_core, res_other, surface_ref, last)
+
     @pl.loop(0, width // CHUNK)
     def _(chunk):
         out_copy(chunk).wait()
@@ -491,19 +489,21 @@
     )
 
 
-def relay_kernel(rows_ref, from_core, _, sent_ref):
-    window = sent_ref.shape[1] // 2
+def relay_kernel(rows_ref, exfil_ref, from_chip, chip_other, _, __, sent_ref):
+    window = sent_ref.shape[1] // 3
     depth = lax.axis_index("depth")
-    is_even = lax.rem(depth, 2) == 0
-    cut = pl.ds(pl.multiple_of(window_start(depth ^ 2, rows_ref.shape[1] // 4, window), LANES), window)
-    own, other = rows_ref[:, cut], from_core[:, pl.ds(window, window)]
-    sent_ref[:, pl.ds(0, window)] = jnp.where(is_even, own, other)
-    sent_ref[:, pl.ds(window, window)] = jnp.where(is_even, other, own)
-
-
-def surface_kernel(
-    own_ref, exfil_ref, pair_core, pair_chip, rows_ref, from_core, from_chip, _, out_ref, last,
-):
+    is_low = depth < 2
+    cut = pl.ds(pl.multiple_of(window_start(depth ^ 1, rows_ref.shape[1] // 4, window), LANES), window)
+    first, second, third = (pl.ds(place * window, window) for place in range(3))
+    own, other = rows_ref[:, cut], from_chip[:, second]
+    sent_ref[:, first] = jnp.where(is_low, own, other)
+    sent_ref[:, second] = jnp.where(is_low, other, own)
+    sent_ref[:, third] = jnp.where(
+        is_low, exfil_ref[:, cut], chip_other[:, pl.ds(chip_other.shape[1] - window, window)]
+    )
+
+
+def surface(own_ref, exfil_ref, rows_ref, from_chip, from_core, chip_other, out_ref, last):
     window = last.shape[1]
     width = exfil_ref.shape[1]
     quarter = width // 4
@@ -511,15 +511,15 @@
     depth = lax.axis_index("depth")
     is_even = lax.rem(depth, 2) == 0
     upper = lax.broadcasted_iota(jnp.int32, (ROWS, window), 0) < 4
-    first, second = pl.ds(0, window), pl.ds(window, window)
+    first, second, third = (pl.ds(place * window, window) for place in range(3))
 
     cut = pl.ds(pl.multiple_of(window_start(depth, quarter, window), LANES), window)
-    mine, other = rows_ref[:, cut], from_core[:, first]
-    here = (jnp.where(is_even, mine, other), jnp.where(is_even, other, mine))
-    there = (from_chip[:, first], from_chip[:, second])
-    outer = [jnp.where(depth < 2, a, b) for a, b in zip(here + there, there + here)]
-    near = jnp.where(depth == 0, exfil_ref[:, first], pair_core[:, pl.ds(3 * width, window)])
-    near = jnp.where(depth < 2, near, pair_chip[:, pl.ds(width, window)])
+    mine, other = rows_ref[:, cut], from_chip[:, first]
+    here = (jnp.where(depth < 2, mine, other), jnp.where(depth < 2, other, mine))
+    there = (from_core[:, first], from_core[:, second])
+    outer = [jnp.where(is_even, a, b) for low, high in zip(here, there) for a, b in ((low, high), (high, low))]
+    near = jnp.where(depth == 0, exfil_ref[:, first], chip_other[:, pl.ds(width, window)])
+    near = jnp.where(is_even, near, from_core[:, third])
 
     def extended(rows, own):
         own = pltpu.roll(own, 4, 0)
@@ -608,7 +608,7 @@
         factor_kernel,
         "factor",
         [in_vmem(tables), in_vmem(exfil)] + [in_hbm(x) for x in (head, head_old, soil)],
-        [padded, padded] + [block] * 5 + [f32(rows, 3 * width + 2 * window)],
+        [padded, padded] + [block] * 5 + [f32(rows, 3 * width)],
         scratch=[
             pltpu.VMEM((nz, rows, width), jnp.float32),
             pltpu.VMEM((nz, rows, width), jnp.int32),
@@ -627,53 +627,54 @@
         pair_kernel,
         "pair",
         [in_vmem(x) for x in (resist, resist_other, exfil, sums)],
-        [plane, plane, f32(rows, width + window)],
+        [plane, plane, f32(rows, width + 2 * window)],
     )
     chip_other = lax.ppermute(chip_sent, "depth", chip)
 
-    flux, ends, field_rows, windows = call(
+    flux, ends, far_ends, field_rows, windows = call(
         halo_kernel,
         "halo",
         [in_vmem(x) for x in (own_up, own_down, from_above, from_below, top_col, bottom_col, sums, gain)],
-        [f32(2, nz, width), f32(2 * rows, width), plane, f32(rows, 2 * window)],
-    )
-    ends_other = lax.ppermute(ends, "depth", core)
-    windows_core = lax.ppermute(windows, "depth", core)
+        [f32(2, nz, width), plane, plane, plane, f32(rows, 2 * window)],
+    )
+    near_other = lax.ppermute(ends, "depth", core)
+    far_other = lax.ppermute(far_ends, "depth", core)
+    windows_chip = lax.ppermute(windows, "depth", chip)
     local = call(
         local_kernel, "local", [in_vmem(x) for x in (flux, base, ratio, inv, head_v)], [block]
     )[0]
     gap, chip_end = call(
-        ends_kernel, "ends", [in_vmem(x) for x in (ends, ends_other, pair_inv, gain)], [plane, plane]
+        ends_kernel, "ends", [in_vmem(x) for x in (ends, near_other, far_ends, far_other, pair_inv, gain)], [plane, plane]
     )
     chip_end_other = lax.ppermute(chip_end, "depth", chip)
     relayed = call(
         relay_kernel,
         "relay",
-        [in_vmem(x) for x in (field_rows, windows_core, chip_end)],
-        [f32(rows, 2 * window)],
+        [in_vmem(x) for x in (field_rows, exfil, windows_chip, chip_other, chip_end, local)],
+        [f32(rows, 3 * window)],
     )[0]
-    windows_chip = lax.ppermute(relayed, "depth", chip)
-    head_new, token = call(
+    windows_core = lax.ppermute(relayed, "depth", core)
+    head_new, surface_new = call(
         final_kernel,
         "final",
         [
             in_vmem(x)
-            for x in (local, top_col, bottom_col, gap, gain, chip_sent, chip_other, chip_end, chip_end_other)
+            for x in (
+                local, top_col, bottom_col, gap, gain, chip_sent, chip_other, chip_end, chip_end_other,
+                own_fields, exfil, field_rows, windows_chip, windows_core,
+            )
         ],
-        [jax.ShapeDtypeStruct((nz, rows, width), jnp.float32), f32(ROWS, LANES)],
+        [
+            jax.ShapeDtypeStruct((nz, rows, width), jnp.float32),
+            jax.ShapeDtypeStruct((rows, width // 4), jnp.float32),
+        ],
         out_specs=[ANY, VMEM],
-        scratch=[pltpu.VMEM((nz, rows, width), jnp.float32), pltpu.SemaphoreType.DMA((width // CHUNK,))],
-    )
-    surface_new = call(
-        surface_kernel,
-        "surface",
-        [
-            in_vmem(x)
-            for x in (own_fields, exfil, resist_other, chip_other, field_rows, windows_core, windows_chip, token)
+        scratch=[
+            pltpu.VMEM((nz, rows, width), jnp.float32),
+            pltpu.VMEM((2 * rows, window), jnp.float32),
+            pltpu.SemaphoreType.DMA((width // CHUNK,)),
         ],
-        [jax.ShapeDtypeStruct((rows, width // 4), jnp.float32)],
-        scratch=[pltpu.VMEM((2 * rows, window), jnp.float32)],
-    )[0]
+    )
     return (head_new, surface_new)
 
 

time: 40.7 us -> 38 us (0.934)
  waiting for transfers between devices: 8.47 us -> 6.09 us
  Pallas kernels: 16 us -> 15.3 us
    ppermute x1, waiting for transfers between devices: 2.81 us -> 0.14 us  [per_device(): chip_end_other = lax.ppermute(chip_end, 'depth', chip)]
    ppermute x3 -> x4, waiting for transfers between devices: 1.24 us -> 3.76 us  [the longest x1 1.54 us: per_device(): windows_chip = lax.ppermute(windows, 'depth', chip)]
    ppermute x1, waiting for transfers between devices: 2.18 us -> 0.05 us  [per_device(): chip_other = lax.ppermute(chip_sent, 'depth', chip)]
    ppermute x3 -> x4, starting transfers between devices: 2.41 us -> 3.11 us  [the longest x1 1.69 us: per_device(): windows_core = lax.ppermute(relayed, 'depth', core)]
    pallas_call x10 -> x9, Pallas kernels: 16 us -> 15.3 us  [call(): pl.pallas_call(kernel, out_shape=out_shape, in_specs=[spec for spec, _ in...]
    ppermute x1, starting transfers between devices: 0.78 us -> 0.31 us  [per_device(): chip_end_other = lax.ppermute(chip_end, 'depth', chip)]
  transfers between devices with their start and end apart: 8 -> 9, of which waited for: 5 -> 6; matrix products, arithmetic and copies ran while one was open for 0% -> 0% of each run, Pallas kernels for 30% -> 30%
where the time goes in v4:
time: 38 us; the launch traced here: 37.9 us
  starting transfers between devices  15.8 us (42%)
  Pallas kernels  15.3 us (40%)
  waiting for transfers between devices  6.09 us (16%)
  between operations  0.7 us (2%)
    pallas_call x9, Pallas kernels, call(): pl.pallas_call(kernel, out_shape=out_shape, in_specs=[spec for spec, _ in...  15.3 us
    ppermute x1, starting transfers between devices, per_device(): from_below = lax.ppermute(own_down, ('lat', 'depth'), down)  8.67 us
    ppermute x1, starting transfers between devices, per_device(): from_above = lax.ppermute(own_up, ('lat', 'depth'), up)  2.54 us
    ppermute x1, waiting for transfers between devices, per_device(): from_above = lax.ppermute(own_up, ('lat', 'depth'), up)  2.14 us
    ppermute x1, starting transfers between devices, per_device(): windows_core = lax.ppermute(relayed, 'depth', core)  1.69 us
    ppermute x1, waiting for transfers between devices, per_device(): windows_chip = lax.ppermute(windows, 'depth', chip)  1.54 us
    ppermute x1, starting transfers between devices, per_device(): near_other = lax.ppermute(ends, 'depth', core)  1.32 us
    ppermute x1, starting transfers between devices, per_device(): resist_other = lax.ppermute(resist, 'depth', core)  1.04 us
  transfers between devices with their start and end apart: 9, of which 6 were waited for; matrix products, arithmetic and copies ran while one was open for 0% of the time, Pallas kernels for 30%

profile of v4, /device:TPU:1, one launch (start us, length us, event | category | flops | bytes accessed | tf_op | source)
XLA Modules:
  0.0 37.9 jit_solution(10796128537085904129)
XLA Ops:
  0.6 1.9 %pack.1 = (f32[8,18432]{1,0:T(8,128)S(1)}, f32[8,18432]{1,0:T(8,128)S(1)}, f32[6,8,128]{2,1,0:T(8,128)S(1)}, f32[8,4096]{1,0:T(8,128)S(1)}, f32[3,8,1280]{2,1,0:T(8,128)S(1)}) custom-call(f32[12]{0:T(128)} %cond_ref.1, f32[12]{0:T(128)} %shape_ref.1, f32[12]{0:T(128)} %pore_ref.1, f32[16,8,4096]{2,1,0:T(8,128)} %head_hbm.1, s32[16,8,4096]{2,1,0:T(8,128)} %soil_hbm.1, ...), custom_call_target="tpu_custom_call" | custom-call | flops 1 | bytes 1 | tf_op jit(solution)/shard_map/pack/pallas_call | solution.py:47
  2.6 2.5 %collective-permute-start = (f32[8,18432]{1,0:T(8,128)S(1)}, f32[8,18432]{1,0:T(8,128)S(1)}, u32[]{:S(2)}, u32[]{:S(2)}) collective-permute-start(f32[8,18432]{1,0:T(8,128)S(1)} %get-tuple-element.27.own_up), channel_id=1, source_target_pairs={{0,4},{1,5},{2,6},{3,7},{4,8},{5,9},{6,10},{7,11},{8,12},{9,13},{1... | collective-permute-start | bytes 1769480 | tf_op jit(solution)/shard_map/ppermute | solution.py:604
  5.1 8.7 %collective-permute-start.1 = (f32[8,18432]{1,0:T(8,128)S(1)}, f32[8,18432]{1,0:T(8,128)S(1)}, u32[]{:S(2)}, u32[]{:S(2)}) collective-permute-start(f32[8,18432]{1,0:T(8,128)S(1)} %get-tuple-element.28.own_down), channel_id=1, source_target_pairs={{4,0},{5,1},{6,2},{7,3},{8,4},{9,5},{10,6},{11,7},{12,8},{13,9},{1... | collective-permute-start | bytes 1769480 | tf_op jit(solution)/shard_map/ppermute | solution.py:605
  13.8 4.9 %factor.1 = (f32[16,8,4224]{2,1,0:T(8,128)S(1)}, f32[16,8,4224]{2,1,0:T(8,128)S(1)}, f32[16,8,4096]{2,1,0:T(8,128)S(1)}, f32[16,8,4096]{2,1,0:T(8,128)S(1)}, f32...) custom-call(f32[6,8,128]{2,1,0:T(8,128)S(1)} %get-tuple-element.29.ta, ...), custom_call_target="tpu_custom_call" | custom-call | flops 1 | bytes 1 | tf_op jit(solution)/shard_map/factor/pallas_call | solution.py:47
  18.7 1.0 %collective-permute-start.2 = (f32[8,12288]{1,0:T(8,128)S(1)}, f32[8,12288]{1,0:T(8,128)S(1)}, u32[]{:S(2)}, u32[]{:S(2)}) collective-permute-start(f32[8,12288]{1,0:T(8,128)S(1)} %get-tuple-element.37.mine), channel_id=1, source_target_pairs={{0,1},{1,0},{2,3},{3,2},{4,5},{5,4},{6,7},{7,6},{8,9},{9,8},{10,11... | collective-permute-start | bytes 1179656 | tf_op jit(solution)/shard_map/ppermute | solution.py:618
  19.7 4.7 %lateral.1 = (f32[16,8,4096]{2,1,0:T(8,128)S(1)}, f32[16,4096]{1,0:T(8,128)S(1)}) custom-call(f32[16,8,4224]{2,1,0:T(8,128)S(1)} %get-tuple-element.33.head_ref, f32[16,8,4224]{2,1,0:T(8,128)S(1)} %get-tuple-element.34.sigma, f32[16,8,4096]{2,1,0:T(8,128)S(1)} %get-tuple-element.35.base_in, f32[16,8,4096]{2,1,0:T(8,128)S(1)} %get-tuple-element.31.top_col, ...), custom_call_target="tpu_custom_call" | custom-call | flops 1 | bytes 1 | tf_op jit(solution)/shard_map/lateral/pallas_call | solution.py:47
  24.4 0.0 collective-permute-done.2.other
  24.4 0.1 pair.1
  24.5 0.1 collective-permute-start.5
  24.6 2.1 %collective-permute-done.from_above = f32[8,18432]{1,0:T(8,128)S(1)} collective-permute-done((f32[8,18432]{1,0:T(8,128)S(1)}, f32[8,18432]{1,0:T(8,128)S(1)}, u32[]{:S(2)}, u32[]{:S(2)}) %collective-permute-start) | collective-permute-done | bytes 589856 | tf_op jit(solution)/shard_map/ppermute | solution.py:604
  26.7 0.0 collective-permute-done.1.from_below
  26.7 0.8 %halo.1 = (f32[2,16,4096]{2,1,0:T(8,128)S(1)}, f32[8,4096]{1,0:T(8,128)S(1)}, f32[8,4096]{1,0:T(8,128)S(1)}, f32[8,4096]{1,0:T(8,128)S(1)}, f32[8,2560]{1,0:T(8,128)S(1)}) custom-call(f32[8,18432]{1,0:T(8,128)S(1)} %get-tuple-element.27.own_up, f32[8,18432]{1,0:T(8,128)S(1)} %get-tuple-element.28.own_down, f32[8,18432]{1,0:T(8,128)S(1)} %collective-permute-done.from_above, ...), custom_call_target="tpu_custom_call" | custom-call | flops 1 | bytes 1 | tf_op jit(solution)/shard_map/halo/pallas_call | solution.py:47
  27.5 1.3 %collective-permute-start.3 = (f32[8,4096]{1,0:T(8,128)S(1)}, f32[8,4096]{1,0:T(8,128)S(1)}, u32[]{:S(2)}, u32[]{:S(2)}) collective-permute-start(f32[8,4096]{1,0:T(8,128)S(1)} %get-tuple-element.43.mine), channel_id=1, source_target_pairs={{0,1},{1,0},{2,3},{3,2},{4,5},{5,4},{6,7},{7,6},{8,9},{9,8},{10,11... | collective-permute-start | bytes 393224 | tf_op jit(solution)/shard_map/ppermute | solution.py:640
  28.8 0.1 collective-permute-start.4
  28.9 0.0 collective-permute-start.7
  28.9 0.9 %collective-permute-done.3.other = f32[8,4096]{1,0:T(8,128)S(1)} collective-permute-done((f32[8,4096]{1,0:T(8,128)S(1)}, f32[8,4096]{1,0:T(8,128)S(1)}, u32[]{:S(2)}, u32[]{:S(2)}) %collective-permute-start.3) | collective-permute-done | bytes 131104 | tf_op jit(solution)/shard_map/ppermute | solution.py:640
  29.8 0.4 collective-permute-done.4.far_other
  30.2 0.1 ends.1
  30.2 0.3 collective-permute-start.6
  30.5 0.9 %local.1.__.local_ref = f32[16,8,4096]{2,1,0:T(8,128)S(1)} custom-call(f32[2,16,4096]{2,1,0:T(8,128)S(1)} %get-tuple-element.39.flux_ref, f32[16,8,4096]{2,1,0:T(8,128)S(1)} %get-tuple-element.40.base, f32[16,8,4096]{2,1,0:T(8,128)S(1)} %get-tuple-element.41.ratio, f32[16,8,4096]{2,1,0:T(8,128)S(1)} %get-tuple-element.42.inv, ...), custom_call_target="tpu_custom_call" | custom-call | flops 1 | bytes 1 | tf_op jit(solution)/shard_map/local/pallas_call | solution.py:47
  31.4 0.0 collective-permute-done.5.chip_other.res_other
  31.5 1.5 %collective-permute-done.7.from_chip = f32[8,2560]{1,0:T(8,128)S(1)} collective-permute-done((f32[8,2560]{1,0:T(8,128)S(1)}, f32[8,2560]{1,0:T(8,128)S(1)}, u32[]{:S(2)}, u32[]{:S(2)}) %collective-permute-start.7) | collective-permute-done | bytes 81952 | tf_op jit(solution)/shard_map/ppermute | solution.py:642
  33.0 1.7 %collective-permute-start.8 = (f32[8,3840]{1,0:T(8,128)S(1)}, f32[8,3840]{1,0:T(8,128)S(1)}, u32[]{:S(2)}, u32[]{:S(2)}) collective-permute-start(f32[8,3840]{1,0:T(8,128)S(1)} %relay.1), channel_id=1, source_target_pairs={{0,1},{1,0},{2,3},{3,2},{4,5},{5,4},{6,7},{7,6},{8,9},{9,8},{10,11... | collective-permute-start | bytes 368648 | tf_op jit(solution)/shard_map/ppermute | solution.py:656
  34.7 1.0 %collective-permute-done.8.from_core = f32[8,3840]{1,0:T(8,128)S(1)} collective-permute-done((f32[8,3840]{1,0:T(8,128)S(1)}, f32[8,3840]{1,0:T(8,128)S(1)}, u32[]{:S(2)}, u32[]{:S(2)}) %collective-permute-start.8) | collective-permute-done | bytes 122912 | tf_op jit(solution)/shard_map/ppermute | solution.py:656
  35.7 0.1 collective-permute-done.6.end_other
  35.8 2.1 %final.1 = (f32[16,8,4096]{2,1,0:T(8,128)}, f32[8,1024]{1,0:T(8,128)}) custom-call(f32[16,8,4096]{2,1,0:T(8,128)S(1)} %local.1.__.local_ref, f32[16,8,4096]{2,1,0:T(8,128)S(1)} %get-tuple-element.31.top_col, f32[16,8,4096]{2,1,0:T(8,128)S(1)} %get-tuple-element.32.bottom_col, f32[8,4096]{1,0:T(8,128)S(1)} %get-tuple-element.46.gap_ref, ...), custom_call_target="tpu_custom_call" | custom-call | flops 1 | bytes 1 | tf_op jit(solution)/shard_map/final/pallas_call | solution.py:47
  (1 shorter events, 0.0 us)
Async XLA Ops:
  2.6 24.2 %collective-permute-start = (f32[8,18432]{1,0:T(8,128)S(1)}, f32[8,18432]{1,0:T(8,128)S(1)}, u32[]{:S(2)}, u32[]{:S(2)}) collective-permute-start(f32[8,18432]{1,0:T(8,128)S(1)} %get-tuple-element.27.own_up), channel_id=1, source_target_pairs={{0,4},{1,5},{2,6},{3,7},{4,8},{5,9},{6,10},{7,11},{8,12},{9,13},{1... | collective-permute-start | bytes 1769480 | tf_op jit(solution)/shard_map/ppermute | solution.py:604
  5.1 21.6 %collective-permute-start.1 = (f32[8,18432]{1,0:T(8,128)S(1)}, f32[8,18432]{1,0:T(8,128)S(1)}, u32[]{:S(2)}, u32[]{:S(2)}) collective-permute-start(f32[8,18432]{1,0:T(8,128)S(1)} %get-tuple-element.28.own_down), channel_id=1, source_target_pairs={{4,0},{5,1},{6,2},{7,3},{8,4},{9,5},{10,6},{11,7},{12,8},{13,9},{1... | collective-permute-start | bytes 1769480 | tf_op jit(solution)/shard_map/ppermute | solution.py:605
  18.7 5.7 %collective-permute-start.2 = (f32[8,12288]{1,0:T(8,128)S(1)}, f32[8,12288]{1,0:T(8,128)S(1)}, u32[]{:S(2)}, u32[]{:S(2)}) collective-permute-start(f32[8,12288]{1,0:T(8,128)S(1)} %get-tuple-element.37.mine), channel_id=1, source_target_pairs={{0,1},{1,0},{2,3},{3,2},{4,5},{5,4},{6,7},{7,6},{8,9},{9,8},{10,11... | collective-permute-start | bytes 1179656 | tf_op jit(solution)/shard_map/ppermute | solution.py:618
  24.5 7.0 %collective-permute-start.5 = (f32[8,6656]{1,0:T(8,128)S(1)}, f32[8,6656]{1,0:T(8,128)S(1)}, u32[]{:S(2)}, u32[]{:S(2)}) collective-permute-start(f32[8,6656]{1,0:T(8,128)S(1)} %get-tuple-element.47.res_ref), channel_id=1, source_target_pairs={{0,2},{2,0},{1,3},{3,1},{4,6},{6,4},{5,7},{7,5},{8,10},{10,8},{9,1... | collective-permute-start | bytes 638984 | tf_op jit(solution)/shard_map/ppermute | solution.py:632
  27.5 2.3 %collective-permute-start.3 = (f32[8,4096]{1,0:T(8,128)S(1)}, f32[8,4096]{1,0:T(8,128)S(1)}, u32[]{:S(2)}, u32[]{:S(2)}) collective-permute-start(f32[8,4096]{1,0:T(8,128)S(1)} %get-tuple-element.43.mine), channel_id=1, source_target_pairs={{0,1},{1,0},{2,3},{3,2},{4,5},{5,4},{6,7},{7,6},{8,9},{9,8},{10,11... | collective-permute-start | bytes 393224 | tf_op jit(solution)/shard_map/ppermute | solution.py:640
  28.8 1.3 %collective-permute-start.4 = (f32[8,4096]{1,0:T(8,128)S(1)}, f32[8,4096]{1,0:T(8,128)S(1)}, u32[]{:S(2)}, u32[]{:S(2)}) collective-permute-start(f32[8,4096]{1,0:T(8,128)S(1)} %get-tuple-element.44.far_mine), channel_id=1, source_target_pairs={{0,1},{1,0},{2,3},{3,2},{4,5},{5,4},{6,7},{7,6},{8,9},{9,8},{10,11... | collective-permute-start | bytes 393224 | tf_op jit(solution)/shard_map/ppermute | solution.py:641
  28.9 4.1 %collective-permute-start.7 = (f32[8,2560]{1,0:T(8,128)S(1)}, f32[8,2560]{1,0:T(8,128)S(1)}, u32[]{:S(2)}, u32[]{:S(2)}) collective-permute-start(f32[8,2560]{1,0:T(8,128)S(1)} %get-tuple-element.51), channel_id=1, source_target_pairs={{0,2},{2,0},{1,3},{3,1},{4,6},{6,4},{5,7},{7,5},{8,10},{10,8},{9,1... | collective-permute-start | bytes 245768 | tf_op jit(solution)/shard_map/ppermute | solution.py:642
  30.2 5.6 %collective-permute-start.6 = (f32[8,4096]{1,0:T(8,128)S(1)}, f32[8,4096]{1,0:T(8,128)S(1)}, u32[]{:S(2)}, u32[]{:S(2)}) collective-permute-start(f32[8,4096]{1,0:T(8,128)S(1)} %get-tuple-element.48._.end_ref), channel_id=1, source_target_pairs={{0,2},{2,0},{1,3},{3,1},{4,6},{6,4},{5,7},{7,5},{8,10},{10,8},{9,1... | collective-permute-start | bytes 393224 | tf_op jit(solution)/shard_map/ppermute | solution.py:649
  33.0 2.7 %collective-permute-start.8 = (f32[8,3840]{1,0:T(8,128)S(1)}, f32[8,3840]{1,0:T(8,128)S(1)}, u32[]{:S(2)}, u32[]{:S(2)}) collective-permute-start(f32[8,3840]{1,0:T(8,128)S(1)} %relay.1), channel_id=1, source_target_pairs={{0,1},{1,0},{2,3},{3,2},{4,5},{5,4},{6,7},{7,6},{8,9},{9,8},{10,11... | collective-permute-start | bytes 368648 | tf_op jit(solution)/shard_map/ppermute | solution.py:656

commit v5 on v4

--- a/solution.py
+++ b/solution.py
@@ -21,6 +21,7 @@
 LANES = 128
 ROWS = 8
 CHUNK = 512
+HALO_CHUNK = 1024
 AHEAD = 3
 VMEM_LIMIT = 8 * 1024 * 1024
 
@@ -279,9 +280,16 @@
 
 
 def lateral_kernel(
-    head_ref, sigma, base_in, top_col, bottom_col, base, sums_ref, carried,
+    head_ref, sigma, base_in, top_col, bottom_col, _, base, sums_ref, rows_ref, carried, sem,
 ):
     nz, _, width = base.shape
+    copies = [
+        pltpu.make_async_copy(array.at[:, row, :], rows_ref.at[2 * place + side], sem.at[2 * place + side])
+        for place, array in enumerate((top_col, bottom_col))
+        for side, row in enumerate((ROWS - 1, 0))
+    ]
+    for copy in copies:
+        copy.start()
     sublane = lax.broadcasted_iota(jnp.int32, (ROWS, CHUNK), 0)
     inner = sublane < ROWS - 1
     lane = lax.broadcasted_iota(jnp.int32, (ROWS, LANES), 1)
@@ -334,8 +342,11 @@
         sums_ref[pl.ds(0, ROWS), lanes] = top_sum + head_ref[0, :, lanes]
         sums_ref[pl.ds(ROWS, ROWS), lanes] = bottom_sum + head_ref[nz - 1, :, lanes]
 
-
-def pair_kernel(mine, other, exfil_ref, _, pair_inv_ref, gain_ref, sent_ref):
+    for copy in copies:
+        copy.wait()
+
+
+def pair_kernel(mine, other, exfil_ref, pair_inv_ref, gain_ref, sent_ref):
     width = gain_ref.shape[1]
     window = (sent_ref.shape[1] - width) // 2
     depth = lax.axis_index("depth")
@@ -353,35 +364,43 @@
 
 
 def halo_kernel(
-    own_up, own_down, from_above, from_below, top_col, bottom_col, sums_ref, _, flux_ref, near_ref, far_ref, rows_ref, windows_ref,
+    own_up, own_down, from_above, from_below, end_rows, sums_ref, _, flux_ref, near_ref, far_ref, rows_ref, windows_ref,
 ):
-    nz, _, width = top_col.shape
+    _, nz, width = flux_ref.shape
     lat = lax.axis_index("lat")
     has_above = jnp.where(lat == 0, 0.0, 1.0)
     has_below = jnp.where(lat == lax.axis_size("lat") - 1, 0.0, 1.0)
     is_even = lax.rem(lax.axis_index("depth"), 2) == 0
-    sublane = lax.broadcasted_iota(jnp.int32, (ROWS, CHUNK), 0)
-    for side, other, own, scale in ((0, from_below, own_up, has_below), (1, from_above, own_down, has_above)):
-        for group in range(nz // ROWS):
-            heads = pl.ds(group * width, width)
-            sigmas = pl.ds((nz // ROWS + group) * width, width)
-            flux_ref[side, pl.ds(group * ROWS, ROWS), :] = rcp(other[:, sigmas] + own[:, sigmas]) * (
-                (other[:, heads] - own[:, heads]) * scale
-            )
-
-    @pl.loop(0, width // CHUNK)
+    sublane = lax.broadcasted_iota(jnp.int32, (ROWS, HALO_CHUNK), 0)
+
+    @pl.loop(0, width // HALO_CHUNK)
     def _(chunk):
-        lanes = pl.ds(pl.multiple_of(chunk * CHUNK, CHUNK), CHUNK)
-        top_sum = sums_ref[pl.ds(0, ROWS), lanes]
-        bottom_sum = sums_ref[pl.ds(ROWS, ROWS), lanes]
-        for z in range(nz):
-            row = pl.ds(z, 1)
-            added = jnp.where(sublane == 0, flux_ref[1, row, lanes], 0.0)
-            added = jnp.where(sublane == ROWS - 1, flux_ref[0, row, lanes], added)
-            top_sum = top_sum + top_col[z, :, lanes] * added
-            bottom_sum = bottom_sum + bottom_col[z, :, lanes] * added
-        near_ref[:, lanes] = jnp.where(is_even, bottom_sum, top_sum)
-        far_ref[:, lanes] = jnp.where(is_even, top_sum, bottom_sum)
+        start = pl.multiple_of(chunk * HALO_CHUNK, HALO_CHUNK)
+        lanes = pl.ds(start, HALO_CHUNK)
+        added = [[], []]
+        for side, other, own, scale in ((0, from_below, own_up, has_below), (1, from_above, own_down, has_above)):
+            totals = [None, None]
+            for group in range(nz // ROWS):
+                heads = pl.ds(pl.multiple_of(group * width + start, HALO_CHUNK), HALO_CHUNK)
+                sigmas = pl.ds(pl.multiple_of((nz // ROWS + group) * width + start, HALO_CHUNK), HALO_CHUNK)
+                layers = pl.ds(group * ROWS, ROWS)
+                flux = rcp(other[:, sigmas] + own[:, sigmas]) * ((other[:, heads] - own[:, heads]) * scale)
+                flux_ref[side, layers, lanes] = flux
+                for end in range(2):
+                    part = flux * end_rows[2 * end + side, layers, lanes]
+                    totals[end] = part if group == 0 else totals[end] + part
+            for end in range(2):
+                total = totals[end]
+                for by in (4, 2, 1):
+                    total = total + pltpu.roll(total, by, 0)
+                added[end].append(total)
+        sums = []
+        for end in range(2):
+            total = jnp.where(sublane == 0, added[end][1], 0.0)
+            total = jnp.where(sublane == ROWS - 1, added[end][0], total)
+            sums.append(sums_ref[pl.ds(end * ROWS, ROWS), lanes] + total)
+        near_ref[:, lanes] = jnp.where(is_even, sums[1], sums[0])
+        far_ref[:, lanes] = jnp.where(is_even, sums[0], sums[1])
 
     half = width // 2
     extra = pl.ds(own_up.shape[1] - half, half)
@@ -431,13 +450,15 @@
 
 
 def final_kernel(
-    local_ref, top_col, bottom_col, gap_ref, gain_ref, res_ref, res_other, end_ref, end_other,
-    own_ref, exfil_ref, rows_ref, from_chip, from_core,
-    out_ref, surface_ref, held, last, sem,
+    local_ref, top_col, bottom_col, gap_ref, gain_ref, res_ref, res_other, end_ref, end_other, level_ref,
+    out_ref, surface_ref, held, sem, level_sem,
 ):
     nz, _, width = local_ref.shape
     depth = lax.axis_index("depth")
     sign = jnp.where(depth < 2, 1.0, -1.0)
+
+    level_copy = pltpu.make_async_copy(level_ref, surface_ref, level_sem)
+    level_copy.start()
 
     def out_copy(chunk):
         lanes = pl.ds(pl.multiple_of(chunk * CHUNK, CHUNK), CHUNK)
@@ -458,11 +479,11 @@
             )
         out_copy(chunk).start()
 
-    surface(own_ref, exfil_ref, rows_ref, from_chip, from_core, res_other, surface_ref, last)
-
     @pl.loop(0, width // CHUNK)
     def _(chunk):
         out_copy(chunk).wait()
+
+    level_copy.wait()
 
 
 def shift_rows(x, by):
@@ -503,7 +524,7 @@
     )
 
 
-def surface(own_ref, exfil_ref, rows_ref, from_chip, from_core, chip_other, out_ref, last):
+def surface_kernel(own_ref, exfil_ref, rows_ref, from_chip, from_core, chip_other, out_ref, last):
     window = last.shape[1]
     width = exfil_ref.shape[1]
     quarter = width // 4
@@ -616,25 +637,25 @@
         ],
     )
     resist_other = lax.ppermute(resist, "depth", core)
-    base, sums = call(
-        lateral_kernel,
-        "lateral",
-        [in_vmem(x) for x in (head_v, sigma, base, top_col, bottom_col)],
-        [block, f32(2 * rows, width)],
-        scratch=[pltpu.VMEM((3, nz, rows, LANES), jnp.float32)],
-    )
     pair_inv, gain, chip_sent = call(
         pair_kernel,
         "pair",
-        [in_vmem(x) for x in (resist, resist_other, exfil, sums)],
+        [in_vmem(x) for x in (resist, resist_other, exfil)],
         [plane, plane, f32(rows, width + 2 * window)],
     )
     chip_other = lax.ppermute(chip_sent, "depth", chip)
 
+    base, sums, end_rows = call(
+        lateral_kernel,
+        "lateral",
+        [in_vmem(x) for x in (head_v, sigma, base, top_col, bottom_col, gain)],
+        [block, f32(2 * rows, width), f32(4, nz, width)],
+        scratch=[pltpu.VMEM((3, nz, rows, LANES), jnp.float32), pltpu.SemaphoreType.DMA((4,))],
+    )
     flux, ends, far_ends, field_rows, windows = call(
         halo_kernel,
         "halo",
-        [in_vmem(x) for x in (own_up, own_down, from_above, from_below, top_col, bottom_col, sums, gain)],
+        [in_vmem(x) for x in (own_up, own_down, from_above, from_below, end_rows, sums, gain)],
         [f32(2, nz, width), plane, plane, plane, f32(rows, 2 * window)],
     )
     near_other = lax.ppermute(ends, "depth", core)
@@ -654,25 +675,34 @@
         [f32(rows, 3 * window)],
     )[0]
     windows_core = lax.ppermute(relayed, "depth", core)
+    level = call(
+        surface_kernel,
+        "surface",
+        [
+            in_vmem(x)
+            for x in (own_fields, exfil, field_rows, windows_chip, windows_core, chip_other)
+        ],
+        [f32(rows, width // 4)],
+        scratch=[pltpu.VMEM((2 * rows, window), jnp.float32)],
+    )[0]
     head_new, surface_new = call(
         final_kernel,
         "final",
         [
             in_vmem(x)
             for x in (
-                local, top_col, bottom_col, gap, gain, chip_sent, chip_other, chip_end, chip_end_other,
-                own_fields, exfil, field_rows, windows_chip, windows_core,
+                local, top_col, bottom_col, gap, gain, chip_sent, chip_other, chip_end, chip_end_other, level,
             )
         ],
         [
             jax.ShapeDtypeStruct((nz, rows, width), jnp.float32),
             jax.ShapeDtypeStruct((rows, width // 4), jnp.float32),
         ],
-        out_specs=[ANY, VMEM],
+        out_specs=[ANY, ANY],
         scratch=[
             pltpu.VMEM((nz, rows, width), jnp.float32),
-            pltpu.VMEM((2 * rows, window), jnp.float32),
             pltpu.SemaphoreType.DMA((width // CHUNK,)),
+            pltpu.SemaphoreType.DMA,
         ],
     )
     return (head_new, surface_new)

time: 38 us -> 37.1 us (0.976)
  waiting for transfers between devices: 6.09 us -> 2.98 us
  starting transfers between devices: 15.8 us -> 17.4 us
  Pallas kernels: 15.3 us -> 15.8 us
    ppermute x1, waiting for transfers between devices: 2.14 us -> 0.01 us  [per_device(): from_above = lax.ppermute(own_up, ('lat', 'depth'), up)]
    ppermute x1, waiting for transfers between devices: 0.01 us -> 1.35 us  [per_device(): resist_other = lax.ppermute(resist, 'depth', core)]
    ppermute x1, waiting for transfers between devices: 1.54 us -> 0.32 us  [per_device(): windows_chip = lax.ppermute(windows, 'depth', chip)]
    ppermute x1, starting transfers between devices: 0.01 us -> 0.93 us  [per_device(): windows_chip = lax.ppermute(windows, 'depth', chip)]
    ppermute x1, waiting for transfers between devices: 0.88 us -> 0.01 us  [per_device(): near_other = lax.ppermute(ends, 'depth', core)]
    ppermute x1, starting transfers between devices: 0.31 us -> 1.01 us  [per_device(): chip_end_other = lax.ppermute(chip_end, 'depth', chip)]
    pallas_call x9 -> x10, Pallas kernels: 15.3 us -> 15.8 us  [call(): pl.pallas_call(kernel, out_shape=out_shape, in_specs=[spec for spec, _ in...]
  transfers between devices with their start and end apart: 9 -> 9, of which waited for: 6 -> 4; matrix products, arithmetic and copies ran while one was open for 0% -> 0% of each run, Pallas kernels for 30% -> 34%
where the time goes in v5:
time: 37.1 us; the launch traced here: 36.9 us
  starting transfers between devices  17.4 us (47%)
  Pallas kernels  15.8 us (43%)
  waiting for transfers between devices  2.98 us (8%)
  between operations  0.73 us (2%)
    pallas_call x10, Pallas kernels, call(): pl.pallas_call(kernel, out_shape=out_shape, in_specs=[spec for spec, _ in...  15.8 us
    ppermute x1, starting transfers between devices, per_device(): from_below = lax.ppermute(own_down, ('lat', 'depth'), down)  8.67 us
    ppermute x1, starting transfers between devices, per_device(): from_above = lax.ppermute(own_up, ('lat', 'depth'), up)  2.54 us
    ppermute x1, starting transfers between devices, per_device(): windows_core = lax.ppermute(relayed, 'depth', core)  1.76 us
    ppermute x1, waiting for transfers between devices, per_device(): resist_other = lax.ppermute(resist, 'depth', core)  1.35 us
    ppermute x1, starting transfers between devices, per_device(): near_other = lax.ppermute(ends, 'depth', core)  1.26 us
    ppermute x1, starting transfers between devices, per_device(): resist_other = lax.ppermute(resist, 'depth', core)  1.04 us
    ppermute x1, starting transfers between devices, per_device(): chip_end_other = lax.ppermute(chip_end, 'depth', chip)  1.01 us
  transfers between devices with their start and end apart: 9, of which 4 were waited for; matrix products, arithmetic and copies ran while one was open for 0% of the time, Pallas kernels for 34%

profile of v5, /device:TPU:1, one launch (start us, length us, event | category | flops | bytes accessed | tf_op | source)
XLA Modules:
  0.0 36.9 jit_solution(985950199723293427)
XLA Ops:
  0.6 1.9 %pack.1 = (f32[8,18432]{1,0:T(8,128)S(1)}, f32[8,18432]{1,0:T(8,128)S(1)}, f32[6,8,128]{2,1,0:T(8,128)S(1)}, f32[8,4096]{1,0:T(8,128)S(1)}, f32[3,8,1280]{2,1,0:T(8,128)S(1)}) custom-call(f32[12]{0:T(128)} %cond_ref.1, f32[12]{0:T(128)} %shape_ref.1, f32[12]{0:T(128)} %pore_ref.1, f32[16,8,4096]{2,1,0:T(8,128)} %head_hbm.1, s32[16,8,4096]{2,1,0:T(8,128)} %soil_hbm.1, ...), custom_call_target="tpu_custom_call" | custom-call | flops 1 | bytes 1 | tf_op jit(solution)/shard_map/pack/pallas_call | solution.py:48
  2.6 2.5 %collective-permute-start = (f32[8,18432]{1,0:T(8,128)S(1)}, f32[8,18432]{1,0:T(8,128)S(1)}, u32[]{:S(2)}, u32[]{:S(2)}) collective-permute-start(f32[8,18432]{1,0:T(8,128)S(1)} %get-tuple-element.28.own_up), channel_id=1, source_target_pairs={{0,4},{1,5},{2,6},{3,7},{4,8},{5,9},{6,10},{7,11},{8,12},{9,13},{1... | collective-permute-start | bytes 1769480 | tf_op jit(solution)/shard_map/ppermute | solution.py:625
  5.1 8.7 %collective-permute-start.1 = (f32[8,18432]{1,0:T(8,128)S(1)}, f32[8,18432]{1,0:T(8,128)S(1)}, u32[]{:S(2)}, u32[]{:S(2)}) collective-permute-start(f32[8,18432]{1,0:T(8,128)S(1)} %get-tuple-element.29.own_down), channel_id=1, source_target_pairs={{4,0},{5,1},{6,2},{7,3},{8,4},{9,5},{10,6},{11,7},{12,8},{13,9},{1... | collective-permute-start | bytes 1769480 | tf_op jit(solution)/shard_map/ppermute | solution.py:626
  13.8 4.9 %factor.1 = (f32[16,8,4224]{2,1,0:T(8,128)S(1)}, f32[16,8,4224]{2,1,0:T(8,128)S(1)}, f32[16,8,4096]{2,1,0:T(8,128)S(1)}, f32[16,8,4096]{2,1,0:T(8,128)S(1)}, f32...) custom-call(f32[6,8,128]{2,1,0:T(8,128)S(1)} %get-tuple-element.30.ta, ...), custom_call_target="tpu_custom_call" | custom-call | flops 1 | bytes 1 | tf_op jit(solution)/shard_map/factor/pallas_call | solution.py:48
  18.7 1.0 %collective-permute-start.2 = (f32[8,12288]{1,0:T(8,128)S(1)}, f32[8,12288]{1,0:T(8,128)S(1)}, u32[]{:S(2)}, u32[]{:S(2)}) collective-permute-start(f32[8,12288]{1,0:T(8,128)S(1)} %get-tuple-element.37.mine), channel_id=1, source_target_pairs={{0,1},{1,0},{2,3},{3,2},{4,5},{5,4},{6,7},{7,6},{8,9},{9,8},{10,11... | collective-permute-start | bytes 1179656 | tf_op jit(solution)/shard_map/ppermute | solution.py:639
  19.7 1.3 %collective-permute-done.2.other = f32[8,12288]{1,0:T(8,128)S(1)} collective-permute-done((f32[8,12288]{1,0:T(8,128)S(1)}, f32[8,12288]{1,0:T(8,128)S(1)}, u32[]{:S(2)}, u32[]{:S(2)}) %collective-permute-start.2) | collective-permute-done | bytes 393248 | tf_op jit(solution)/shard_map/ppermute | solution.py:639
  21.1 0.1 collective-permute-start.5
  21.2 5.5 %lateral.1 = (f32[16,8,4096]{2,1,0:T(8,128)S(1)}, f32[16,4096]{1,0:T(8,128)S(1)}, f32[4,16,4096]{2,1,0:T(8,128)S(1)}) custom-call(f32[16,8,4224]{2,1,0:T(8,128)S(1)} %get-tuple-element.32.head_ref, f32[16,8,4224]{2,1,0:T(8,128)S(1)} %get-tuple-element.33.sigma, f32[16,8,4096]{2,1,0:T(8,128)S(1)} %get-tuple-element.34.base_in, ...), custom_call_target="tpu_custom_call" | custom-call | flops 1 | bytes 1 | tf_op jit(solution)/shard_map/lateral/pallas_call | solution.py:48
  26.8 0.0 collective-permute-done.from_above
  26.8 0.0 collective-permute-done.1.from_below
  26.8 0.3 halo.1
  27.1 1.3 %collective-permute-start.3 = (f32[8,4096]{1,0:T(8,128)S(1)}, f32[8,4096]{1,0:T(8,128)S(1)}, u32[]{:S(2)}, u32[]{:S(2)}) collective-permute-start(f32[8,4096]{1,0:T(8,128)S(1)} %get-tuple-element.45.mine), channel_id=1, source_target_pairs={{0,1},{1,0},{2,3},{3,2},{4,5},{5,4},{6,7},{7,6},{8,9},{9,8},{10,11... | collective-permute-start | bytes 393224 | tf_op jit(solution)/shard_map/ppermute | solution.py:661
  28.4 0.1 collective-permute-start.4
  28.5 0.9 %collective-permute-start.7 = (f32[8,2560]{1,0:T(8,128)S(1)}, f32[8,2560]{1,0:T(8,128)S(1)}, u32[]{:S(2)}, u32[]{:S(2)}) collective-permute-start(f32[8,2560]{1,0:T(8,128)S(1)} %get-tuple-element.53), channel_id=1, source_target_pairs={{0,2},{2,0},{1,3},{3,1},{4,6},{6,4},{5,7},{7,5},{8,10},{10,8},{9,1... | collective-permute-start | bytes 245768 | tf_op jit(solution)/shard_map/ppermute | solution.py:663
  29.4 0.0 collective-permute-done.3.other
  29.4 0.3 collective-permute-done.4.far_other
  29.7 0.1 ends.1
  29.8 1.0 %collective-permute-start.6 = (f32[8,4096]{1,0:T(8,128)S(1)}, f32[8,4096]{1,0:T(8,128)S(1)}, u32[]{:S(2)}, u32[]{:S(2)}) collective-permute-start(f32[8,4096]{1,0:T(8,128)S(1)} %get-tuple-element.50._.end_ref), channel_id=1, source_target_pairs={{0,2},{2,0},{1,3},{3,1},{4,6},{6,4},{5,7},{7,5},{8,10},{10,8},{9,1... | collective-permute-start | bytes 393224 | tf_op jit(solution)/shard_map/ppermute | solution.py:670
  30.8 1.0 %local.1.__.local_ref = f32[16,8,4096]{2,1,0:T(8,128)S(1)} custom-call(f32[2,16,4096]{2,1,0:T(8,128)S(1)} %get-tuple-element.41.flux_ref, f32[16,8,4096]{2,1,0:T(8,128)S(1)} %get-tuple-element.42.base, f32[16,8,4096]{2,1,0:T(8,128)S(1)} %get-tuple-element.43.ratio, f32[16,8,4096]{2,1,0:T(8,128)S(1)} %get-tuple-element.44.inv, ...), custom_call_target="tpu_custom_call" | custom-call | flops 1 | bytes 1 | tf_op jit(solution)/shard_map/local/pallas_call | solution.py:48
  31.8 0.0 collective-permute-done.5.chip_other.res_other
  31.8 0.3 collective-permute-done.7.from_chip
  32.1 1.8 %collective-permute-start.8 = (f32[8,3840]{1,0:T(8,128)S(1)}, f32[8,3840]{1,0:T(8,128)S(1)}, u32[]{:S(2)}, u32[]{:S(2)}) collective-permute-start(f32[8,3840]{1,0:T(8,128)S(1)} %relay.1), channel_id=1, source_target_pairs={{0,1},{1,0},{2,3},{3,2},{4,5},{5,4},{6,7},{7,6},{8,9},{9,8},{10,11... | collective-permute-start | bytes 368648 | tf_op jit(solution)/shard_map/ppermute | solution.py:677
  33.9 1.0 %collective-permute-done.8.from_core = f32[8,3840]{1,0:T(8,128)S(1)} collective-permute-done((f32[8,3840]{1,0:T(8,128)S(1)}, f32[8,3840]{1,0:T(8,128)S(1)}, u32[]{:S(2)}, u32[]{:S(2)}) %collective-permute-start.8) | collective-permute-done | bytes 122912 | tf_op jit(solution)/shard_map/ppermute | solution.py:677
  34.9 0.6 %surface.1.level_ref = f32[8,1024]{1,0:T(8,128)S(1)} custom-call(f32[3,8,1280]{2,1,0:T(8,128)S(1)} %get-tuple-element.51.own_ref, f32[8,4096]{1,0:T(8,128)S(1)} %get-tuple-element.31.exfil_ref, f32[8,4096]{1,0:T(8,128)S(1)} %get-tuple-element.52.rows_ref, f32[8,2560]{1,0:T(8,128)S(1)} %collective-permute-done.7.from_chip, ...), custom_call_target="tpu_custom_call" | custom-call | flops 1 | bytes 1 | tf_op jit(solution)/shard_map/surface/pallas_call | solution.py:48
  35.5 0.0 collective-permute-done.6.end_other
  35.5 1.5 %final.1 = (f32[16,8,4096]{2,1,0:T(8,128)}, f32[8,1024]{1,0:T(8,128)}) custom-call(f32[16,8,4096]{2,1,0:T(8,128)S(1)} %local.1.__.local_ref, f32[16,8,4096]{2,1,0:T(8,128)S(1)} %get-tuple-element.35.top_col, f32[16,8,4096]{2,1,0:T(8,128)S(1)} %get-tuple-element.36.bottom_col, f32[8,4096]{1,0:T(8,128)S(1)} %get-tuple-element.48.gap_ref, ...), custom_call_target="tpu_custom_call" | custom-call | flops 1 | bytes 1 | tf_op jit(solution)/shard_map/final/pallas_call | solution.py:48
  (2 shorter events, 0.1 us)
Async XLA Ops:
  2.6 24.2 %collective-permute-start = (f32[8,18432]{1,0:T(8,128)S(1)}, f32[8,18432]{1,0:T(8,128)S(1)}, u32[]{:S(2)}, u32[]{:S(2)}) collective-permute-start(f32[8,18432]{1,0:T(8,128)S(1)} %get-tuple-element.28.own_up), channel_id=1, source_target_pairs={{0,4},{1,5},{2,6},{3,7},{4,8},{5,9},{6,10},{7,11},{8,12},{9,13},{1... | collective-permute-start | bytes 1769480 | tf_op jit(solution)/shard_map/ppermute | solution.py:625
  5.1 21.7 %collective-permute-start.1 = (f32[8,18432]{1,0:T(8,128)S(1)}, f32[8,18432]{1,0:T(8,128)S(1)}, u32[]{:S(2)}, u32[]{:S(2)}) collective-permute-start(f32[8,18432]{1,0:T(8,128)S(1)} %get-tuple-element.29.own_down), channel_id=1, source_target_pairs={{4,0},{5,1},{6,2},{7,3},{8,4},{9,5},{10,6},{11,7},{12,8},{13,9},{1... | collective-permute-start | bytes 1769480 | tf_op jit(solution)/shard_map/ppermute | solution.py:626
  18.7 2.4 %collective-permute-start.2 = (f32[8,12288]{1,0:T(8,128)S(1)}, f32[8,12288]{1,0:T(8,128)S(1)}, u32[]{:S(2)}, u32[]{:S(2)}) collective-permute-start(f32[8,12288]{1,0:T(8,128)S(1)} %get-tuple-element.37.mine), channel_id=1, source_target_pairs={{0,1},{1,0},{2,3},{3,2},{4,5},{5,4},{6,7},{7,6},{8,9},{9,8},{10,11... | collective-permute-start | bytes 1179656 | tf_op jit(solution)/shard_map/ppermute | solution.py:639
  21.1 10.6 %collective-permute-start.5 = (f32[8,6656]{1,0:T(8,128)S(1)}, f32[8,6656]{1,0:T(8,128)S(1)}, u32[]{:S(2)}, u32[]{:S(2)}) collective-permute-start(f32[8,6656]{1,0:T(8,128)S(1)} %get-tuple-element.49.res_ref), channel_id=1, source_target_pairs={{0,2},{2,0},{1,3},{3,1},{4,6},{6,4},{5,7},{7,5},{8,10},{10,8},{9,1... | collective-permute-start | bytes 638984 | tf_op jit(solution)/shard_map/ppermute | solution.py:646
  27.1 2.3 %collective-permute-start.3 = (f32[8,4096]{1,0:T(8,128)S(1)}, f32[8,4096]{1,0:T(8,128)S(1)}, u32[]{:S(2)}, u32[]{:S(2)}) collective-permute-start(f32[8,4096]{1,0:T(8,128)S(1)} %get-tuple-element.45.mine), channel_id=1, source_target_pairs={{0,1},{1,0},{2,3},{3,2},{4,5},{5,4},{6,7},{7,6},{8,9},{9,8},{10,11... | collective-permute-start | bytes 393224 | tf_op jit(solution)/shard_map/ppermute | solution.py:661
  28.4 1.3 %collective-permute-start.4 = (f32[8,4096]{1,0:T(8,128)S(1)}, f32[8,4096]{1,0:T(8,128)S(1)}, u32[]{:S(2)}, u32[]{:S(2)}) collective-permute-start(f32[8,4096]{1,0:T(8,128)S(1)} %get-tuple-element.46.far_mine), channel_id=1, source_target_pairs={{0,1},{1,0},{2,3},{3,2},{4,5},{5,4},{6,7},{7,6},{8,9},{9,8},{10,11... | collective-permute-start | bytes 393224 | tf_op jit(solution)/shard_map/ppermute | solution.py:662
  28.5 3.6 %collective-permute-start.7 = (f32[8,2560]{1,0:T(8,128)S(1)}, f32[8,2560]{1,0:T(8,128)S(1)}, u32[]{:S(2)}, u32[]{:S(2)}) collective-permute-start(f32[8,2560]{1,0:T(8,128)S(1)} %get-tuple-element.53), channel_id=1, source_target_pairs={{0,2},{2,0},{1,3},{3,1},{4,6},{6,4},{5,7},{7,5},{8,10},{10,8},{9,1... | collective-permute-start | bytes 245768 | tf_op jit(solution)/shard_map/ppermute | solution.py:663
  29.8 5.7 %collective-permute-start.6 = (f32[8,4096]{1,0:T(8,128)S(1)}, f32[8,4096]{1,0:T(8,128)S(1)}, u32[]{:S(2)}, u32[]{:S(2)}) collective-permute-start(f32[8,4096]{1,0:T(8,128)S(1)} %get-tuple-element.50._.end_ref), channel_id=1, source_target_pairs={{0,2},{2,0},{1,3},{3,1},{4,6},{6,4},{5,7},{7,5},{8,10},{10,8},{9,1... | collective-permute-start | bytes 393224 | tf_op jit(solution)/shard_map/ppermute | solution.py:670
  32.1 2.7 %collective-permute-start.8 = (f32[8,3840]{1,0:T(8,128)S(1)}, f32[8,3840]{1,0:T(8,128)S(1)}, u32[]{:S(2)}, u32[]{:S(2)}) collective-permute-start(f32[8,3840]{1,0:T(8,128)S(1)} %relay.1), channel_id=1, source_target_pairs={{0,1},{1,0},{2,3},{3,2},{4,5},{5,4},{6,7},{7,6},{8,9},{9,8},{10,11... | collective-permute-start | bytes 368648 | tf_op jit(solution)/shard_map/ppermute | solution.py:677

commit v6 on v5

--- a/solution.py
+++ b/solution.py
@@ -22,7 +22,7 @@
 ROWS = 8
 CHUNK = 512
 HALO_CHUNK = 1024
-AHEAD = 3
+AHEAD = 5
 VMEM_LIMIT = 8 * 1024 * 1024
 
 VMEM = pl.BlockSpec(memory_space=pltpu.VMEM)
@@ -280,16 +280,9 @@
 
 
 def lateral_kernel(
-    head_ref, sigma, base_in, top_col, bottom_col, _, base, sums_ref, rows_ref, carried, sem,
+    head_ref, sigma, base_in, top_col, bottom_col, _, base, sums_ref, rows_ref, carried,
 ):
     nz, _, width = base.shape
-    copies = [
-        pltpu.make_async_copy(array.at[:, row, :], rows_ref.at[2 * place + side], sem.at[2 * place + side])
-        for place, array in enumerate((top_col, bottom_col))
-        for side, row in enumerate((ROWS - 1, 0))
-    ]
-    for copy in copies:
-        copy.start()
     sublane = lax.broadcasted_iota(jnp.int32, (ROWS, CHUNK), 0)
     inner = sublane < ROWS - 1
     lane = lax.broadcasted_iota(jnp.int32, (ROWS, LANES), 1)
@@ -335,15 +328,15 @@
             flux_x = jnp.where(inner, flux_x, 0.0)
             b = base_in[z, :, lanes] + (flux_y - flux_left) + (flux_x - pltpu.roll(flux_x, 1, 0))
             base[z, :, lanes] = b
-            first = top_col[z, :, lanes] * b
-            last = bottom_col[z, :, lanes] * b
+            ends = (top_col[z, :, lanes], bottom_col[z, :, lanes])
+            for place, end in enumerate(ends):
+                rows_ref[2 * place, pl.ds(z, 1), lanes] = end[ROWS - 1 :]
+                rows_ref[2 * place + 1, pl.ds(z, 1), lanes] = end[:1]
+            first, last = (end * b for end in ends)
             top_sum = first if z == 0 else top_sum + first
             bottom_sum = last if z == 0 else bottom_sum + last
         sums_ref[pl.ds(0, ROWS), lanes] = top_sum + head_ref[0, :, lanes]
         sums_ref[pl.ds(ROWS, ROWS), lanes] = bottom_sum + head_ref[nz - 1, :, lanes]
-
-    for copy in copies:
-        copy.wait()
 
 
 def pair_kernel(mine, other, exfil_ref, pair_inv_ref, gain_ref, sent_ref):
@@ -650,7 +643,7 @@
         "lateral",
         [in_vmem(x) for x in (head_v, sigma, base, top_col, bottom_col, gain)],
         [block, f32(2 * rows, width), f32(4, nz, width)],
-        scratch=[pltpu.VMEM((3, nz, rows, LANES), jnp.float32), pltpu.SemaphoreType.DMA((4,))],
+        scratch=[pltpu.VMEM((3, nz, rows, LANES), jnp.float32)],
     )
     flux, ends, far_ends, field_rows, windows = call(
         halo_kernel,

time: 37.1 us -> 37.1 us (level)
  waiting for transfers between devices: 2.98 us -> 5.14 us
  starting transfers between devices: 17.4 us -> 16 us
  Pallas kernels: 15.8 us -> 15.1 us
    pallas_call x10, Pallas kernels: 15.8 us -> 15.1 us  [call(): pl.pallas_call(kernel, out_shape=out_shape, in_specs=[spec for spec, _ in...]
    ppermute x1, starting transfers between devices: 0.93 us -> 0.18 us  [per_device(): windows_chip = lax.ppermute(windows, 'depth', chip)]
    ppermute x1, waiting for transfers between devices: 0.01 us -> 0.73 us  [per_device(): from_above = lax.ppermute(own_up, ('lat', 'depth'), up)]
    ppermute x1, waiting for transfers between devices: 0.32 us -> 1.02 us  [per_device(): windows_chip = lax.ppermute(windows, 'depth', chip)]
    ppermute x1, starting transfers between devices: 1.01 us -> 0.31 us  [per_device(): chip_end_other = lax.ppermute(chip_end, 'depth', chip)]
    ppermute x1, waiting for transfers between devices: 0.01 us -> 0.7 us  [per_device(): near_other = lax.ppermute(ends, 'depth', core)]
  transfers between devices with their start and end apart: 9 -> 9, of which waited for: 4 -> 6; matrix products, arithmetic and copies ran while one was open for 0% -> 0% of each run, Pallas kernels for 34% -> 32%
where the time goes in v6:
time: 37.1 us; the launch traced here: 36.9 us
  starting transfers between devices  16 us (43%)
  Pallas kernels  15.1 us (41%)
  waiting for transfers between devices  5.14 us (14%)
  between operations  0.71 us (2%)
    pallas_call x10, Pallas kernels, call(): pl.pallas_call(kernel, out_shape=out_shape, in_specs=[spec for spec, _ in...  15.1 us
    ppermute x1, starting transfers between devices, per_device(): from_below = lax.ppermute(own_down, ('lat', 'depth'), down)  8.67 us
    ppermute x1, starting transfers between devices, per_device(): from_above = lax.ppermute(own_up, ('lat', 'depth'), up)  2.54 us
    ppermute x1, starting transfers between devices, per_device(): windows_core = lax.ppermute(relayed, 'depth', core)  1.76 us
    ppermute x1, waiting for transfers between devices, per_device(): resist_other = lax.ppermute(resist, 'depth', core)  1.35 us
    ppermute x1, starting transfers between devices, per_device(): near_other = lax.ppermute(ends, 'depth', core)  1.32 us
    ppermute x1, starting transfers between devices, per_device(): resist_other = lax.ppermute(resist, 'depth', core)  1.04 us
    ppermute x1, waiting for transfers between devices, per_device(): windows_chip = lax.ppermute(windows, 'depth', chip)  1.02 us
  transfers between devices with their start and end apart: 9, of which 6 were waited for; matrix products, arithmetic and copies ran while one was open for 0% of the time, Pallas kernels for 32%

profile of v6, /device:TPU:1, one launch (start us, length us, event | category | flops | bytes accessed | tf_op | source)
XLA Modules:
  0.0 36.9 jit_solution(872631502317655639)
XLA Ops:
  0.6 1.9 %pack.1 = (f32[8,18432]{1,0:T(8,128)S(1)}, f32[8,18432]{1,0:T(8,128)S(1)}, f32[6,8,128]{2,1,0:T(8,128)S(1)}, f32[8,4096]{1,0:T(8,128)S(1)}, f32[3,8,1280]{2,1,0:T(8,128)S(1)}) custom-call(f32[12]{0:T(128)} %cond_ref.1, f32[12]{0:T(128)} %shape_ref.1, f32[12]{0:T(128)} %pore_ref.1, f32[16,8,4096]{2,1,0:T(8,128)} %head_hbm.1, s32[16,8,4096]{2,1,0:T(8,128)} %soil_hbm.1, ...), custom_call_target="tpu_custom_call" | custom-call | flops 1 | bytes 1 | tf_op jit(solution)/shard_map/pack/pallas_call | solution.py:48
  2.6 2.5 %collective-permute-start = (f32[8,18432]{1,0:T(8,128)S(1)}, f32[8,18432]{1,0:T(8,128)S(1)}, u32[]{:S(2)}, u32[]{:S(2)}) collective-permute-start(f32[8,18432]{1,0:T(8,128)S(1)} %get-tuple-element.28.own_up), channel_id=1, source_target_pairs={{0,4},{1,5},{2,6},{3,7},{4,8},{5,9},{6,10},{7,11},{8,12},{9,13},{1... | collective-permute-start | bytes 1769480 | tf_op jit(solution)/shard_map/ppermute | solution.py:618
  5.1 8.7 %collective-permute-start.1 = (f32[8,18432]{1,0:T(8,128)S(1)}, f32[8,18432]{1,0:T(8,128)S(1)}, u32[]{:S(2)}, u32[]{:S(2)}) collective-permute-start(f32[8,18432]{1,0:T(8,128)S(1)} %get-tuple-element.29.own_down), channel_id=1, source_target_pairs={{4,0},{5,1},{6,2},{7,3},{8,4},{9,5},{10,6},{11,7},{12,8},{13,9},{1... | collective-permute-start | bytes 1769480 | tf_op jit(solution)/shard_map/ppermute | solution.py:619
  13.8 4.9 %factor.1 = (f32[16,8,4224]{2,1,0:T(8,128)S(1)}, f32[16,8,4224]{2,1,0:T(8,128)S(1)}, f32[16,8,4096]{2,1,0:T(8,128)S(1)}, f32[16,8,4096]{2,1,0:T(8,128)S(1)}, f32...) custom-call(f32[6,8,128]{2,1,0:T(8,128)S(1)} %get-tuple-element.30.ta, ...), custom_call_target="tpu_custom_call" | custom-call | flops 1 | bytes 1 | tf_op jit(solution)/shard_map/factor/pallas_call | solution.py:48
  18.7 1.0 %collective-permute-start.2 = (f32[8,12288]{1,0:T(8,128)S(1)}, f32[8,12288]{1,0:T(8,128)S(1)}, u32[]{:S(2)}, u32[]{:S(2)}) collective-permute-start(f32[8,12288]{1,0:T(8,128)S(1)} %get-tuple-element.37.mine), channel_id=1, source_target_pairs={{0,1},{1,0},{2,3},{3,2},{4,5},{5,4},{6,7},{7,6},{8,9},{9,8},{10,11... | collective-permute-start | bytes 1179656 | tf_op jit(solution)/shard_map/ppermute | solution.py:632
  19.7 1.3 %collective-permute-done.2.other = f32[8,12288]{1,0:T(8,128)S(1)} collective-permute-done((f32[8,12288]{1,0:T(8,128)S(1)}, f32[8,12288]{1,0:T(8,128)S(1)}, u32[]{:S(2)}, u32[]{:S(2)}) %collective-permute-start.2) | collective-permute-done | bytes 393248 | tf_op jit(solution)/shard_map/ppermute | solution.py:632
  21.1 0.1 collective-permute-start.5
  21.2 4.8 %lateral.1 = (f32[16,8,4096]{2,1,0:T(8,128)S(1)}, f32[16,4096]{1,0:T(8,128)S(1)}, f32[4,16,4096]{2,1,0:T(8,128)S(1)}) custom-call(f32[16,8,4224]{2,1,0:T(8,128)S(1)} %get-tuple-element.32.head_ref, f32[16,8,4224]{2,1,0:T(8,128)S(1)} %get-tuple-element.33.sigma, f32[16,8,4096]{2,1,0:T(8,128)S(1)} %get-tuple-element.34.base_in, ...), custom_call_target="tpu_custom_call" | custom-call | flops 1 | bytes 1 | tf_op jit(solution)/shard_map/lateral/pallas_call | solution.py:48
  26.0 0.7 %collective-permute-done.from_above = f32[8,18432]{1,0:T(8,128)S(1)} collective-permute-done((f32[8,18432]{1,0:T(8,128)S(1)}, f32[8,18432]{1,0:T(8,128)S(1)}, u32[]{:S(2)}, u32[]{:S(2)}) %collective-permute-start) | collective-permute-done | bytes 589856 | tf_op jit(solution)/shard_map/ppermute | solution.py:618
  26.7 0.0 collective-permute-done.1.from_below
  26.7 0.3 halo.1
  27.1 1.3 %collective-permute-start.3 = (f32[8,4096]{1,0:T(8,128)S(1)}, f32[8,4096]{1,0:T(8,128)S(1)}, u32[]{:S(2)}, u32[]{:S(2)}) collective-permute-start(f32[8,4096]{1,0:T(8,128)S(1)} %get-tuple-element.45.mine), channel_id=1, source_target_pairs={{0,1},{1,0},{2,3},{3,2},{4,5},{5,4},{6,7},{7,6},{8,9},{9,8},{10,11... | collective-permute-start | bytes 393224 | tf_op jit(solution)/shard_map/ppermute | solution.py:654
  28.4 0.1 collective-permute-start.4
  28.5 0.2 collective-permute-start.7
  28.7 0.7 %collective-permute-done.3.other = f32[8,4096]{1,0:T(8,128)S(1)} collective-permute-done((f32[8,4096]{1,0:T(8,128)S(1)}, f32[8,4096]{1,0:T(8,128)S(1)}, u32[]{:S(2)}, u32[]{:S(2)}) %collective-permute-start.3) | collective-permute-done | bytes 131104 | tf_op jit(solution)/shard_map/ppermute | solution.py:654
  29.4 0.4 collective-permute-done.4.far_other
  29.7 0.1 ends.1
  29.8 0.3 collective-permute-start.6
  30.1 1.0 %local.1.__.local_ref = f32[16,8,4096]{2,1,0:T(8,128)S(1)} custom-call(f32[2,16,4096]{2,1,0:T(8,128)S(1)} %get-tuple-element.41.flux_ref, f32[16,8,4096]{2,1,0:T(8,128)S(1)} %get-tuple-element.42.base, f32[16,8,4096]{2,1,0:T(8,128)S(1)} %get-tuple-element.43.ratio, f32[16,8,4096]{2,1,0:T(8,128)S(1)} %get-tuple-element.44.inv, ...), custom_call_target="tpu_custom_call" | custom-call | flops 1 | bytes 1 | tf_op jit(solution)/shard_map/local/pallas_call | solution.py:48
  31.1 0.0 collective-permute-done.5.chip_other.res_other
  31.1 1.0 %collective-permute-done.7.from_chip = f32[8,2560]{1,0:T(8,128)S(1)} collective-permute-done((f32[8,2560]{1,0:T(8,128)S(1)}, f32[8,2560]{1,0:T(8,128)S(1)}, u32[]{:S(2)}, u32[]{:S(2)}) %collective-permute-start.7) | collective-permute-done | bytes 81952 | tf_op jit(solution)/shard_map/ppermute | solution.py:656
  32.1 1.8 %collective-permute-start.8 = (f32[8,3840]{1,0:T(8,128)S(1)}, f32[8,3840]{1,0:T(8,128)S(1)}, u32[]{:S(2)}, u32[]{:S(2)}) collective-permute-start(f32[8,3840]{1,0:T(8,128)S(1)} %relay.1), channel_id=1, source_target_pairs={{0,1},{1,0},{2,3},{3,2},{4,5},{5,4},{6,7},{7,6},{8,9},{9,8},{10,11... | collective-permute-start | bytes 368648 | tf_op jit(solution)/shard_map/ppermute | solution.py:670
  33.9 1.0 %collective-permute-done.8.from_core = f32[8,3840]{1,0:T(8,128)S(1)} collective-permute-done((f32[8,3840]{1,0:T(8,128)S(1)}, f32[8,3840]{1,0:T(8,128)S(1)}, u32[]{:S(2)}, u32[]{:S(2)}) %collective-permute-start.8) | collective-permute-done | bytes 122912 | tf_op jit(solution)/shard_map/ppermute | solution.py:670
  34.9 0.6 %surface.1.level_ref = f32[8,1024]{1,0:T(8,128)S(1)} custom-call(f32[3,8,1280]{2,1,0:T(8,128)S(1)} %get-tuple-element.51.own_ref, f32[8,4096]{1,0:T(8,128)S(1)} %get-tuple-element.31.exfil_ref, f32[8,4096]{1,0:T(8,128)S(1)} %get-tuple-element.52.rows_ref, f32[8,2560]{1,0:T(8,128)S(1)} %collective-permute-done.7.from_chip, ...), custom_call_target="tpu_custom_call" | custom-call | flops 1 | bytes 1 | tf_op jit(solution)/shard_map/surface/pallas_call | solution.py:48
  35.5 0.0 collective-permute-done.6.end_other
  35.5 1.5 %final.1 = (f32[16,8,4096]{2,1,0:T(8,128)}, f32[8,1024]{1,0:T(8,128)}) custom-call(f32[16,8,4096]{2,1,0:T(8,128)S(1)} %local.1.__.local_ref, f32[16,8,4096]{2,1,0:T(8,128)S(1)} %get-tuple-element.35.top_col, f32[16,8,4096]{2,1,0:T(8,128)S(1)} %get-tuple-element.36.bottom_col, f32[8,4096]{1,0:T(8,128)S(1)} %get-tuple-element.48.gap_ref, ...), custom_call_target="tpu_custom_call" | custom-call | flops 1 | bytes 1 | tf_op jit(solution)/shard_map/final/pallas_call | solution.py:48
  (2 shorter events, 0.1 us)
Async XLA Ops:
  2.6 24.2 %collective-permute-start = (f32[8,18432]{1,0:T(8,128)S(1)}, f32[8,18432]{1,0:T(8,128)S(1)}, u32[]{:S(2)}, u32[]{:S(2)}) collective-permute-start(f32[8,18432]{1,0:T(8,128)S(1)} %get-tuple-element.28.own_up), channel_id=1, source_target_pairs={{0,4},{1,5},{2,6},{3,7},{4,8},{5,9},{6,10},{7,11},{8,12},{9,13},{1... | collective-permute-start | bytes 1769480 | tf_op jit(solution)/shard_map/ppermute | solution.py:618
  5.1 21.6 %collective-permute-start.1 = (f32[8,18432]{1,0:T(8,128)S(1)}, f32[8,18432]{1,0:T(8,128)S(1)}, u32[]{:S(2)}, u32[]{:S(2)}) collective-permute-start(f32[8,18432]{1,0:T(8,128)S(1)} %get-tuple-element.29.own_down), channel_id=1, source_target_pairs={{4,0},{5,1},{6,2},{7,3},{8,4},{9,5},{10,6},{11,7},{12,8},{13,9},{1... | collective-permute-start | bytes 1769480 | tf_op jit(solution)/shard_map/ppermute | solution.py:619
  18.7 2.4 %collective-permute-start.2 = (f32[8,12288]{1,0:T(8,128)S(1)}, f32[8,12288]{1,0:T(8,128)S(1)}, u32[]{:S(2)}, u32[]{:S(2)}) collective-permute-start(f32[8,12288]{1,0:T(8,128)S(1)} %get-tuple-element.37.mine), channel_id=1, source_target_pairs={{0,1},{1,0},{2,3},{3,2},{4,5},{5,4},{6,7},{7,6},{8,9},{9,8},{10,11... | collective-permute-start | bytes 1179656 | tf_op jit(solution)/shard_map/ppermute | solution.py:632
  21.1 9.9 %collective-permute-start.5 = (f32[8,6656]{1,0:T(8,128)S(1)}, f32[8,6656]{1,0:T(8,128)S(1)}, u32[]{:S(2)}, u32[]{:S(2)}) collective-permute-start(f32[8,6656]{1,0:T(8,128)S(1)} %get-tuple-element.49.res_ref), channel_id=1, source_target_pairs={{0,2},{2,0},{1,3},{3,1},{4,6},{6,4},{5,7},{7,5},{8,10},{10,8},{9,1... | collective-permute-start | bytes 638984 | tf_op jit(solution)/shard_map/ppermute | solution.py:639
  27.1 2.3 %collective-permute-start.3 = (f32[8,4096]{1,0:T(8,128)S(1)}, f32[8,4096]{1,0:T(8,128)S(1)}, u32[]{:S(2)}, u32[]{:S(2)}) collective-permute-start(f32[8,4096]{1,0:T(8,128)S(1)} %get-tuple-element.45.mine), channel_id=1, source_target_pairs={{0,1},{1,0},{2,3},{3,2},{4,5},{5,4},{6,7},{7,6},{8,9},{9,8},{10,11... | collective-permute-start | bytes 393224 | tf_op jit(solution)/shard_map/ppermute | solution.py:654
  28.4 1.3 %collective-permute-start.4 = (f32[8,4096]{1,0:T(8,128)S(1)}, f32[8,4096]{1,0:T(8,128)S(1)}, u32[]{:S(2)}, u32[]{:S(2)}) collective-permute-start(f32[8,4096]{1,0:T(8,128)S(1)} %get-tuple-element.46.far_mine), channel_id=1, source_target_pairs={{0,1},{1,0},{2,3},{3,2},{4,5},{5,4},{6,7},{7,6},{8,9},{9,8},{10,11... | collective-permute-start | bytes 393224 | tf_op jit(solution)/shard_map/ppermute | solution.py:655
  28.5 3.6 %collective-permute-start.7 = (f32[8,2560]{1,0:T(8,128)S(1)}, f32[8,2560]{1,0:T(8,128)S(1)}, u32[]{:S(2)}, u32[]{:S(2)}) collective-permute-start(f32[8,2560]{1,0:T(8,128)S(1)} %get-tuple-element.53), channel_id=1, source_target_pairs={{0,2},{2,0},{1,3},{3,1},{4,6},{6,4},{5,7},{7,5},{8,10},{10,8},{9,1... | collective-permute-start | bytes 245768 | tf_op jit(solution)/shard_map/ppermute | solution.py:656
  29.8 5.7 %collective-permute-start.6 = (f32[8,4096]{1,0:T(8,128)S(1)}, f32[8,4096]{1,0:T(8,128)S(1)}, u32[]{:S(2)}, u32[]{:S(2)}) collective-permute-start(f32[8,4096]{1,0:T(8,128)S(1)} %get-tuple-element.50._.end_ref), channel_id=1, source_target_pairs={{0,2},{2,0},{1,3},{3,1},{4,6},{6,4},{5,7},{7,5},{8,10},{10,8},{9,1... | collective-permute-start | bytes 393224 | tf_op jit(solution)/shard_map/ppermute | solution.py:663
  32.1 2.7 %collective-permute-start.8 = (f32[8,3840]{1,0:T(8,128)S(1)}, f32[8,3840]{1,0:T(8,128)S(1)}, u32[]{:S(2)}, u32[]{:S(2)}) collective-permute-start(f32[8,3840]{1,0:T(8,128)S(1)} %relay.1), channel_id=1, source_target_pairs={{0,1},{1,0},{2,3},{3,2},{4,5},{5,4},{6,7},{7,6},{8,9},{9,8},{10,11... | collective-permute-start | bytes 368648 | tf_op jit(solution)/shard_map/ppermute | solution.py:670

commit v7 on v6

--- a/solution.py
+++ b/solution.py
@@ -21,7 +21,7 @@
 LANES = 128
 ROWS = 8
 CHUNK = 512
-HALO_CHUNK = 1024
+HALO_CHUNK = 2048
 AHEAD = 5
 VMEM_LIMIT = 8 * 1024 * 1024
 

time: 37.1 us -> 37 us (level)
  no operation moved by 1% of the time
where the time goes in v7:
time: 37 us; the launch traced here: 36.9 us
  starting transfers between devices  16 us (43%)
  Pallas kernels  15.1 us (41%)
  waiting for transfers between devices  5.14 us (14%)
  between operations  0.71 us (2%)
    pallas_call x10, Pallas kernels, call(): pl.pallas_call(kernel, out_shape=out_shape, in_specs=[spec for spec, _ in...  15.1 us
    ppermute x1, starting transfers between devices, per_device(): from_below = lax.ppermute(own_down, ('lat', 'depth'), down)  8.67 us
    ppermute x1, starting transfers between devices, per_device(): from_above = lax.ppermute(own_up, ('lat', 'depth'), up)  2.54 us
    ppermute x1, starting transfers between devices, per_device(): windows_core = lax.ppermute(relayed, 'depth', core)  1.76 us
    ppermute x1, waiting for transfers between devices, per_device(): resist_other = lax.ppermute(resist, 'depth', core)  1.35 us
    ppermute x1, starting transfers between devices, per_device(): near_other = lax.ppermute(ends, 'depth', core)  1.32 us
    ppermute x1, starting transfers between devices, per_device(): resist_other = lax.ppermute(resist, 'depth', core)  1.04 us
    ppermute x1, waiting for transfers between devices, per_device(): windows_chip = lax.ppermute(windows, 'depth', chip)  1.02 us
  transfers between devices with their start and end apart: 9, of which 6 were waited for; matrix products, arithmetic and copies ran while one was open for 0% of the time, Pallas kernels for 32%

profile of v7, /device:TPU:1, one launch (start us, length us, event | category | flops | bytes accessed | tf_op | source)
XLA Modules:
  0.0 36.9 jit_solution(13431492640160360186)
XLA Ops:
  0.6 1.9 %pack.1 = (f32[8,18432]{1,0:T(8,128)S(1)}, f32[8,18432]{1,0:T(8,128)S(1)}, f32[6,8,128]{2,1,0:T(8,128)S(1)}, f32[8,4096]{1,0:T(8,128)S(1)}, f32[3,8,1280]{2,1,0:T(8,128)S(1)}) custom-call(f32[12]{0:T(128)} %cond_ref.1, f32[12]{0:T(128)} %shape_ref.1, f32[12]{0:T(128)} %pore_ref.1, f32[16,8,4096]{2,1,0:T(8,128)} %head_hbm.1, s32[16,8,4096]{2,1,0:T(8,128)} %soil_hbm.1, ...), custom_call_target="tpu_custom_call" | custom-call | flops 1 | bytes 1 | tf_op jit(solution)/shard_map/pack/pallas_call | solution.py:48
  2.6 2.5 %collective-permute-start = (f32[8,18432]{1,0:T(8,128)S(1)}, f32[8,18432]{1,0:T(8,128)S(1)}, u32[]{:S(2)}, u32[]{:S(2)}) collective-permute-start(f32[8,18432]{1,0:T(8,128)S(1)} %get-tuple-element.28.own_up), channel_id=1, source_target_pairs={{0,4},{1,5},{2,6},{3,7},{4,8},{5,9},{6,10},{7,11},{8,12},{9,13},{1... | collective-permute-start | bytes 1769480 | tf_op jit(solution)/shard_map/ppermute | solution.py:618
  5.1 8.7 %collective-permute-start.1 = (f32[8,18432]{1,0:T(8,128)S(1)}, f32[8,18432]{1,0:T(8,128)S(1)}, u32[]{:S(2)}, u32[]{:S(2)}) collective-permute-start(f32[8,18432]{1,0:T(8,128)S(1)} %get-tuple-element.29.own_down), channel_id=1, source_target_pairs={{4,0},{5,1},{6,2},{7,3},{8,4},{9,5},{10,6},{11,7},{12,8},{13,9},{1... | collective-permute-start | bytes 1769480 | tf_op jit(solution)/shard_map/ppermute | solution.py:619
  13.8 4.9 %factor.1 = (f32[16,8,4224]{2,1,0:T(8,128)S(1)}, f32[16,8,4224]{2,1,0:T(8,128)S(1)}, f32[16,8,4096]{2,1,0:T(8,128)S(1)}, f32[16,8,4096]{2,1,0:T(8,128)S(1)}, f32...) custom-call(f32[6,8,128]{2,1,0:T(8,128)S(1)} %get-tuple-element.30.ta, ...), custom_call_target="tpu_custom_call" | custom-call | flops 1 | bytes 1 | tf_op jit(solution)/shard_map/factor/pallas_call | solution.py:48
  18.7 1.0 %collective-permute-start.2 = (f32[8,12288]{1,0:T(8,128)S(1)}, f32[8,12288]{1,0:T(8,128)S(1)}, u32[]{:S(2)}, u32[]{:S(2)}) collective-permute-start(f32[8,12288]{1,0:T(8,128)S(1)} %get-tuple-element.37.mine), channel_id=1, source_target_pairs={{0,1},{1,0},{2,3},{3,2},{4,5},{5,4},{6,7},{7,6},{8,9},{9,8},{10,11... | collective-permute-start | bytes 1179656 | tf_op jit(solution)/shard_map/ppermute | solution.py:632
  19.7 1.3 %collective-permute-done.2.other = f32[8,12288]{1,0:T(8,128)S(1)} collective-permute-done((f32[8,12288]{1,0:T(8,128)S(1)}, f32[8,12288]{1,0:T(8,128)S(1)}, u32[]{:S(2)}, u32[]{:S(2)}) %collective-permute-start.2) | collective-permute-done | bytes 393248 | tf_op jit(solution)/shard_map/ppermute | solution.py:632
  21.1 0.1 collective-permute-start.5
  21.2 4.8 %lateral.1 = (f32[16,8,4096]{2,1,0:T(8,128)S(1)}, f32[16,4096]{1,0:T(8,128)S(1)}, f32[4,16,4096]{2,1,0:T(8,128)S(1)}) custom-call(f32[16,8,4224]{2,1,0:T(8,128)S(1)} %get-tuple-element.32.head_ref, f32[16,8,4224]{2,1,0:T(8,128)S(1)} %get-tuple-element.33.sigma, f32[16,8,4096]{2,1,0:T(8,128)S(1)} %get-tuple-element.34.base_in, ...), custom_call_target="tpu_custom_call" | custom-call | flops 1 | bytes 1 | tf_op jit(solution)/shard_map/lateral/pallas_call | solution.py:48
  26.0 0.7 %collective-permute-done.from_above = f32[8,18432]{1,0:T(8,128)S(1)} collective-permute-done((f32[8,18432]{1,0:T(8,128)S(1)}, f32[8,18432]{1,0:T(8,128)S(1)}, u32[]{:S(2)}, u32[]{:S(2)}) %collective-permute-start) | collective-permute-done | bytes 589856 | tf_op jit(solution)/shard_map/ppermute | solution.py:618
  26.7 0.0 collective-permute-done.1.from_below
  26.7 0.3 halo.1
  27.1 1.3 %collective-permute-start.3 = (f32[8,4096]{1,0:T(8,128)S(1)}, f32[8,4096]{1,0:T(8,128)S(1)}, u32[]{:S(2)}, u32[]{:S(2)}) collective-permute-start(f32[8,4096]{1,0:T(8,128)S(1)} %get-tuple-element.45.mine), channel_id=1, source_target_pairs={{0,1},{1,0},{2,3},{3,2},{4,5},{5,4},{6,7},{7,6},{8,9},{9,8},{10,11... | collective-permute-start | bytes 393224 | tf_op jit(solution)/shard_map/ppermute | solution.py:654
  28.4 0.1 collective-permute-start.4
  28.5 0.2 collective-permute-start.7
  28.7 0.7 %collective-permute-done.3.other = f32[8,4096]{1,0:T(8,128)S(1)} collective-permute-done((f32[8,4096]{1,0:T(8,128)S(1)}, f32[8,4096]{1,0:T(8,128)S(1)}, u32[]{:S(2)}, u32[]{:S(2)}) %collective-permute-start.3) | collective-permute-done | bytes 131104 | tf_op jit(solution)/shard_map/ppermute | solution.py:654
  29.4 0.4 collective-permute-done.4.far_other
  29.7 0.1 ends.1
  29.8 0.3 collective-permute-start.6
  30.1 1.0 %local.1.__.local_ref = f32[16,8,4096]{2,1,0:T(8,128)S(1)} custom-call(f32[2,16,4096]{2,1,0:T(8,128)S(1)} %get-tuple-element.41.flux_ref, f32[16,8,4096]{2,1,0:T(8,128)S(1)} %get-tuple-element.42.base, f32[16,8,4096]{2,1,0:T(8,128)S(1)} %get-tuple-element.43.ratio, f32[16,8,4096]{2,1,0:T(8,128)S(1)} %get-tuple-element.44.inv, ...), custom_call_target="tpu_custom_call" | custom-call | flops 1 | bytes 1 | tf_op jit(solution)/shard_map/local/pallas_call | solution.py:48
  31.1 0.0 collective-permute-done.5.chip_other.res_other
  31.1 1.0 %collective-permute-done.7.from_chip = f32[8,2560]{1,0:T(8,128)S(1)} collective-permute-done((f32[8,2560]{1,0:T(8,128)S(1)}, f32[8,2560]{1,0:T(8,128)S(1)}, u32[]{:S(2)}, u32[]{:S(2)}) %collective-permute-start.7) | collective-permute-done | bytes 81952 | tf_op jit(solution)/shard_map/ppermute | solution.py:656
  32.1 1.8 %collective-permute-start.8 = (f32[8,3840]{1,0:T(8,128)S(1)}, f32[8,3840]{1,0:T(8,128)S(1)}, u32[]{:S(2)}, u32[]{:S(2)}) collective-permute-start(f32[8,3840]{1,0:T(8,128)S(1)} %relay.1), channel_id=1, source_target_pairs={{0,1},{1,0},{2,3},{3,2},{4,5},{5,4},{6,7},{7,6},{8,9},{9,8},{10,11... | collective-permute-start | bytes 368648 | tf_op jit(solution)/shard_map/ppermute | solution.py:670
  33.9 1.0 %collective-permute-done.8.from_core = f32[8,3840]{1,0:T(8,128)S(1)} collective-permute-done((f32[8,3840]{1,0:T(8,128)S(1)}, f32[8,3840]{1,0:T(8,128)S(1)}, u32[]{:S(2)}, u32[]{:S(2)}) %collective-permute-start.8) | collective-permute-done | bytes 122912 | tf_op jit(solution)/shard_map/ppermute | solution.py:670
  34.8 0.6 %surface.1.level_ref = f32[8,1024]{1,0:T(8,128)S(1)} custom-call(f32[3,8,1280]{2,1,0:T(8,128)S(1)} %get-tuple-element.51.own_ref, f32[8,4096]{1,0:T(8,128)S(1)} %get-tuple-element.31.exfil_ref, f32[8,4096]{1,0:T(8,128)S(1)} %get-tuple-element.52.rows_ref, f32[8,2560]{1,0:T(8,128)S(1)} %collective-permute-done.7.from_chip, ...), custom_call_target="tpu_custom_call" | custom-call | flops 1 | bytes 1 | tf_op jit(solution)/shard_map/surface/pallas_call | solution.py:48
  35.5 0.0 collective-permute-done.6.end_other
  35.5 1.5 %final.1 = (f32[16,8,4096]{2,1,0:T(8,128)}, f32[8,1024]{1,0:T(8,128)}) custom-call(f32[16,8,4096]{2,1,0:T(8,128)S(1)} %local.1.__.local_ref, f32[16,8,4096]{2,1,0:T(8,128)S(1)} %get-tuple-element.35.top_col, f32[16,8,4096]{2,1,0:T(8,128)S(1)} %get-tuple-element.36.bottom_col, f32[8,4096]{1,0:T(8,128)S(1)} %get-tuple-element.48.gap_ref, ...), custom_call_target="tpu_custom_call" | custom-call | flops 1 | bytes 1 | tf_op jit(solution)/shard_map/final/pallas_call | solution.py:48
  (2 shorter events, 0.1 us)
Async XLA Ops:
  2.6 24.2 %collective-permute-start = (f32[8,18432]{1,0:T(8,128)S(1)}, f32[8,18432]{1,0:T(8,128)S(1)}, u32[]{:S(2)}, u32[]{:S(2)}) collective-permute-start(f32[8,18432]{1,0:T(8,128)S(1)} %get-tuple-element.28.own_up), channel_id=1, source_target_pairs={{0,4},{1,5},{2,6},{3,7},{4,8},{5,9},{6,10},{7,11},{8,12},{9,13},{1... | collective-permute-start | bytes 1769480 | tf_op jit(solution)/shard_map/ppermute | solution.py:618
  5.1 21.6 %collective-permute-start.1 = (f32[8,18432]{1,0:T(8,128)S(1)}, f32[8,18432]{1,0:T(8,128)S(1)}, u32[]{:S(2)}, u32[]{:S(2)}) collective-permute-start(f32[8,18432]{1,0:T(8,128)S(1)} %get-tuple-element.29.own_down), channel_id=1, source_target_pairs={{4,0},{5,1},{6,2},{7,3},{8,4},{9,5},{10,6},{11,7},{12,8},{13,9},{1... | collective-permute-start | bytes 1769480 | tf_op jit(solution)/shard_map/ppermute | solution.py:619
  18.7 2.4 %collective-permute-start.2 = (f32[8,12288]{1,0:T(8,128)S(1)}, f32[8,12288]{1,0:T(8,128)S(1)}, u32[]{:S(2)}, u32[]{:S(2)}) collective-permute-start(f32[8,12288]{1,0:T(8,128)S(1)} %get-tuple-element.37.mine), channel_id=1, source_target_pairs={{0,1},{1,0},{2,3},{3,2},{4,5},{5,4},{6,7},{7,6},{8,9},{9,8},{10,11... | collective-permute-start | bytes 1179656 | tf_op jit(solution)/shard_map/ppermute | solution.py:632
  21.1 9.9 %collective-permute-start.5 = (f32[8,6656]{1,0:T(8,128)S(1)}, f32[8,6656]{1,0:T(8,128)S(1)}, u32[]{:S(2)}, u32[]{:S(2)}) collective-permute-start(f32[8,6656]{1,0:T(8,128)S(1)} %get-tuple-element.49.res_ref), channel_id=1, source_target_pairs={{0,2},{2,0},{1,3},{3,1},{4,6},{6,4},{5,7},{7,5},{8,10},{10,8},{9,1... | collective-permute-start | bytes 638984 | tf_op jit(solution)/shard_map/ppermute | solution.py:639
  27.1 2.3 %collective-permute-start.3 = (f32[8,4096]{1,0:T(8,128)S(1)}, f32[8,4096]{1,0:T(8,128)S(1)}, u32[]{:S(2)}, u32[]{:S(2)}) collective-permute-start(f32[8,4096]{1,0:T(8,128)S(1)} %get-tuple-element.45.mine), channel_id=1, source_target_pairs={{0,1},{1,0},{2,3},{3,2},{4,5},{5,4},{6,7},{7,6},{8,9},{9,8},{10,11... | collective-permute-start | bytes 393224 | tf_op jit(solution)/shard_map/ppermute | solution.py:654
  28.4 1.3 %collective-permute-start.4 = (f32[8,4096]{1,0:T(8,128)S(1)}, f32[8,4096]{1,0:T(8,128)S(1)}, u32[]{:S(2)}, u32[]{:S(2)}) collective-permute-start(f32[8,4096]{1,0:T(8,128)S(1)} %get-tuple-element.46.far_mine), channel_id=1, source_target_pairs={{0,1},{1,0},{2,3},{3,2},{4,5},{5,4},{6,7},{7,6},{8,9},{9,8},{10,11... | collective-permute-start | bytes 393224 | tf_op jit(solution)/shard_map/ppermute | solution.py:655
  28.5 3.6 %collective-permute-start.7 = (f32[8,2560]{1,0:T(8,128)S(1)}, f32[8,2560]{1,0:T(8,128)S(1)}, u32[]{:S(2)}, u32[]{:S(2)}) collective-permute-start(f32[8,2560]{1,0:T(8,128)S(1)} %get-tuple-element.53), channel_id=1, source_target_pairs={{0,2},{2,0},{1,3},{3,1},{4,6},{6,4},{5,7},{7,5},{8,10},{10,8},{9,1... | collective-permute-start | bytes 245768 | tf_op jit(solution)/shard_map/ppermute | solution.py:656
  29.8 5.7 %collective-permute-start.6 = (f32[8,4096]{1,0:T(8,128)S(1)}, f32[8,4096]{1,0:T(8,128)S(1)}, u32[]{:S(2)}, u32[]{:S(2)}) collective-permute-start(f32[8,4096]{1,0:T(8,128)S(1)} %get-tuple-element.50._.end_ref), channel_id=1, source_target_pairs={{0,2},{2,0},{1,3},{3,1},{4,6},{6,4},{5,7},{7,5},{8,10},{10,8},{9,1... | collective-permute-start | bytes 393224 | tf_op jit(solution)/shard_map/ppermute | solution.py:663
  32.1 2.7 %collective-permute-start.8 = (f32[8,3840]{1,0:T(8,128)S(1)}, f32[8,3840]{1,0:T(8,128)S(1)}, u32[]{:S(2)}, u32[]{:S(2)}) collective-permute-start(f32[8,3840]{1,0:T(8,128)S(1)} %relay.1), channel_id=1, source_target_pairs={{0,1},{1,0},{2,3},{3,2},{4,5},{5,4},{6,7},{7,6},{8,9},{9,8},{10,11... | collective-permute-start | bytes 368648 | tf_op jit(solution)/shard_map/ppermute | solution.py:670
